TPU v7x, 32 devices: a whole 2x2x4 slice. The times are simulated.
32 devices in a mesh: dp: 8 (over z, core), tensor: 4 (over y, x).
Axes of the slice: x: 2, y: 2, z: 4, core: 2. Of those that a mesh axis runs over, the one named last changes fastest.
Arguments:
- tokens: bfloat16 [2, 8192, 2560], P(None, ('dp', 'tensor')), may hold values from -6 to 6
- prefix: int32 [2, 8], P(None, 'dp'), may hold values from 102 to 512
- input_gain: bfloat16 [2560], P(('dp', 'tensor')), may hold values from 0.5 to 1.5
- query_down: bfloat16 [2560, 768], P(('dp', 'tensor')), may hold values from -0.125 to 0.125
- query_gain: bfloat16 [768], P(('dp', 'tensor')), may hold values from 0.5 to 1.5
- query_up: bfloat16 [768, 3840], P('dp', 'tensor'), may hold values from -0.21875 to 0.21875
- latent_down: bfloat16 [2560, 288], P(('dp', 'tensor')), may hold values from -0.125 to 0.125
- latent_gain: bfloat16 [256], P(('dp', 'tensor')), may hold values from 0.5 to 1.5
- latent_up: bfloat16 [256, 5120], P('dp', 'tensor'), may hold values from -0.375 to 0.375
- out_proj: bfloat16 [2560, 2560], P('tensor', 'dp'), may hold values from -4 to 4
- post_gain: bfloat16 [2560], P(('dp', 'tensor')), may hold values from 0.5 to 1.5
- gate_proj: bfloat16 [2560, 6400], P('dp', 'tensor'), may hold values from -0.125 to 0.125
- up_proj: bfloat16 [2560, 6400], P('dp', 'tensor'), may hold values from -0.125 to 0.125
- down_proj: bfloat16 [6400, 2560], P('tensor', 'dp'), may hold values from -0.875 to 0.875
- cotangent: bfloat16 [2, 8192, 2560], P(None, ('dp', 'tensor')), may hold values from -6 to 6
Outputs:
- mixed: bfloat16 [2, 8192, 2560], P(None, ('dp', 'tensor'))
- d_tokens: float32 [2, 8192, 2560], P(None, ('dp', 'tensor'))
- input_gain_grad: float32 [2560], P(('dp', 'tensor'))
- query_down_grad: float32 [2560, 768], P(('dp', 'tensor'))
- query_gain_grad: float32 [768], P(('dp', 'tensor'))
- query_up_grad: float32 [768, 3840], P('dp', 'tensor')
- latent_down_grad: float32 [2560, 288], P(('dp', 'tensor'))
- latent_gain_grad: float32 [256], P(('dp', 'tensor'))
- latent_up_grad: float32 [256, 5120], P('dp', 'tensor')
- out_proj_grad: float32 [2560, 2560], P('tensor', 'dp')
- post_gain_grad: float32 [2560], P(('dp', 'tensor'))
- gate_grad: float32 [2560, 6400], P('dp', 'tensor')
- up_grad: float32 [2560, 6400], P('dp', 'tensor')
- down_grad: float32 [6400, 2560], P('tensor', 'dp')
Inputs may be any that keep to these rules, and one draw needn't show every extreme that they name: prefix of each sequence: its first that many tokens attend to each other both ways.
All inputs are finite; a program needn't handle non-finite values.
Results may differ from a plain program's by a relative error of at most 0.024.
Values may be sent and summed in bfloat16 or wider, within the bound.
No kernel may reach another device: no remote copies, remote signals or barrier semaphores. Data moves between devices by JAX's collectives and lax.ppermute only.
A program may use at most 208 MiB of HBM per device.

v0:
```python
import math

import jax
import jax.numpy as jnp
from jax import lax
from jax.sharding import PartitionSpec as P

NOPE = 64
ROPE = 32
VD = 64
KVR = 256


EPSILON = 1e-05
RESIDUAL = 1.4 / math.sqrt(62.0)
NEGATIVE = -1e30
ROPE_BASE = 10000.0


def product(left_side, right_side):
    return jnp.dot(left_side, right_side, preferred_element_type=jnp.float32)


def product_tn(left_side, right_side):
    return lax.dot_general(
        left_side, right_side, (((0,), (0,)), ((), ())), preferred_element_type=jnp.float32
    )


def product_nt(left_side, right_side):
    return lax.dot_general(
        left_side, right_side, (((1,), (1,)), ((), ())), preferred_element_type=jnp.float32
    )


def inverse_rms(values):
    return lax.rsqrt(jnp.mean(values * values, axis=-1, keepdims=True) + EPSILON)


def norm_back(values, gain_vec, grad_out):
    scale_inv = inverse_rms(values)
    normal = values * scale_inv
    grad_norm = grad_out * gain_vec
    grad_values = scale_inv * (
        grad_norm - normal * jnp.mean(grad_norm * normal, axis=-1, keepdims=True)
    )
    return (grad_values, jnp.sum(grad_out * normal, axis=0))


def rotary(row_count, row_start, rope_width):
    half_width = rope_width // 2
    frequency = ROPE_BASE ** (-2.0 * jnp.arange(half_width).astype(jnp.float32) / rope_width)
    angles = (row_start + jnp.arange(row_count)).astype(jnp.float32)[:, None] * frequency[None, :]
    return (jnp.cos(angles), jnp.sin(angles))


def rotate(values, cosine, sine_table):
    half_width = values.shape[-1] // 2
    first_half = values[..., :half_width]
    second_half = values[..., half_width:]
    return jnp.concatenate(
        [
            first_half * cosine - second_half * sine_table,
            second_half * cosine + first_half * sine_table,
        ],
        axis=-1,
    )


def fetch_latent(input_gain, query_down, query_gain, latent_down, latent_gain, post_gain):
    return (
        lax.all_gather(input_gain, ("dp", "tensor"), axis=0, tiled=True),
        lax.all_gather(query_down, ("dp", "tensor"), axis=0, tiled=True),
        lax.all_gather(query_gain, ("dp", "tensor"), axis=0, tiled=True),
        lax.all_gather(latent_down, ("dp", "tensor"), axis=0, tiled=True),
        lax.all_gather(latent_gain, ("dp", "tensor"), axis=0, tiled=True),
        lax.all_gather(post_gain, ("dp", "tensor"), axis=0, tiled=True),
    )


def fetch_heads(query_up, latent_up, out_proj, gate_proj, up_proj, down_proj):
    return (
        lax.all_gather(query_up, "dp", axis=0, tiled=True),
        lax.all_gather(latent_up, "dp", axis=0, tiled=True),
        lax.all_gather(out_proj, "dp", axis=1, tiled=True),
        lax.all_gather(gate_proj, "dp", axis=0, tiled=True),
        lax.all_gather(up_proj, "dp", axis=0, tiled=True),
        lax.all_gather(down_proj, "dp", axis=1, tiled=True),
    )


def reduce_grads(latent_grads, head_grads):
    latent_part = (
        lax.psum_scatter(latent_grads[0], ("dp", "tensor"), scatter_dimension=0, tiled=True),
        lax.psum_scatter(latent_grads[1], ("dp", "tensor"), scatter_dimension=0, tiled=True),
        lax.psum_scatter(latent_grads[2], ("dp", "tensor"), scatter_dimension=0, tiled=True),
        lax.psum_scatter(latent_grads[3], ("dp", "tensor"), scatter_dimension=0, tiled=True),
        lax.psum_scatter(latent_grads[4], ("dp", "tensor"), scatter_dimension=0, tiled=True),
        lax.psum_scatter(latent_grads[5], ("dp", "tensor"), scatter_dimension=0, tiled=True),
    )
    head_part = (
        lax.psum_scatter(
            head_grads[0].astype(jnp.bfloat16), "dp", scatter_dimension=0, tiled=True
        ).astype(jnp.float32),
        lax.psum_scatter(
            head_grads[1].astype(jnp.bfloat16), "dp", scatter_dimension=0, tiled=True
        ).astype(jnp.float32),
        lax.psum_scatter(
            head_grads[2].astype(jnp.bfloat16), "dp", scatter_dimension=1, tiled=True
        ).astype(jnp.float32),
        lax.psum_scatter(
            head_grads[3].astype(jnp.bfloat16), "dp", scatter_dimension=0, tiled=True
        ).astype(jnp.float32),
        lax.psum_scatter(
            head_grads[4].astype(jnp.bfloat16), "dp", scatter_dimension=0, tiled=True
        ).astype(jnp.float32),
        lax.psum_scatter(
            head_grads[5].astype(jnp.bfloat16), "dp", scatter_dimension=1, tiled=True
        ).astype(jnp.float32),
    )
    return (latent_part, head_part)


def layer_pass(
    tokens_micro, cot_micro, prefix_len, latent_weights, head_weights, first_row, seq_length
):
    gain_in, down_query, gain_query, down_latent, gain_latent, gain_post = latent_weights
    up_query, up_latent, proj_out, proj_gate, proj_up, proj_down = head_weights
    gain_in = gain_in.astype(jnp.float32)
    gain_query = gain_query.astype(jnp.float32)
    gain_latent = gain_latent.astype(jnp.float32)
    gain_post = gain_post.astype(jnp.float32)
    local_rows = tokens_micro.shape[0]
    residual = tokens_micro.astype(jnp.float32)
    cos_local, sin_local = rotary(local_rows, first_row, ROPE)
    normed = (residual * inverse_rms(residual) * gain_in).astype(jnp.bfloat16)
    query_lat = product(normed, down_query)
    query_comp = (query_lat * inverse_rms(query_lat) * gain_query).astype(jnp.bfloat16)
    latent_all = product(normed, down_latent)
    latent_comp = latent_all[:, :KVR]
    latent_norm = (latent_comp * inverse_rms(latent_comp) * gain_latent).astype(jnp.bfloat16)
    key_local = rotate(latent_all[:, KVR:], cos_local, sin_local).astype(jnp.bfloat16)
    query_full, latent_full, rope_full = (
        lax.all_gather(query_comp, "tensor", axis=0, tiled=True),
        lax.all_gather(latent_norm, "tensor", axis=0, tiled=True),
        lax.all_gather(key_local, "tensor", axis=0, tiled=True),
    )
    cos_all, sin_all = rotary(seq_length, 0, ROPE)
    head_count = up_query.shape[1] // (NOPE + ROPE)
    query_raw = product(query_full, up_query).reshape(seq_length, head_count, NOPE + ROPE)
    queries = jnp.concatenate(
        [query_raw[..., :NOPE], rotate(query_raw[..., NOPE:], cos_all[:, None], sin_all[:, None])],
        axis=-1,
    ).astype(jnp.bfloat16)
    keyval = (
        product(latent_full, up_latent)
        .astype(jnp.bfloat16)
        .reshape(seq_length, head_count, NOPE + VD)
    )
    key_nope = keyval[..., :NOPE]
    values = keyval[..., NOPE:]
    block_rows = 512
    block_count = seq_length // block_rows
    score_scale = (NOPE + ROPE) ** (-0.5)
    columns = jnp.arange(seq_length)

    def block_scores(query_part, row_start):
        positions = row_start + jnp.arange(block_rows)
        visible = (columns[None, :] <= positions[:, None]) | (columns[None, :] < prefix_len)
        raw_scores = jnp.einsum(
            "qhd,khd->hqk", query_part[..., :NOPE], key_nope, preferred_element_type=jnp.float32
        )
        raw_scores = raw_scores + jnp.einsum(
            "qhd,kd->hqk", query_part[..., NOPE:], rope_full, preferred_element_type=jnp.float32
        )
        return jnp.where(visible[None], raw_scores * score_scale, NEGATIVE)

    def attend_block(block_item):
        query_part, row_start = block_item
        scores = block_scores(query_part, row_start)
        row_peak = jnp.max(scores, axis=-1, keepdims=True)
        exp_scores = jnp.exp(scores - row_peak)
        row_total = jnp.sum(exp_scores, axis=-1, keepdims=True)
        attn_probs = (exp_scores / row_total).astype(jnp.bfloat16)
        block_out = jnp.einsum(
            "hqk,khd->qhd", attn_probs, values, preferred_element_type=jnp.float32
        )
        return (block_out.astype(jnp.bfloat16), row_peak[..., 0] + jnp.log(row_total[..., 0]))

    query_blocks = queries.reshape(block_count, block_rows, head_count, NOPE + ROPE)
    starts = jnp.arange(block_count) * block_rows
    attended, log_totals = lax.map(attend_block, (query_blocks, starts))
    attn_flat = attended.reshape(seq_length, head_count * VD)
    attn_rows = lax.psum_scatter(
        product(attn_flat, proj_out).astype(jnp.bfloat16), "tensor", scatter_dimension=0, tiled=True
    ).astype(jnp.float32)
    middle = residual + RESIDUAL * attn_rows
    hidden_in = (middle * inverse_rms(middle) * gain_post).astype(jnp.bfloat16)
    hidden_all = lax.all_gather(hidden_in, "tensor", axis=0, tiled=True)
    gate_val = product(hidden_all, proj_gate)
    up_val = product(hidden_all, proj_up)
    sigmoid_gate = jax.nn.sigmoid(gate_val)
    silu_val = gate_val * sigmoid_gate
    active = (silu_val * up_val).astype(jnp.bfloat16)
    mlp_rows = lax.psum_scatter(
        product(active, proj_down).astype(jnp.bfloat16), "tensor", scatter_dimension=0, tiled=True
    ).astype(jnp.float32)
    output = (middle + RESIDUAL * mlp_rows).astype(jnp.bfloat16)
    grad_out = cot_micro.astype(jnp.float32)
    grad_branch = (RESIDUAL * grad_out).astype(jnp.bfloat16)
    branch_all = lax.all_gather(grad_branch, "tensor", axis=0, tiled=True)
    grad_active = product_nt(branch_all, proj_down)
    grad_down = product_tn(active, branch_all)
    grad_gate = (
        grad_active * up_val * sigmoid_gate * (1.0 + gate_val * (1.0 - sigmoid_gate))
    ).astype(jnp.bfloat16)
    grad_up = (grad_active * silu_val).astype(jnp.bfloat16)
    grad_gate_w = product_tn(hidden_all, grad_gate)
    grad_up_w = product_tn(hidden_all, grad_up)
    hidden_part = product_nt(grad_gate, proj_gate) + product_nt(grad_up, proj_up)
    grad_hidden = lax.psum_scatter(
        hidden_part.astype(jnp.bfloat16), "tensor", scatter_dimension=0, tiled=True
    ).astype(jnp.float32)
    grad_mid_norm, grad_gain_post = norm_back(middle, gain_post, grad_hidden)
    grad_mid = grad_out + grad_mid_norm
    grad_attn = (RESIDUAL * grad_mid).astype(jnp.bfloat16)
    attn_grad_all = lax.all_gather(grad_attn, "tensor", axis=0, tiled=True)
    grad_proj_out = product_tn(attn_flat, attn_grad_all)
    grad_flat = product_nt(attn_grad_all, proj_out).astype(jnp.bfloat16)
    grad_blocks = grad_flat.reshape(block_count, block_rows, head_count, VD)

    def back_block(carried, block_item):
        acc_key, acc_value, acc_rope = carried
        query_part, grad_part, log_part, row_start = block_item
        scores = block_scores(query_part, row_start)
        soft = jnp.exp(scores - log_part[..., None])
        grad_probs = jnp.einsum(
            "qhd,khd->hqk", grad_part, values, preferred_element_type=jnp.float32
        )
        row_delta = jnp.sum(soft * grad_probs, axis=-1, keepdims=True)
        grad_scores = (soft * (grad_probs - row_delta)).astype(jnp.bfloat16)
        grad_q_nope = jnp.einsum(
            "hqk,khd->qhd", grad_scores, key_nope, preferred_element_type=jnp.float32
        )
        grad_q_rope = jnp.einsum(
            "hqk,kd->qhd", grad_scores, rope_full, preferred_element_type=jnp.float32
        )
        acc_key = acc_key + score_scale * jnp.einsum(
            "hqk,qhd->khd", grad_scores, query_part[..., :NOPE], preferred_element_type=jnp.float32
        )
        acc_rope = acc_rope + score_scale * jnp.einsum(
            "hqk,qhd->kd", grad_scores, query_part[..., NOPE:], preferred_element_type=jnp.float32
        )
        acc_value = acc_value + jnp.einsum(
            "hqk,qhd->khd", soft.astype(jnp.bfloat16), grad_part, preferred_element_type=jnp.float32
        )
        grad_query_part = score_scale * jnp.concatenate([grad_q_nope, grad_q_rope], axis=-1)
        return ((acc_key, acc_value, acc_rope), grad_query_part)

    initial = (
        jnp.zeros((seq_length, head_count, NOPE), jnp.float32),
        jnp.zeros((seq_length, head_count, VD), jnp.float32),
        jnp.zeros((seq_length, ROPE), jnp.float32),
    )
    (acc_key, acc_value, acc_rope), grad_query_blocks = lax.scan(
        back_block, initial, (query_blocks, grad_blocks, log_totals, starts)
    )
    grad_query = grad_query_blocks.reshape(seq_length, head_count, NOPE + ROPE)
    grad_query_raw = (
        jnp.concatenate(
            [
                grad_query[..., :NOPE],
                rotate(grad_query[..., NOPE:], cos_all[:, None], -sin_all[:, None]),
            ],
            axis=-1,
        )
        .reshape(seq_length, head_count * (NOPE + ROPE))
        .astype(jnp.bfloat16)
    )
    grad_keyval = (
        jnp.concatenate([acc_key, acc_value], axis=-1)
        .reshape(seq_length, head_count * (NOPE + VD))
        .astype(jnp.bfloat16)
    )
    grad_up_query = product_tn(query_full, grad_query_raw)
    grad_up_latent = product_tn(latent_full, grad_keyval)
    comp_part = product_nt(grad_query_raw, up_query)
    norm_part = product_nt(grad_keyval, up_latent)
    grad_comp, grad_lnorm, grad_rope = (
        lax.psum_scatter(
            comp_part.astype(jnp.bfloat16), "tensor", scatter_dimension=0, tiled=True
        ).astype(jnp.float32),
        lax.psum_scatter(
            norm_part.astype(jnp.bfloat16), "tensor", scatter_dimension=0, tiled=True
        ).astype(jnp.float32),
        lax.psum_scatter(
            acc_rope.astype(jnp.bfloat16), "tensor", scatter_dimension=0, tiled=True
        ).astype(jnp.float32),
    )
    grad_qlat, grad_gain_query = norm_back(query_lat, gain_query, grad_comp)
    grad_qlat = grad_qlat.astype(jnp.bfloat16)
    grad_latent_comp, grad_gain_latent = norm_back(latent_comp, gain_latent, grad_lnorm)
    grad_rope_raw = rotate(grad_rope, cos_local, -sin_local)
    grad_latent_all = jnp.concatenate([grad_latent_comp, grad_rope_raw], axis=-1).astype(
        jnp.bfloat16
    )
    grad_down_query = product_tn(normed, grad_qlat)
    grad_down_latent = product_tn(normed, grad_latent_all)
    grad_normed = product_nt(grad_qlat, down_query) + product_nt(grad_latent_all, down_latent)
    grad_resid_norm, grad_gain_in = norm_back(residual, gain_in, grad_normed)
    grad_tokens = grad_mid + grad_resid_norm
    latent_grads = (
        grad_gain_in,
        grad_down_query,
        grad_gain_query,
        grad_down_latent,
        grad_gain_latent,
        grad_gain_post,
    )
    head_grads = (grad_up_query, grad_up_latent, grad_proj_out, grad_gate_w, grad_up_w, grad_down)
    return (output, grad_tokens, latent_grads, head_grads)


def body(
    tokens,
    prefix,
    input_gain,
    query_down,
    query_gain,
    query_up,
    latent_down,
    latent_gain,
    latent_up,
    out_proj,
    post_gain,
    gate_proj,
    up_proj,
    down_proj,
    cotangent,
):
    micro_count = tokens.shape[0]
    local_rows = tokens.shape[1]
    seq_length = local_rows * lax.axis_size("tensor")
    first_row = lax.axis_index("tensor") * local_rows
    outputs_list = []
    grads_list = []
    latent_total = None
    head_total = None
    for micro_index in range(micro_count):
        latent_weights = fetch_latent(
            input_gain, query_down, query_gain, latent_down, latent_gain, post_gain
        )
        head_weights = fetch_heads(query_up, latent_up, out_proj, gate_proj, up_proj, down_proj)
        output, grad_tokens, latent_grads, head_grads = layer_pass(
            tokens[micro_index],
            cotangent[micro_index],
            prefix[micro_index, 0],
            latent_weights,
            head_weights,
            first_row,
            seq_length,
        )
        outputs_list.append(output)
        grads_list.append(grad_tokens)
        if micro_index == 0:
            latent_total = latent_grads
            head_total = head_grads
        else:
            latent_total = jax.tree.map(jnp.add, latent_total, latent_grads)
            head_total = jax.tree.map(jnp.add, head_total, head_grads)
    latent_total, head_total = reduce_grads(latent_total, head_total)
    mixed = jnp.stack(outputs_list, axis=0)
    d_tokens = jnp.stack(grads_list, axis=0)
    return (
        mixed,
        d_tokens,
        latent_total[0],
        latent_total[1],
        latent_total[2],
        head_total[0],
        latent_total[3],
        latent_total[4],
        head_total[1],
        head_total[2],
        latent_total[5],
        head_total[3],
        head_total[4],
        head_total[5],
    )


def solution(mesh):
    return jax.shard_map(
        body,
        mesh=mesh,
        in_specs=(
            P(None, ("dp", "tensor"), None),
            P(None, "dp"),
            P(("dp", "tensor")),
            P(("dp", "tensor"), None),
            P(("dp", "tensor")),
            P("dp", "tensor"),
            P(("dp", "tensor"), None),
            P(("dp", "tensor")),
            P("dp", "tensor"),
            P("tensor", "dp"),
            P(("dp", "tensor")),
            P("dp", "tensor"),
            P("dp", "tensor"),
            P("tensor", "dp"),
            P(None, ("dp", "tensor"), None),
        ),
        out_specs=(
            P(None, ("dp", "tensor"), None),
            P(None, ("dp", "tensor"), None),
            P(("dp", "tensor")),
            P(("dp", "tensor"), None),
            P(("dp", "tensor")),
            P("dp", "tensor"),
            P(("dp", "tensor"), None),
            P(("dp", "tensor")),
            P("dp", "tensor"),
            P("tensor", "dp"),
            P(("dp", "tensor")),
            P("dp", "tensor"),
            P("dp", "tensor"),
            P("tensor", "dp"),
        ),
        check_vma=False,
    )
```

profile of v0, /device:TPU:0, one launch (start us, length us, event | category | flops | bytes accessed | tf_op | source)
XLA Modules:
  0.0 2698.2 jit_solution(9487478756392357905)
XLA Ops:
  12.9 42.3 %all-reduce.9 = (bf16[2560]{0:T(1024)(128)(2,1)S(1)}, bf16[768]{0:T(1024)(128)(2,1)S(1)}, bf16[256]{0:T(256)(128)(2,1)S(1)}, bf16[2560]{0:T(1024)(128)(2,1)}) all-reduce(bf16[2560]{0:T(1024)(128)(2,1)S(1)} %dynamic-update-slice, bf16[768]{0:T(1024)(128)(2,1)S(1)} %dynamic-update-slice.1, ...), channel_id=1, replica_groups=mesh['dp'=8,'tensor'=4] {'dp','tensor'}, use_global_device_ids=true, to_apply=%add | all-reduce | flops 6144 | bytes 24576
  57.6 17.3 all-gather.16.cloned.1.call-done
  82.8 15.2 all_gather.92
  99.7 33.1 %all-gather.22.cloned.1.call-done = bf16[2560,288]{1,0:T(8,128)(2,1)} async-done(((bf16[80,288]{1,0:T(8,128)(2,1)}), bf16[2560,288]{1,0:T(8,128)(2,1)}) %all-gather.22.cloned.1.call-update) | async-done | bytes 1474576 | tf_op jit(solution)/shard_map/all_gather | solution.py:75
  137.1 14.4 all_gather.101
  166.4 14.5 all_gather.91
  207.3 19.2 all-gather.18.cloned.1.call-done
  247.9 90.0 %while.65 = (s32[]{:T(128)}, bf16[2,512,10,64]{1,3,2,0:T(8,128)(2,1)}, f32[2,10,512]{2,1,0:T(8,128)S(1)}, s32[2]{0:T(128)S(1)}, s32[]{:T(128)}, /*index=5*/bf16[...) while((s32[]{:T(128)}, ...), condition=%wide.region_16.17_spmd.clone.clone, body=%wide.region_13.16_spmd.clone.clone.sunk | while | flops 1726280192 | bytes 112405112 | solution.py:192
  260.2 13.6 fusion.393
  305.2 13.5 fusion.393
  345.0 17.4 convolution_convert_fusion.1
  370.7 91.0 %while.64 = (s32[]{:T(128)}, bf16[2,512,10,64]{1,3,2,0:T(8,128)(2,1)}, f32[2,10,512]{2,1,0:T(8,128)S(1)}, s32[2]{0:T(128)S(1)}, s32[]{:T(128)}, /*index=5*/bf16[...) while((s32[]{:T(128)}, ...), condition=%wide.region_6.7_spmd.clone.clone, body=%wide.region_3.6_spmd.clone.clone.sunk | while | flops 1726280192 | bytes 112405112 | solution.py:192
  383.2 14.0 fusion.384
  428.9 13.5 fusion.384
  473.2 61.6 %reduce-scatter.21.cloned.1.call-done = bf16[256,2560]{1,0:T(8,128)(2,1)} async-done(((bf16[1024,2560]{1,0:T(8,128)(2,1)}), bf16[256,2560]{1,0:T(8,128)(2,1)}) %reduce-scatter.21.cloned.1.call-update) | async-done | bytes 1310736 | tf_op jit(solution)/shard_map/reduce_scatter | solution.py:194
  547.1 72.5 %all-gather.28.cloned.1.call-done = bf16[2560,1600]{1,0:T(8,128)(2,1)} async-done(((bf16[320,1600]{1,0:T(8,128)(2,1)}), bf16[2560,1600]{1,0:T(8,128)(2,1)}) %all-gather.28.cloned.1.call-update) | async-done | bytes 8192016 | tf_op jit(solution)/shard_map/all_gather | solution.py:86
  619.6 62.2 %all-gather.36.cloned.1.call-done = bf16[1024,2560]{1,0:T(8,128)(2,1)} async-done(((bf16[256,2560]{1,0:T(8,128)(2,1)}), bf16[1024,2560]{1,0:T(8,128)(2,1)}) %all-gather.36.cloned.1.call-update) | async-done | bytes 5242896 | tf_op jit(solution)/shard_map/all_gather | solution.py:199
  681.9 14.8 fusion.211
  696.7 70.0 %all-gather.30.cloned.1.call-done = bf16[2560,1600]{1,0:T(8,128)(2,1)} async-done(((bf16[320,1600]{1,0:T(8,128)(2,1)}), bf16[2560,1600]{1,0:T(8,128)(2,1)}) %all-gather.30.cloned.1.call-update) | async-done | bytes 8192016 | tf_op jit(solution)/shard_map/all_gather | solution.py:87
  766.7 14.9 fusion.212
  781.6 47.3 %all-gather.42.cloned.1.call-done = bf16[1024,2560]{1,0:T(8,128)(2,1)} async-done(((bf16[256,2560]{1,0:T(8,128)(2,1)}), bf16[1024,2560]{1,0:T(8,128)(2,1)}) %all-gather.42.cloned.1.call-update) | async-done | bytes 5242896 | tf_op jit(solution)/shard_map/all_gather | solution.py:211
  828.9 84.8 %all-gather.32.cloned.1.call-done = bf16[1600,2560]{0,1:T(8,128)(2,1)} async-done(((bf16[1600,320]{0,1:T(8,128)(2,1)}), bf16[1600,2560]{0,1:T(8,128)(2,1)}) %all-gather.32.cloned.1.call-update) | async-done | bytes 8192016 | tf_op jit(solution)/shard_map/all_gather | solution.py:88
  913.8 20.7 multiply_convert_fusion.2
  947.9 15.1 add_convert_fusion.3
  976.0 15.1 fusion.208
  991.1 14.0 fusion.209
  1005.1 34.1 %all-gather.38.cloned.1.call-done = bf16[1024,2560]{1,0:T(8,128)(2,1)} async-done(((bf16[256,2560]{1,0:T(8,128)(2,1)}), bf16[1024,2560]{1,0:T(8,128)(2,1)}) %all-gather.38.cloned.1.call-update) | async-done | bytes 5242896 | tf_op jit(solution)/shard_map/all_gather | solution.py:211
  1039.2 21.0 multiply_convert_fusion.4
  1060.2 13.7 fusion.213
  1073.9 15.0 add_convert_fusion.4
  1090.8 13.8 convolution_convert_fusion
  1104.7 63.6 %reduce-scatter.29.cloned.1.call-done = bf16[256,2560]{1,0:T(8,128)(2,1)} async-done(((bf16[1024,2560]{1,0:T(8,128)(2,1)}), bf16[256,2560]{1,0:T(8,128)(2,1)}) %reduce-scatter.29.cloned.1.call-update) | async-done | bytes 1310736 | tf_op jit(solution)/shard_map/reduce_scatter | solution.py:221
  1173.0 59.6 %reduce-scatter.27.cloned.1.call-done = bf16[256,2560]{1,0:T(8,128)(2,1)} async-done(((bf16[1024,2560]{1,0:T(8,128)(2,1)}), bf16[256,2560]{1,0:T(8,128)(2,1)}) %reduce-scatter.27.cloned.1.call-update) | async-done | bytes 1310736 | tf_op jit(solution)/shard_map/reduce_scatter | solution.py:205
  1239.4 60.9 %all-gather.40.cloned.1.call-done = bf16[1024,2560]{1,0:T(8,128)(2,1)} async-done(((bf16[256,2560]{1,0:T(8,128)(2,1)}), bf16[1024,2560]{1,0:T(8,128)(2,1)}) %all-gather.40.cloned.1.call-update) | async-done | bytes 5242896 | tf_op jit(solution)/shard_map/all_gather | solution.py:227
  1314.4 246.6 %while.66 = (s32[]{:T(128)}, f32[1024,10,64]{0,2,1:T(8,128)}, f32[1024,10,64]{0,2,1:T(8,128)}, f32[1024,32]{0,1:T(8,128)}, f32[2,512,10,96]{1,0,3,2:T(2,128)}, /...) while((s32[]{:T(128)}, f32[1024,10,64]{0,2,1:T(8,128)}, ...), condition=%wide.region_24.25_spmd.clone.clone, body=%wide.region_22.24_spmd.clone.clone.sunk | while | flops 4419908096 | bytes 358885984 | solution.py:265
  1331.8 20.6 multiply_reduce_fusion.10
  1352.4 13.4 multiply_convert_fusion.18
  1381.4 36.0 %dynamic_update_slice.47 = f32[2,512,10,96]{1,0,3,2:T(2,128)} dynamic-update-slice(f32[2,512,10,96]{1,0,3,2:T(2,128)} %get-tuple-element.1200, f32[1,512,10,96]{1,0,3,2:T(1,128)} %copy.103, s32[]{:T(128)} %get-tuple-element.1196, s32[]{:T(128)} %constant.113.clone.1..sunk, s32[]{:T(128)} %constant.113.clone.1..sunk, s32[]{:T(128)} %constant.113.clone.1..sunk) | dynamic-update-slice | bytes 3932164 | tf_op jit(solution)/shard_map/while/body/jit(dynamic_update_index_in_dim)/dynamic_update_slice | solution.py:265
  1454.5 19.7 multiply_reduce_fusion.10
  1474.3 13.4 multiply_convert_fusion.18
  1503.2 36.0 %dynamic_update_slice.47 = f32[2,512,10,96]{1,0,3,2:T(2,128)} dynamic-update-slice(f32[2,512,10,96]{1,0,3,2:T(2,128)} %get-tuple-element.1200, f32[1,512,10,96]{1,0,3,2:T(1,128)} %copy.103, s32[]{:T(128)} %get-tuple-element.1196, s32[]{:T(128)} %constant.113.clone.1..sunk, s32[]{:T(128)} %constant.113.clone.1..sunk, s32[]{:T(128)} %constant.113.clone.1..sunk) | dynamic-update-slice | bytes 3932164 | tf_op jit(solution)/shard_map/while/body/jit(dynamic_update_index_in_dim)/dynamic_update_slice | solution.py:265
  1581.1 245.8 %while.67 = (s32[]{:T(128)}, f32[1024,10,64]{0,2,1:T(8,128)}, f32[1024,10,64]{0,2,1:T(8,128)}, f32[1024,32]{0,1:T(8,128)}, f32[2,512,10,96]{1,0,3,2:T(2,128)}, /...) while((s32[]{:T(128)}, f32[1024,10,64]{0,2,1:T(8,128)}, ...), condition=%wide.region_35.36_spmd.clone.clone, body=%wide.region_33.35_spmd.clone.clone.sunk | while | flops 4419908096 | bytes 358885984 | solution.py:265
  1597.2 19.7 multiply_reduce_fusion.11
  1616.9 13.4 multiply_convert_fusion.19
  1646.8 36.0 %dynamic_update_slice.48 = f32[2,512,10,96]{1,0,3,2:T(2,128)} dynamic-update-slice(f32[2,512,10,96]{1,0,3,2:T(2,128)} %get-tuple-element.1245, f32[1,512,10,96]{1,0,3,2:T(1,128)} %copy.104, s32[]{:T(128)} %get-tuple-element.1241, s32[]{:T(128)} %constant.113.clone.1..sunk.1, s32[]{:T(128)} %constant.113.clone.1..sunk.1, s32[]{:T(128)} %constant.113.clone.1..sunk.1) | dynamic-update-slice | bytes 3932164 | tf_op jit(solution)/shard_map/while/body/jit(dynamic_update_index_in_dim)/dynamic_update_slice | solution.py:265
  1719.0 19.7 multiply_reduce_fusion.11
  1738.7 13.4 multiply_convert_fusion.19
  1768.6 36.0 %dynamic_update_slice.48 = f32[2,512,10,96]{1,0,3,2:T(2,128)} dynamic-update-slice(f32[2,512,10,96]{1,0,3,2:T(2,128)} %get-tuple-element.1245, f32[1,512,10,96]{1,0,3,2:T(1,128)} %copy.104, s32[]{:T(128)} %get-tuple-element.1241, s32[]{:T(128)} %constant.113.clone.1..sunk.1, s32[]{:T(128)} %constant.113.clone.1..sunk.1, s32[]{:T(128)} %constant.113.clone.1..sunk.1) | dynamic-update-slice | bytes 3932164 | tf_op jit(solution)/shard_map/while/body/jit(dynamic_update_index_in_dim)/dynamic_update_slice | solution.py:265
  1871.4 16.2 fusion.220
  1887.6 16.3 add_convert_fusion.1
  1905.8 15.2 fusion.219
  1921.0 17.2 add_convert_fusion.2
  1940.1 15.3 fusion.221
  1955.4 17.3 add_convert_fusion
  1985.1 14.9 convolution_convert_fusion.2
  2041.2 55.1 %reduce-scatter.57.cloned.1.call-done = bf16[320,1600]{1,0:T(8,128)(2,1)} async-done(((bf16[2560,1600]{1,0:T(8,128)(2,1)}), bf16[320,1600]{1,0:T(8,128)(2,1)}) %reduce-scatter.57.cloned.1.call-update) | async-done | bytes 1024016 | tf_op jit(solution)/shard_map/reduce_scatter | solution.py:114
  2098.9 88.9 %reduce-scatter.55.cloned.1.call-done = bf16[320,1600]{1,0:T(8,128)(2,1)} async-done(((bf16[2560,1600]{1,0:T(8,128)(2,1)}), bf16[320,1600]{1,0:T(8,128)(2,1)}) %reduce-scatter.55.cloned.1.call-update) | async-done | bytes 1024016 | tf_op jit(solution)/shard_map/reduce_scatter | solution.py:111
  2190.6 88.9 %reduce-scatter.59.cloned.1.call-done = bf16[1600,320]{0,1:T(8,128)(2,1)} async-done(((bf16[1600,2560]{0,1:T(8,128)(2,1)}), bf16[1600,320]{0,1:T(8,128)(2,1)}) %reduce-scatter.59.cloned.1.call-update) | async-done | bytes 1024016 | tf_op jit(solution)/shard_map/reduce_scatter | solution.py:117
  2282.7 28.5 %reduce-scatter.51.cloned.1.call-done = bf16[32,1280]{1,0:T(8,128)(2,1)} async-done(((bf16[256,1280]{1,0:T(8,128)(2,1)}), bf16[32,1280]{1,0:T(8,128)(2,1)}) %reduce-scatter.51.cloned.1.call-update) | async-done | bytes 81936 | tf_op jit(solution)/shard_map/reduce_scatter | solution.py:105
  2312.8 33.9 %reduce-scatter.47.cloned.1.call-done = bf16[96,960]{1,0:T(8,128)(2,1)} async-done(((bf16[768,960]{1,0:T(8,128)(2,1)}), bf16[96,960]{1,0:T(8,128)(2,1)}) %reduce-scatter.47.cloned.1.call-update) | async-done | bytes 184336 | tf_op jit(solution)/shard_map/reduce_scatter | solution.py:102
  2359.4 38.7 %all-reduce.8 = (f32[2560]{0:T(1024)S(1)}, f32[768]{0:T(1024)S(1)}, f32[256]{0:T(256)S(1)}, f32[2560]{0:T(1024)S(1)}) all-reduce(f32[2560]{0:T(1024)S(1)} %add.382, f32[768]{0:T(1024)S(1)} %copy-done.126, f32[256]{0:T(256)S(1)} %copy-done.142, f32[2560]{0:T(1024)S(1)} %copy-done.102), channel_id=14, replica_groups=mesh['dp'=8,'tensor'=4] {'dp','tensor'}, use_global_device_ids=true, to_apply=%region_44.45.clone | all-reduce | flops 6144 | bytes 49152
  2423.8 31.0 %reduce-scatter.53.cloned.1.call-done = bf16[640,320]{0,1:T(8,128)(2,1)} async-done(((bf16[640,2560]{0,1:T(8,128)(2,1)}), bf16[640,320]{0,1:T(8,128)(2,1)}) %reduce-scatter.53.cloned.1.call-update) | async-done | bytes 409616 | tf_op jit(solution)/shard_map/reduce_scatter | solution.py:108
  2456.7 106.8 %reduce-scatter.49.cloned.1.call-done = f32[80,288]{1,0:T(8,128)} async-done(((f32[2560,288]{1,0:T(8,128)}), f32[80,288]{1,0:T(8,128)}) %reduce-scatter.49.cloned.1.call-update) | async-done | bytes 92176 | tf_op jit(solution)/shard_map/reduce_scatter | solution.py:97
  2563.5 127.7 %reduce-scatter.45.cloned.1.call-done = f32[80,768]{1,0:T(8,128)} async-done(((f32[2560,768]{1,0:T(8,128)}), f32[80,768]{1,0:T(8,128)}) %reduce-scatter.45.cloned.1.call-update) | async-done | bytes 245776 | tf_op jit(solution)/shard_map/reduce_scatter | solution.py:95
  (724 shorter events, 687.5 us)
Async XLA Ops:
  7.2 67.7 %copy-start.8 = (bf16[2,256,2560]{2,1,0:T(8,128)(2,1)S(1)}, bf16[2,256,2560]{2,1,0:T(8,128)(2,1)}, u32[]{:S(2)}) copy-start(bf16[2,256,2560]{2,1,0:T(8,128)(2,1)} %param.23) | copy-start | bytes 7864324
  7.2 67.7 %all-gather.16.cloned.1.call-start = ((), (), s32[]{:S(2)}) async-start(), calls=%async_computation.20 | async-start | bytes 4055040 | tf_op jit(solution)/shard_map/all_gather | solution.py:73
  7.9 124.8 %all-gather.22.cloned.1.call-start = ((), (), s32[]{:S(2)}) async-start(), calls=%async_computation.23 | async-start | bytes 2027520 | tf_op jit(solution)/shard_map/all_gather | solution.py:75
  8.7 191.7 %all-gather.20.cloned.1.call-start = ((), (), s32[]{:S(2)}) async-start(), calls=%async_computation.22 | async-start | bytes 1769472 | tf_op jit(solution)/shard_map/all_gather | solution.py:83
  9.4 191.0 %all-gather.34.cloned.1.call-start = ((), (), s32[]{:S(2)}) async-start(), calls=%async_computation.31 | async-start | bytes 1966080 | tf_op jit(solution)/shard_map/all_gather | solution.py:144
  55.2 80.2 %copy-start.77 = (f32[2560]{0:T(1024)}, f32[2560]{0:T(1024)S(1)}, u32[]{:S(2)}) copy-start(f32[2560]{0:T(1024)S(1)} %convert_element_type.370) | copy-start | bytes 30724
  57.5 75.2 %copy-start.127 = (f32[256]{0:T(256)}, f32[256]{0:T(256)S(1)}, u32[]{:S(2)}) copy-start(f32[256]{0:T(256)S(1)} %add_rsqrt_fusion.3) | copy-start | bytes 3076
  57.6 77.9 %copy-start.105 = (f32[256]{0:T(256)}, f32[256]{0:T(256)S(1)}, u32[]{:S(2)}) copy-start(f32[256]{0:T(256)S(1)} %add_rsqrt_fusion.7) | copy-start | bytes 3076
  79.9 55.5 %copy-start.99 = (f32[256]{0:T(256)}, f32[256]{0:T(256)S(1)}, u32[]{:S(2)}) copy-start(f32[256]{0:T(256)S(1)} %get-tuple-element.835) | copy-start | bytes 3076
  79.9 55.5 %copy-start.125 = (f32[256]{0:T(256)}, f32[256]{0:T(256)S(1)}, u32[]{:S(2)}) copy-start(f32[256]{0:T(256)S(1)} %get-tuple-element.836) | copy-start | bytes 3076
  81.0 145.4 %all-gather.18.cloned.1.call-start = ((), (), s32[]{:S(2)}) async-start(), calls=%async_computation.21 | async-start | bytes 1966080 | tf_op jit(solution)/shard_map/all_gather | solution.py:144
  81.6 263.4 %all-gather.24.cloned.1.call-start = ((), (), s32[]{:S(2)}) async-start(), calls=%async_computation.24 | async-start | bytes 3686400 | tf_op jit(solution)/shard_map/all_gather | solution.py:85
  82.2 391.0 %reduce-scatter.25.cloned.1.call-start = ((), (), s32[]{:S(2)}) async-start(), calls=%async_computation.32 | async-start | bytes 6553600 | tf_op jit(solution)/shard_map/reduce_scatter | solution.py:194
  82.3 75.6 %copy-start.136 = (f32[16]{0:T(128)}, f32[16]{0:T(128)S(1)}, u32[]{:S(2)}) copy-start(f32[16]{0:T(128)S(1)} %multiply_power_fusion) | copy-start | bytes 196
  82.8 53.7 %copy-start.119 = (f32[256]{0:T(256)}, f32[256]{0:T(256)S(1)}, u32[]{:S(2)}) copy-start(f32[256]{0:T(256)S(1)} %convert_element_type.376) | copy-start | bytes 3076
  98.0 82.9 %copy-start.46 = (bf16[256,1280]{1,0:T(8,128)(2,1)}, bf16[256,1280]{1,0:T(8,128)(2,1)S(1)}, u32[]{:S(2)}) copy-start(bf16[256,1280]{1,0:T(8,128)(2,1)S(1)} %all_gather.92) | copy-start | bytes 1966084
  98.0 59.9 %copy-start.138 = (f32[256]{0:T(256)}, f32[256]{0:T(256)S(1)}, u32[]{:S(2)}) copy-start(f32[256]{0:T(256)S(1)} %add_convert_fusion.13) | copy-start | bytes 3076
  99.7 130.5 %copy-start.83 = (f32[1024,16]{0,1:T(8,128)}, f32[1024,16]{0,1:T(8,128)S(1)}, u32[]{:S(2)}) copy-start(f32[1024,16]{0,1:T(8,128)S(1)} %get-tuple-element.817) | copy-start | bytes 196612
  362.4 172.4 %reduce-scatter.21.cloned.1.call-start = ((), (), s32[]{:S(2)}) async-start(), calls=%async_computation.25 | async-start | bytes 6553600 | tf_op jit(solution)/shard_map/reduce_scatter | solution.py:194
  472.3 62.5 %copy-start.9 = (bf16[2,256,2560]{2,1,0:T(8,128)(2,1)S(1)}, bf16[2,256,2560]{2,1,0:T(8,128)(2,1)}, u32[]{:S(2)}) copy-start(bf16[2,256,2560]{2,1,0:T(8,128)(2,1)} %param.23) | copy-start | bytes 7864324
  472.3 147.3 %all-gather.28.cloned.1.call-start = ((), (), s32[]{:S(2)}) async-start(), calls=%async_computation.27 | async-start | bytes 9584640 | tf_op jit(solution)/shard_map/all_gather | solution.py:86
  473.1 208.8 %all-gather.36.cloned.1.call-start = ((), (), s32[]{:S(2)}) async-start(), calls=%async_computation.33 | async-start | bytes 6553600 | tf_op jit(solution)/shard_map/all_gather | solution.py:199
  473.1 64.7 %copy-start.87 = (f32[2560]{0:T(1024)}, f32[2560]{0:T(1024)S(1)}, u32[]{:S(2)}) copy-start(f32[2560]{0:T(1024)S(1)} %convert_element_type.382) | copy-start | bytes 30724
  540.6 226.1 %all-gather.30.cloned.1.call-start = ((), (), s32[]{:S(2)}) async-start(), calls=%async_computation.28 | async-start | bytes 9584640 | tf_op jit(solution)/shard_map/all_gather | solution.py:87
  541.4 287.6 %all-gather.42.cloned.1.call-start = ((), (), s32[]{:S(2)}) async-start(), calls=%async_computation.41 | async-start | bytes 6553600 | tf_op jit(solution)/shard_map/all_gather | solution.py:211
  545.2 368.6 %all-gather.32.cloned.1.call-start = ((), (), s32[]{:S(2)}) async-start(), calls=%async_computation.29 | async-start | bytes 9584640 | tf_op jit(solution)/shard_map/all_gather | solution.py:88
  545.9 430.1 %all-gather.26.cloned.1.call-start = ((), (), s32[]{:S(2)}) async-start(), calls=%async_computation.26 | async-start | bytes 6553600 | tf_op jit(solution)/shard_map/all_gather | solution.py:199
  546.5 492.7 %all-gather.38.cloned.1.call-start = ((), (), s32[]{:S(2)}) async-start(), calls=%async_computation.35 | async-start | bytes 6553600 | tf_op jit(solution)/shard_map/all_gather | solution.py:211
  547.1 557.6 %reduce-scatter.37.cloned.1.call-start = ((), (), s32[]{:S(2)}) async-start(), calls=%async_computation.42 | async-start | bytes 6553600 | tf_op jit(solution)/shard_map/reduce_scatter | solution.py:221
  962.9 205.4 %reduce-scatter.29.cloned.1.call-start = ((), (), s32[]{:S(2)}) async-start(), calls=%async_computation.36 | async-start | bytes 6553600 | tf_op jit(solution)/shard_map/reduce_scatter | solution.py:221
  1088.9 143.7 %reduce-scatter.27.cloned.1.call-start = ((), (), s32[]{:S(2)}) async-start(), calls=%async_computation.34 | async-start | bytes 6553600 | tf_op jit(solution)/shard_map/reduce_scatter | solution.py:205
  1104.6 63.7 %copy-start.10 = (bf16[2,256,2560]{2,1,0:T(8,128)(2,1)S(1)}, bf16[2,256,2560]{2,1,0:T(8,128)(2,1)}, u32[]{:S(2)}) copy-start(bf16[2,256,2560]{2,1,0:T(8,128)(2,1)} %param.23) | copy-start | bytes 7864324
  1104.6 63.7 %copy-start.88 = (f32[2560]{0:T(1024)S(1)}, f32[2560]{0:T(1024)}, u32[]{:S(2)}) copy-start(f32[2560]{0:T(1024)} %copy-done.87) | copy-start | bytes 30724
  1104.6 63.7 %copy-start.114 = (f32[256]{0:T(256)S(1)}, f32[256]{0:T(256)}, u32[]{:S(2)}) copy-start(f32[256]{0:T(256)} %copy-done.113) | copy-start | bytes 3076
  1104.6 63.7 %copy-start.117 = (f32[256]{0:T(256)S(1)}, f32[256]{0:T(256)}, u32[]{:S(2)}) copy-start(f32[256]{0:T(256)} %copy-done.116) | copy-start | bytes 3076
  1104.6 195.8 %all-gather.40.cloned.1.call-start = ((), (), s32[]{:S(2)}) async-start(), calls=%async_computation.37 | async-start | bytes 6553600 | tf_op jit(solution)/shard_map/all_gather | solution.py:227
  1173.0 65.8 %copy-start.131 = (f32[256]{0:T(256)}, f32[256]{0:T(256)S(1)}, u32[]{:S(2)}) copy-start(f32[256]{0:T(256)S(1)} %broadcast_multiply_fusion.5) | copy-start | bytes 3076
  1173.0 65.8 %copy-start.133 = (f32[256]{0:T(256)}, f32[256]{0:T(256)S(1)}, u32[]{:S(2)}) copy-start(f32[256]{0:T(256)S(1)} %broadcast_multiply_fusion.7) | copy-start | bytes 3076
  1238.8 328.3 %all-gather.44.cloned.1.call-start = ((), (), s32[]{:S(2)}) async-start(), calls=%async_computation.43 | async-start | bytes 6553600 | tf_op jit(solution)/shard_map/all_gather | solution.py:227
  1239.4 777.4 %reduce-scatter.43.cloned.1.call-start = ((), (), s32[]{:S(2)}) async-start(), calls=%async_computation.46 | async-start | bytes 81920 | tf_op jit(solution)/shard_map/reduce_scatter | solution.py:296
  1381.4 36.0 %copy-start.5 = (bf16[512,10,96]{0,2,1:T(8,128)(2,1)S(1)}, bf16[512,10,96]{0,2,1:T(8,128)(2,1)}, u32[]{:S(2)}) copy-start(bf16[512,10,96]{0,2,1:T(8,128)(2,1)} %copy-done.4) | copy-start | bytes 2949124 | tf_op jit(solution)/shard_map/while
  1381.4 43.6 %slice-start = ((s8[10485760]{0:T(1024)(128)(4,1)}), s8[2097152]{0:T(1024)(128)(4,1)S(1)}, s32[]{:S(2)}) async-start(s8[10485760]{0:T(1024)(128)(4,1)} %bitcast.454), calls=%async_computation.55 | async-start | bytes 4194304 | tf_op jit(solution)/shard_map/while
  1503.2 44.4 %slice-start = ((s8[10485760]{0:T(1024)(128)(4,1)}), s8[2097152]{0:T(1024)(128)(4,1)S(1)}, s32[]{:S(2)}) async-start(s8[10485760]{0:T(1024)(128)(4,1)} %bitcast.454), calls=%async_computation.55 | async-start | bytes 4194304 | tf_op jit(solution)/shard_map/while
  1646.8 36.0 %copy-start.7 = (bf16[512,10,96]{0,2,1:T(8,128)(2,1)S(1)}, bf16[512,10,96]{0,2,1:T(8,128)(2,1)}, u32[]{:S(2)}) copy-start(bf16[512,10,96]{0,2,1:T(8,128)(2,1)} %copy-done.6) | copy-start | bytes 2949124 | tf_op jit(solution)/shard_map/while
  1646.8 43.7 %slice-start.3 = ((s8[10485760]{0:T(1024)(128)(4,1)}), s8[2097152]{0:T(1024)(128)(4,1)S(1)}, s32[]{:S(2)}) async-start(s8[10485760]{0:T(1024)(128)(4,1)} %bitcast.456), calls=%async_computation.58 | async-start | bytes 4194304 | tf_op jit(solution)/shard_map/while
  1768.6 36.0 %copy-start.7 = (bf16[512,10,96]{0,2,1:T(8,128)(2,1)S(1)}, bf16[512,10,96]{0,2,1:T(8,128)(2,1)}, u32[]{:S(2)}) copy-start(bf16[512,10,96]{0,2,1:T(8,128)(2,1)} %copy-done.6) | copy-start | bytes 2949124 | tf_op jit(solution)/shard_map/while
  1768.6 44.4 %slice-start.3 = ((s8[10485760]{0:T(1024)(128)(4,1)}), s8[2097152]{0:T(1024)(128)(4,1)S(1)}, s32[]{:S(2)}) async-start(s8[10485760]{0:T(1024)(128)(4,1)} %bitcast.456), calls=%async_computation.58 | async-start | bytes 4194304 | tf_op jit(solution)/shard_map/while
  1828.4 189.2 %reduce-scatter.35.cloned.1.call-start = ((), (), s32[]{:S(2)}) async-start(), calls=%async_computation.40 | async-start | bytes 81920 | tf_op jit(solution)/shard_map/reduce_scatter | solution.py:296
  1833.6 185.0 %reduce-scatter.33.cloned.1.call-start = ((), (), s32[]{:S(2)}) async-start(), calls=%async_computation.39 | async-start | bytes 655360 | tf_op jit(solution)/shard_map/reduce_scatter | solution.py:293
  1837.2 183.0 %reduce-scatter.41.cloned.1.call-start = ((), (), s32[]{:S(2)}) async-start(), calls=%async_computation.45 | async-start | bytes 655360 | tf_op jit(solution)/shard_map/reduce_scatter | solution.py:293
  1842.9 184.4 %reduce-scatter.31.cloned.1.call-start = ((), (), s32[]{:S(2)}) async-start(), calls=%async_computation.38 | async-start | bytes 1966080 | tf_op jit(solution)/shard_map/reduce_scatter | solution.py:290
  1864.7 165.6 %reduce-scatter.39.cloned.1.call-start = ((), (), s32[]{:S(2)}) async-start(), calls=%async_computation.44 | async-start | bytes 1966080 | tf_op jit(solution)/shard_map/reduce_scatter | solution.py:290
  1871.3 224.9 %reduce-scatter.57.cloned.1.call-start = ((), (), s32[]{:S(2)}) async-start(), calls=%async_computation.53 | async-start | bytes 9584640 | tf_op jit(solution)/shard_map/reduce_scatter | solution.py:114
  1903.9 283.9 %reduce-scatter.55.cloned.1.call-start = ((), (), s32[]{:S(2)}) async-start(), calls=%async_computation.52 | async-start | bytes 9584640 | tf_op jit(solution)/shard_map/reduce_scatter | solution.py:111
  1938.2 341.2 %reduce-scatter.59.cloned.1.call-start = ((), (), s32[]{:S(2)}) async-start(), calls=%async_computation.54 | async-start | bytes 9584640 | tf_op jit(solution)/shard_map/reduce_scatter | solution.py:117
  1972.8 338.5 %reduce-scatter.51.cloned.1.call-start = ((), (), s32[]{:S(2)}) async-start(), calls=%async_computation.50 | async-start | bytes 737280 | tf_op jit(solution)/shard_map/reduce_scatter | solution.py:105
  1978.3 368.4 %reduce-scatter.47.cloned.1.call-start = ((), (), s32[]{:S(2)}) async-start(), calls=%async_computation.48 | async-start | bytes 1769472 | tf_op jit(solution)/shard_map/reduce_scatter | solution.py:102
  1985.1 426.1 %reduce-scatter.23.cloned.1.call-start = ((), (), s32[]{:S(2)}) async-start(), calls=%async_computation.30 | async-start | bytes 6553600 | tf_op jit(solution)/shard_map/reduce_scatter | solution.py:205
  2000.0 454.7 %reduce-scatter.53.cloned.1.call-start = ((), (), s32[]{:S(2)}) async-start(), calls=%async_computation.51 | async-start | bytes 3686400 | tf_op jit(solution)/shard_map/reduce_scatter | solution.py:108
  2016.7 546.8 %reduce-scatter.49.cloned.1.call-start = ((), (), s32[]{:S(2)}) async-start(), calls=%async_computation.49 | async-start | bytes 4055040 | tf_op jit(solution)/shard_map/reduce_scatter | solution.py:97
  2027.0 664.2 %reduce-scatter.45.cloned.1.call-start = ((), (), s32[]{:S(2)}) async-start(), calls=%async_computation.47 | async-start | bytes 8110080 | tf_op jit(solution)/shard_map/reduce_scatter | solution.py:95
  2355.9 55.2 %copy-start.89 = (f32[2560]{0:T(1024)S(1)}, f32[2560]{0:T(1024)}, u32[]{:S(2)}) copy-start(f32[2560]{0:T(1024)} %copy-done.87) | copy-start | bytes 30724
  2355.9 55.2 %copy-start.118 = (f32[256]{0:T(256)S(1)}, f32[256]{0:T(256)}, u32[]{:S(2)}) copy-start(f32[256]{0:T(256)} %copy-done.116) | copy-start | bytes 3076
  2356.0 55.2 %copy-start.134 = (f32[256]{0:T(256)S(1)}, f32[256]{0:T(256)}, u32[]{:S(2)}) copy-start(f32[256]{0:T(256)} %copy-done.133) | copy-start | bytes 3076
  (162 other events, 869.4 us)
Sparse Core Ops, SparseCore 0:
  10.9 63.9 all-gather.15
  77.8 54.9 all-gather.21
  134.4 23.8 all-gather.19
  160.6 32.4 all-gather.33
  195.3 31.1 all-gather.17
  228.0 39.3 all-gather.23
  362.5 61.4 reduce-scatter.24
  472.5 62.3 reduce-scatter.20
  536.5 83.1 all-gather.27
  621.9 59.9 all-gather.35
  683.5 83.1 all-gather.29
  768.9 59.9 all-gather.41
  830.6 83.1 all-gather.31
  916.0 59.9 all-gather.25
  977.7 61.4 all-gather.37
  1042.0 61.4 reduce-scatter.36
  1106.9 61.4 reduce-scatter.28
  1171.2 61.4 reduce-scatter.26
  1238.9 61.4 all-gather.39
  1302.0 61.4 all-gather.43
  1828.6 23.6 reduce-scatter.42
  1855.8 23.6 reduce-scatter.34
  1882.4 24.7 reduce-scatter.32
  1910.1 24.7 reduce-scatter.40
  1937.9 30.8 reduce-scatter.30
  1972.2 30.9 reduce-scatter.38
  2005.4 90.8 reduce-scatter.56
  2098.6 89.1 reduce-scatter.54
  2190.2 89.2 reduce-scatter.58
  2281.7 29.5 reduce-scatter.50
  2314.2 32.4 reduce-scatter.46
  2350.6 60.5 reduce-scatter.22
  2413.4 41.3 reduce-scatter.52
  2460.7 102.6 reduce-scatter.48
  2569.7 121.4 reduce-scatter.44
where the time goes:
time: 2720 us; the launch traced here: 2700 us
  waiting for transfers between devices  1280 us (47%)
  matrix products  787 us (29%)
  local copies, waits for them, and re-layouts  270 us (10%)
  other arithmetic  201 us (7%)
  blocking collectives  141 us (5%)
    dynamic_update_slice x8, local copies, waits for them, and re-layouts, layer_pass(): lax.scan(back_block, initial, (query_blocks, grad_blocks, log_totals, sta...  157 us
    dot_general x16, matrix products, product_nt(): lax.dot_general(left_side, right_side, (((1,), (1,)), ((), ())), preferre...  135 us
    dot_general x8, matrix products, block_scores(): jnp.einsum('qhd,khd->hqk', query_part[..., :NOPE], key_nope, preferred_el...  134 us
    dot_general x16, matrix products, product_tn(): lax.dot_general(left_side, right_side, (((0,), (0,)), ((), ())), preferre...  133 us
    dot_general x16, matrix products, product(): return jnp.dot(left_side, right_side, preferred_element_type=jnp.float32)  130 us
    reduce_scatter x1, waiting for transfers between devices, reduce_grads(): lax.psum_scatter(latent_grads[1], ('dp', 'tensor'), scatter_dimension=0,...  128 us
    reduce_scatter x1, waiting for transfers between devices, reduce_grads(): lax.psum_scatter(latent_grads[3], ('dp', 'tensor'), scatter_dimension=0,...  107 us
    reduce_scatter x1, waiting for transfers between devices, reduce_grads(): lax.psum_scatter(head_grads[3].astype(jnp.bfloat16), 'dp', scatter_dimens...  88.9 us
  transfers between devices with their start and end apart: 35, of which 23 were waited for; matrix products, arithmetic and copies ran while one was open for 35% of the time, Pallas kernels for 0%

commit v1 on v0

v1 whole, which is shorter than its diff:
```python
import math

import jax
import jax.numpy as jnp
from jax import lax
from jax.experimental import pallas as pl
from jax.experimental.pallas import tpu as pltpu
from jax.sharding import Mesh
from jax.sharding import PartitionSpec as P

NOPE = 64
ROPE = 32
VD = 64
KVR = 256
HEAD = NOPE + ROPE
PREFIX_MAX = 512
BLOCK = 256

DP = ("ring", "core")
EVERYWHERE = ("ring", "core", "tensor")

EPSILON = 1e-05
RESIDUAL = 1.4 / math.sqrt(62.0)
NEGATIVE = -1e30
ROPE_BASE = 10000.0
SCALE = HEAD ** (-0.5)

BF16 = jnp.bfloat16
F32 = jnp.float32


def dot(left_side, right_side, left_dim, right_dim):
    return lax.dot_general(
        left_side, right_side, (((left_dim,), (right_dim,)), ((), ())), preferred_element_type=F32
    )


def inverse_rms(values):
    return lax.rsqrt(jnp.mean(values * values, axis=-1, keepdims=True) + EPSILON)


def norm_back(values, gain_vec, grad_out):
    scale_inv = inverse_rms(values)
    normal = values * scale_inv
    grad_norm = grad_out * gain_vec
    grad_values = scale_inv * (
        grad_norm - normal * jnp.mean(grad_norm * normal, axis=-1, keepdims=True)
    )
    return (grad_values, jnp.sum(grad_out * normal, axis=0))


def rotary(row_count, row_start):
    half_width = ROPE // 2
    frequency = ROPE_BASE ** (-2.0 * jnp.arange(half_width).astype(F32) / ROPE)
    angles = (row_start + jnp.arange(row_count)).astype(F32)[:, None] * frequency[None, :]
    return (jnp.cos(angles), jnp.sin(angles))


def rotate(values, cosine, sine_table, axis=-1):
    first_half, second_half = jnp.split(values, 2, axis=axis)
    return jnp.concatenate(
        [
            first_half * cosine - second_half * sine_table,
            second_half * cosine + first_half * sine_table,
        ],
        axis=axis,
    )


def key_width(block_index, seq_length):
    return min(max((block_index + 1) * BLOCK, PREFIX_MAX), seq_length)


def block_scores(keys, query_block, block_index, width, prefix_len):
    scores = jnp.dot(keys[:width], query_block, preferred_element_type=F32)
    first = block_index * BLOCK
    tail = scores[first:]
    key_at = first + lax.broadcasted_iota(jnp.int32, tail.shape, 0)
    query_at = first + lax.broadcasted_iota(jnp.int32, tail.shape, 1)
    tail = jnp.where((key_at <= query_at) | (key_at < prefix_len), tail, NEGATIVE)
    if first:
        return jnp.concatenate([scores[:first], tail], axis=0)
    return tail


def attend_kernel(prefix_ref, query_ref, keyval_ref, rope_ref, out_ref, log_ref):
    seq_length = query_ref.shape[-1]
    prefix_len = prefix_ref[0]
    keyval = keyval_ref[0]
    keys = jnp.concatenate([keyval[:NOPE], rope_ref[...]], axis=0).T
    values_t = keyval[NOPE:]
    for block_index in range(seq_length // BLOCK):
        at = pl.ds(block_index * BLOCK, BLOCK)
        width = key_width(block_index, seq_length)
        scores = block_scores(keys, query_ref[0, :, at], block_index, width, prefix_len)
        peak = jnp.max(scores, axis=0, keepdims=True)
        exp_scores = jnp.exp((scores - peak) * SCALE)
        total = jnp.sum(exp_scores, axis=0, keepdims=True)
        block_out = jnp.dot(
            values_t[:, :width], exp_scores.astype(BF16), preferred_element_type=F32
        )
        out_ref[0, :, at] = (block_out / total).astype(BF16)
        log_ref[0, :, at] = peak * SCALE + jnp.log(total)


def attend(prefix_len, queries_t, keyval_t, rope_t):
    heads, _, seq_length = queries_t.shape
    head_block = lambda rows: pl.BlockSpec((1, rows, seq_length), lambda h: (h, 0, 0))
    return pl.pallas_call(
        attend_kernel,
        grid=(heads,),
        in_specs=[
            pl.BlockSpec(memory_space=pltpu.SMEM),
            head_block(HEAD),
            head_block(NOPE + VD),
            pl.BlockSpec((ROPE, seq_length), lambda h: (0, 0)),
        ],
        out_specs=[head_block(VD), head_block(1)],
        out_shape=[
            jax.ShapeDtypeStruct((heads, VD, seq_length), BF16),
            jax.ShapeDtypeStruct((heads, 1, seq_length), F32),
        ],
        compiler_params=pltpu.CompilerParams(vmem_limit_bytes=40 * 2**20),
        cost_estimate=pl.CostEstimate(
            flops=2 * heads * seq_length * seq_length * 384,
            bytes_accessed=heads * seq_length * 600,
            transcendentals=heads * seq_length * seq_length,
        ),
        name="attend",
    )(prefix_len, queries_t, keyval_t, rope_t)


def attend_back_kernel(
    prefix_ref,
    query_ref,
    keyval_ref,
    rope_ref,
    grad_ref,
    log_ref,
    cos_ref,
    sin_ref,
    dquery_ref,
    dkeyval_ref,
    drope_ref,
    dkey_acc,
    dvalue_acc,
):
    seq_length = query_ref.shape[-1]
    prefix_len = prefix_ref[0]
    keyval = keyval_ref[0]
    keys_t = jnp.concatenate([keyval[:NOPE], rope_ref[...]], axis=0)
    keys = keys_t.T
    values = keyval[NOPE:].T
    dkey_acc[...] = jnp.zeros_like(dkey_acc)
    dvalue_acc[...] = jnp.zeros_like(dvalue_acc)
    for block_index in range(seq_length // BLOCK):
        at = pl.ds(block_index * BLOCK, BLOCK)
        width = key_width(block_index, seq_length)
        query_block = query_ref[0, :, at]
        grad_block = grad_ref[0, :, at]
        scores = block_scores(keys, query_block, block_index, width, prefix_len)
        soft = jnp.exp(scores * SCALE - log_ref[0, :, at])
        grad_probs = jnp.dot(values[:width], grad_block, preferred_element_type=F32)
        delta = jnp.sum(soft * grad_probs, axis=0, keepdims=True)
        grad_scores = (soft * (grad_probs - delta)).astype(BF16)
        dquery = SCALE * jnp.dot(keys_t[:, :width], grad_scores, preferred_element_type=F32)
        dquery_ref[0, :NOPE, at] = dquery[:NOPE].astype(BF16)
        dquery_ref[0, NOPE:, at] = rotate(
            dquery[NOPE:], cos_ref[:, at], -sin_ref[:, at], axis=0
        ).astype(BF16)
        dkey_acc[:, :width] += dot(query_block, grad_scores, 1, 1)
        dvalue_acc[:, :width] += dot(grad_block, soft.astype(BF16), 1, 1)
    dkeyval_ref[0, :NOPE, :] = (SCALE * dkey_acc[:NOPE, :]).astype(BF16)
    dkeyval_ref[0, NOPE:, :] = dvalue_acc[...].astype(BF16)
    rope_part = SCALE * dkey_acc[NOPE:, :]

    @pl.when(pl.program_id(0) == 0)
    def _():
        drope_ref[...] = rope_part

    @pl.when(pl.program_id(0) > 0)
    def _():
        drope_ref[...] += rope_part


def attend_back(prefix_len, queries_t, keyval_t, rope_t, grad_t, logs, cos_t, sin_t):
    heads, _, seq_length = queries_t.shape
    head_block = lambda rows: pl.BlockSpec((1, rows, seq_length), lambda h: (h, 0, 0))
    whole = lambda rows: pl.BlockSpec((rows, seq_length), lambda h: (0, 0))
    return pl.pallas_call(
        attend_back_kernel,
        grid=(heads,),
        in_specs=[
            pl.BlockSpec(memory_space=pltpu.SMEM),
            head_block(HEAD),
            head_block(NOPE + VD),
            whole(ROPE),
            head_block(VD),
            head_block(1),
            whole(ROPE // 2),
            whole(ROPE // 2),
        ],
        out_specs=[head_block(HEAD), head_block(NOPE + VD), whole(ROPE)],
        out_shape=[
            jax.ShapeDtypeStruct((heads, HEAD, seq_length), BF16),
            jax.ShapeDtypeStruct((heads, NOPE + VD, seq_length), BF16),
            jax.ShapeDtypeStruct((ROPE, seq_length), F32),
        ],
        scratch_shapes=[
            pltpu.VMEM((HEAD, seq_length), F32),
            pltpu.VMEM((VD, seq_length), F32),
        ],
        compiler_params=pltpu.CompilerParams(vmem_limit_bytes=40 * 2**20),
        cost_estimate=pl.CostEstimate(
            flops=2 * heads * seq_length * seq_length * 960,
            bytes_accessed=heads * seq_length * 1100,
            transcendentals=heads * seq_length * seq_length,
        ),
        name="attend_back",
    )(prefix_len, queries_t, keyval_t, rope_t, grad_t, logs, cos_t, sin_t)


def weight_grad_kernel(*refs):
    out_ref = refs[-1]
    pairs = len(refs) // 2
    total = None
    for left_ref, right_ref in zip(refs[:pairs], refs[pairs:]):
        term = dot(left_ref[...], right_ref[...], 0, 0)
        total = term if total is None else total + term
    out_ref[...] = total.astype(BF16)


def weight_grad(lefts, rights):
    tokens, rows = lefts[0].shape
    columns = rights[0].shape[1]
    tile = 512 if rows % 512 == 0 else rows
    return pl.pallas_call(
        weight_grad_kernel,
        grid=(rows // tile,),
        in_specs=[pl.BlockSpec((tokens, tile), lambda i: (0, i))] * len(lefts)
        + [pl.BlockSpec((tokens, columns), lambda i: (0, 0))] * len(rights),
        out_specs=pl.BlockSpec((tile, columns), lambda i: (i, 0)),
        out_shape=jax.ShapeDtypeStruct((rows, columns), BF16),
        compiler_params=pltpu.CompilerParams(vmem_limit_bytes=56 * 2**20),
        cost_estimate=pl.CostEstimate(
            flops=2 * len(lefts) * tokens * rows * columns,
            bytes_accessed=2 * (len(lefts) * tokens * (rows + columns) + rows * columns),
            transcendentals=0,
        ),
        name="weight_grad",
    )(*lefts, *rights)


def swap(values, bit):
    return lax.ppermute(values, "tensor", [(index, index ^ bit) for index in range(4)])


def gather_blocks(values, hold=()):
    half = values.shape[0] // 2
    from_x = swap(values, 1)
    from_y = swap(values, 2)
    if hold:
        from_x, from_y = after((from_x, from_y), *hold)
    far_top = swap(from_y[:half], 1)
    far_low = swap(from_x[half:], 2)
    return (values, from_x, far_top, far_low, from_y)


def two_by_two():
    return lax.axis_size("tensor") == 4


def gather_ring(values, hold=()):
    if not two_by_two():
        return lax.all_gather(values, "tensor", axis=0, tiled=True)
    return jnp.concatenate(gather_blocks(values, hold), axis=0)


def scatter_ring(part):
    if not two_by_two():
        total = part("all", None).astype(BF16)
        return lax.psum_scatter(total, "tensor", scatter_dimension=0, tiled=True).astype(F32)
    rx = swap(part("xd", 0).astype(BF16), 1)
    ry = swap(part("dy", 1).astype(BF16), 2)
    rows = rx.shape[0] // 2
    to_y = (part("y", 0) + rx[rows:].astype(F32)).astype(BF16)
    to_x = (part("x", 1) + ry[:rows].astype(F32)).astype(BF16)
    ry2 = swap(to_y, 2)
    rx2 = swap(to_x, 1)
    left = part("o", 0) + rx[:rows].astype(F32) + ry2.astype(F32)
    right = part("o", 1) + ry[rows:].astype(F32) + rx2.astype(F32)
    return jnp.concatenate([left, right], axis=-1)


RING = {"o": (0, 1), "x": (1, 1), "xd": (1, 2), "dy": (2, 2), "y": (3, 1)}
FLIP = {"o": 0, "x": 1, "d": 3, "y": 2}


def ring_rows(values, names, rows):
    if names == "all":
        return values
    start, count = RING[names]
    return values[start * rows : (start + count) * rows]


def half_rows(weight, half):
    if half is None:
        return weight
    size = weight.shape[0] // 2
    return weight[half * size : (half + 1) * size]


def half_columns(values, half):
    if half is None:
        return values
    split = round(values.shape[1] / 256) * 128
    return values[:, split:] if half else values[:, :split]


def after(values, *others):
    return lax.optimization_barrier((values, *others))[0]


def widen(values, columns):
    return jnp.pad(values, ((0, 0), (0, columns - values.shape[1])))


def swap_cores(values):
    return lax.ppermute(values, "core", [(0, 1), (1, 0)])


def gather_everywhere(values):
    if not two_by_two():
        return lax.all_gather(values, EVERYWHERE, axis=0, tiled=True)
    rows, columns = values.shape
    own = lax.all_gather(values, DP, axis=0, tiled=True)
    size = own.shape[0] // 2
    core = lax.axis_index("core")
    tensor_at = lax.axis_index("tensor")
    mine = gather_ring(lax.dynamic_slice_in_dim(own, core * size, size, 0))
    other = swap_cores(mine)
    result = jnp.zeros((2, size // rows, 4, rows, columns), values.dtype)
    for side, pieces in ((core, mine), (1 - core, other)):
        for index, bit in enumerate((0, 1, 3, 2)):
            piece = pieces[index * size : (index + 1) * size]
            result = lax.dynamic_update_slice(
                result,
                piece.reshape(1, size // rows, 1, rows, columns),
                (side, 0, tensor_at ^ bit, 0, 0),
            )
    return result.reshape(-1, columns)


def scatter_everywhere(values, last_after):
    if not two_by_two():
        return lax.psum_scatter(values, EVERYWHERE, scatter_dimension=0, tiled=True)
    columns = values.shape[1]
    ring = lax.axis_size("ring")
    rows = values.shape[0] // (ring * 8)
    core = lax.axis_index("core")
    tensor_at = lax.axis_index("tensor")
    blocks = values.reshape(ring, 2, 4, rows, columns)
    pick = lambda index: lax.dynamic_slice_in_dim(blocks, index, 1, 1)[:, 0]
    chip = pick(core).astype(F32) + swap_cores(pick(1 - core)).astype(F32)
    chip = chip.astype(BF16)

    def part(names, half):
        pieces = [
            lax.dynamic_slice_in_dim(chip, tensor_at ^ FLIP[name], 1, 1).reshape(-1, columns)
            for name in names
        ]
        return half_columns(jnp.concatenate(pieces, axis=0), half).astype(F32)

    mine = after(scatter_ring(part).astype(BF16), *last_after)
    return lax.psum_scatter(mine, "ring", scatter_dimension=0, tiled=True)


def body(
    tokens,
    prefix,
    input_gain,
    query_down,
    query_gain,
    query_up,
    latent_down,
    latent_gain,
    latent_up,
    out_proj,
    post_gain,
    gate_proj,
    up_proj,
    down_proj,
    cotangent,
):
    micros = range(tokens.shape[0])
    rows = tokens.shape[1]
    width = tokens.shape[2]
    tensor_at = lax.axis_index("tensor")
    devices = lax.axis_size(EVERYWHERE)
    dp_size = lax.axis_size(DP)
    seq_length = rows * lax.axis_size("tensor")
    query_rank = query_down.shape[1]
    latent_rank = latent_down.shape[1]
    down_rank = query_rank + latent_rank
    packed_width = -(-(down_rank + 3) // 128) * 128
    own_rows = input_gain.shape[0]
    query_own = query_gain.shape[0]
    latent_own = latent_gain.shape[0]

    def gather_dp(values):
        return lax.all_gather(values, DP, axis=0, tiled=True)

    def scatter_dp(values):
        return lax.psum_scatter(values, DP, scatter_dimension=0, tiled=True)

    small = jnp.zeros((own_rows,), BF16)
    small = small.at[:query_own].set(query_gain)
    small = small.at[query_own : query_own + latent_own].set(latent_gain)
    packed = gather_everywhere(
        widen(
            jnp.concatenate(
                [query_down, latent_down, input_gain[:, None], post_gain[:, None], small[:, None]],
                axis=1,
            ),
            packed_width,
        )
    )
    query_rows, query_columns = query_up.shape
    latent_rows, latent_columns = latent_up.shape
    ups = gather_dp(jnp.concatenate([widen(query_up, latent_columns), latent_up], axis=0))
    ups = ups.reshape(dp_size, query_rows + latent_rows, latent_columns)
    up_query = ups[:, :query_rows, :query_columns].reshape(-1, query_columns)
    up_latent = ups[:, query_rows:].reshape(-1, latent_columns)
    out_t = gather_dp(out_proj.T)
    proj_gate = gather_dp(gate_proj)
    proj_up = gather_dp(up_proj)
    down_t = gather_dp(down_proj.T)

    gains = packed[:, down_rank : down_rank + 3].astype(F32)
    gain_in = gains[:, 0]
    gain_post = gains[:, 1]
    small_all = gains[:, 2].reshape(devices, own_rows)
    gain_query = small_all[:, :query_own].reshape(query_rank)
    gain_latent = small_all[:, query_own : query_own + latent_own].reshape(KVR)

    first_row = tensor_at * rows
    cos_local, sin_local = rotary(rows, first_row)
    cos_all, sin_all = rotary(seq_length, 0)
    cos_t, sin_t = cos_all.T, sin_all.T
    heads = up_query.shape[1] // HEAD

    def true_order(values):
        if not two_by_two():
            return lax.all_gather(values, "tensor", axis=0, tiled=True)
        own, from_x, far_top, far_low, from_y = gather_blocks(values)
        far = jnp.concatenate([far_top, far_low], axis=0)
        result = jnp.zeros((seq_length, values.shape[1]), values.dtype)
        for bit, piece in ((0, own), (1, from_x), (2, from_y), (3, far)):
            result = lax.dynamic_update_slice(result, piece, ((tensor_at ^ bit) * rows, 0))
        return result

    def true_block(values, name, axis):
        return lax.dynamic_slice_in_dim(values, (tensor_at ^ FLIP[name]) * rows, rows, axis)

    def true_rows(values, names, axis):
        if names == "all":
            return values
        pieces = [true_block(values, name, axis) for name in names]
        return pieces[0] if len(pieces) == 1 else jnp.concatenate(pieces, axis=axis)

    residual = tokens.reshape(-1, width).astype(F32)
    normed = (residual * inverse_rms(residual) * gain_in).astype(BF16)
    lat = dot(normed, packed, 1, 0)
    query_lat = lat[:, :query_rank]
    latent_comp = lat[:, query_rank : query_rank + KVR]
    query_comp = (query_lat * inverse_rms(query_lat) * gain_query).astype(BF16)
    latent_norm = (latent_comp * inverse_rms(latent_comp) * gain_latent).astype(BF16)
    cos_both = jnp.concatenate([cos_local for micro in micros], axis=0)
    sin_both = jnp.concatenate([sin_local for micro in micros], axis=0)
    key_rope = rotate(lat[:, query_rank + KVR : down_rank], cos_both, sin_both).astype(BF16)
    latents = jnp.concatenate([query_comp, latent_norm, key_rope], axis=1)

    def of_micro(values, micro):
        return values[micro * rows : (micro + 1) * rows]

    state = []
    for micro in micros:
        full = true_order(of_micro(latents, micro))
        state.append(
            dict(
                query_full=full[:, :query_rank],
                latent_full=full[:, query_rank : query_rank + KVR],
                rope_t=full[:, query_rank + KVR :].T,
            )
        )

    def gather_branch(micro, start_after, hold):
        branch = (RESIDUAL * cotangent[micro].astype(F32)).astype(BF16)
        return gather_ring(after(branch, start_after), (hold,))

    for micro in micros:
        st = state[micro]
        raw_t = dot(up_query, st["query_full"], 0, 1).reshape(heads, HEAD, seq_length)
        st["queries_t"] = jnp.concatenate(
            [raw_t[:, :NOPE], rotate(raw_t[:, NOPE:], cos_t[None], sin_t[None], axis=1)], axis=1
        ).astype(BF16)
        st["keyval_t"] = (
            dot(up_latent, st["latent_full"], 0, 1)
            .astype(BF16)
            .reshape(heads, NOPE + VD, seq_length)
        )
        attended_t, st["logs"] = attend(
            prefix[micro], st["queries_t"], st["keyval_t"], st["rope_t"]
        )
        st["attended_t"] = attended_t.reshape(heads * VD, seq_length)
        attn_rows = scatter_ring(
            lambda names, half: dot(
                true_rows(st["attended_t"], names, 1), half_rows(out_t, half), 0, 1
            )
        )
        st["middle"] = tokens[micro].astype(F32) + RESIDUAL * attn_rows
        hidden_in = (st["middle"] * inverse_rms(st["middle"]) * gain_post).astype(BF16)
        st["hidden"] = gather_ring(hidden_in)

    state[0]["branch"] = gather_branch(0, state[1]["query_full"], state[0]["attended_t"])

    def add_micros(term):
        total = term(state[0])
        for micro in micros[1:]:
            total = total + term(state[micro])
        return total.astype(BF16)

    state[0]["hidden"] = after(state[0]["hidden"], *[st["attended_t"] for st in state[1:]])
    for micro in micros:
        st = state[micro]
        gate_val = dot(st["hidden"], proj_gate, 1, 0).astype(BF16)
        up_val = dot(st["hidden"], proj_up, 1, 0).astype(BF16)
        gate_val, up_val = lax.optimization_barrier((gate_val, up_val))
        st["gate"], st["up"] = gate_val, up_val
        st["active"] = after(
            (jax.nn.silu(gate_val.astype(F32)) * up_val.astype(F32)).astype(BF16)
        )
    for micro in micros[1:]:
        state[micro]["branch"] = gather_branch(micro, state[0]["hidden"], state[0]["active"])

    def both(name):
        return [st[name] for st in state]

    down_part = weight_grad(both("branch"), both("active"))
    down_grad = scatter_dp(down_part)

    for micro in micros:
        st = state[micro]
        gate_val, up_val = st["gate"].astype(F32), st["up"].astype(F32)
        sigmoid_gate = jax.nn.sigmoid(gate_val)
        grad_active = dot(st["branch"], down_t, 1, 0)
        grad_gate = (
            grad_active * up_val * sigmoid_gate * (1.0 + gate_val * (1.0 - sigmoid_gate))
        ).astype(BF16)
        grad_up = (grad_active * gate_val * sigmoid_gate).astype(BF16)
        grad_gate, grad_up = after((grad_gate, grad_up), down_part)
        st["grad_gate"], st["grad_up"] = grad_gate, grad_up
        grad_hidden = scatter_ring(
            lambda names, half: dot(
                ring_rows(grad_gate, names, rows), half_rows(proj_gate, half), 1, 1
            )
            + dot(ring_rows(grad_up, names, rows), half_rows(proj_up, half), 1, 1)
        )
        grad_mid_norm, st["post_gain_grad"] = norm_back(st["middle"], gain_post, grad_hidden)
        st["grad_mid"] = cotangent[micro].astype(F32) + grad_mid_norm
        st["attn_grad"] = true_order((RESIDUAL * st["grad_mid"]).astype(BF16))
    gate_part = weight_grad(both("hidden"), both("grad_gate"))
    gate_grad = scatter_dp(after(gate_part, down_grad))
    up_part = weight_grad(both("hidden"), both("grad_up"))
    up_grad = scatter_dp(after(up_part, gate_grad))

    for micro in micros:
        st = state[micro]
        attn_grad = after(st["attn_grad"], gate_part, up_part)
        grad_t = dot(out_t, attn_grad, 0, 1).astype(BF16).reshape(heads, VD, seq_length)
        dquery_t, dkeyval_t, drope_t = attend_back(
            prefix[micro],
            st["queries_t"],
            st["keyval_t"],
            st["rope_t"],
            grad_t,
            st["logs"],
            cos_t,
            sin_t,
        )
        st["dquery_t"] = dquery_t.reshape(heads * HEAD, seq_length)
        st["dkeyval_t"] = dkeyval_t.reshape(heads * (NOPE + VD), seq_length)
        comp_part = dot(st["dquery_t"], up_query, 0, 1)
        norm_part = dot(st["dkeyval_t"], up_latent, 0, 1)
        latent_part = jnp.concatenate(
            [comp_part.astype(BF16), norm_part.astype(BF16), drope_t.T.astype(BF16)], axis=1
        )
        st["grad_lat"] = scatter_ring(
            lambda names, half: true_rows(half_columns(latent_part, half), names, 0).astype(F32)
        )

    out_part = add_micros(lambda st: dot(st["attn_grad"], st["attended_t"], 0, 1))
    out_grad = scatter_dp(after(out_part, up_grad))
    query_up_part = add_micros(lambda st: dot(st["query_full"], st["dquery_t"], 0, 1))
    latent_up_part = add_micros(lambda st: dot(st["latent_full"], st["dkeyval_t"], 0, 1))
    ups_part = jnp.concatenate(
        [
            widen(query_up_part, latent_columns).reshape(dp_size, query_rows, latent_columns),
            latent_up_part.reshape(dp_size, latent_rows, latent_columns),
        ],
        axis=1,
    ).reshape(-1, latent_columns)
    ups_grad = scatter_dp(after(ups_part, out_grad))

    grad_lat = jnp.concatenate([st["grad_lat"] for st in state], axis=0)
    grad_qlat, query_gain_grad = norm_back(query_lat, gain_query, grad_lat[:, :query_rank])
    grad_comp, latent_gain_grad = norm_back(
        latent_comp, gain_latent, grad_lat[:, query_rank : query_rank + KVR]
    )
    grad_rope = rotate(grad_lat[:, query_rank + KVR :], cos_both, -sin_both)
    grad_down = widen(
        jnp.concatenate(
            [grad_qlat.astype(BF16), grad_comp.astype(BF16), grad_rope.astype(BF16)], axis=1
        ),
        packed_width,
    )
    grad_normed = dot(grad_down, packed, 1, 1)
    grad_resid, input_gain_grad = norm_back(residual, gain_in, grad_normed)
    small_grad = jnp.concatenate(
        [
            query_gain_grad.reshape(devices, query_own),
            latent_gain_grad.reshape(devices, latent_own),
            jnp.zeros((devices, own_rows - query_own - latent_own), F32),
        ],
        axis=1,
    ).reshape(width)
    post_gain_grad = sum(st["post_gain_grad"] for st in state)
    vectors = jnp.stack([input_gain_grad, post_gain_grad, small_grad], axis=1)
    vectors = jnp.pad(vectors, ((0, 0), (down_rank, packed_width - down_rank - 3)))
    packed_grad = scatter_everywhere(
        (dot(normed, grad_down, 0, 0) + vectors).astype(BF16), (ups_grad,)
    )
    packed_grad = packed_grad.astype(F32)
    d_tokens = [
        st["grad_mid"] + of_micro(grad_resid, micro) for micro, st in enumerate(state)
    ]

    mixed = []
    for micro in micros:
        st = state[micro]
        active = after(st["active"], state[-1]["attn_grad"])
        mlp_rows = scatter_ring(
            lambda names, half: dot(
                ring_rows(active, names, rows), half_rows(down_t, half), 1, 1
            )
        )
        mixed.append((st["middle"] + RESIDUAL * mlp_rows).astype(BF16))

    small_grad = packed_grad[:, down_rank + 2]
    return (
        jnp.stack(mixed, axis=0),
        jnp.stack(d_tokens, axis=0),
        packed_grad[:, down_rank],
        packed_grad[:, :query_rank],
        small_grad[:query_own],
        ups_grad[:query_rows, :query_columns].astype(F32),
        packed_grad[:, query_rank:down_rank],
        small_grad[query_own : query_own + latent_own],
        ups_grad[query_rows:].astype(F32),
        out_grad.T.astype(F32),
        packed_grad[:, down_rank + 1],
        gate_grad.astype(F32),
        up_grad.astype(F32),
        down_grad.T.astype(F32),
    )


def solution(mesh):
    dp_size, tensor_size = mesh.devices.shape
    mesh = Mesh(mesh.devices.reshape(dp_size // 2, 2, tensor_size), EVERYWHERE)
    return jax.shard_map(
        body,
        mesh=mesh,
        in_specs=(
            P(None, EVERYWHERE, None),
            P(None, DP),
            P(EVERYWHERE),
            P(EVERYWHERE, None),
            P(EVERYWHERE),
            P(DP, "tensor"),
            P(EVERYWHERE, None),
            P(EVERYWHERE),
            P(DP, "tensor"),
            P("tensor", DP),
            P(EVERYWHERE),
            P(DP, "tensor"),
            P(DP, "tensor"),
            P("tensor", DP),
            P(None, EVERYWHERE, None),
        ),
        out_specs=(
            P(None, EVERYWHERE, None),
            P(None, EVERYWHERE, None),
            P(EVERYWHERE),
            P(EVERYWHERE, None),
            P(EVERYWHERE),
            P(DP, "tensor"),
            P(EVERYWHERE, None),
            P(EVERYWHERE),
            P(DP, "tensor"),
            P("tensor", DP),
            P(EVERYWHERE),
            P(DP, "tensor"),
            P(DP, "tensor"),
            P("tensor", DP),
        ),
        check_vma=False,
    )
```

time: 2720 us -> 1120 us (0.41)
  waiting for transfers between devices: 1280 us -> 358 us
  matrix products: 787 us -> 298 us
  Pallas kernels: 0 us -> 183 us
  local copies, waits for them, and re-layouts: 270 us -> 107 us
  blocking collectives: 141 us -> 0 us
  other arithmetic: 201 us -> 72.6 us
  starting transfers between devices: 2.05 us -> 76 us
    reduce_scatter x20 -> x6, waiting for transfers between devices: 757 us -> 17.6 us  [the longest x1 16.7 us: scatter_everywhere(): return lax.psum_scatter(mine, 'ring', scatter_dimension=0, tiled=True)]
    all_gather x15 -> x6, waiting for transfers between devices: 514 us -> 23.6 us  [the longest x1 23.6 us: gather_everywhere(): own = lax.all_gather(values, DP, axis=0, tiled=True)]
    dot_general x92 -> x73, matrix products: 787 us -> 298 us  [dot(): lax.dot_general(left_side, right_side, (((left_dim,), (right_dim,)), ((),...]
    ppermute x0 -> x74, waiting for transfers between devices: none -> 315 us  [the longest x72 315 us: swap(): lax.ppermute(values, 'tensor', [(index, index ^ bit) for index in range(4)])]
    pallas_call x0 -> x7, Pallas kernels: none -> 183 us  [the longest x3 75.3 us: weight_grad(): pl.pallas_call(weight_grad_kernel, grid=(rows // tile,), in_specs=[pl.Blo...]
    dynamic_update_slice x8 -> x17, local copies, waits for them, and re-layouts: 157 us -> 13.7 us  [the longest x9 10.5 us: true_order(): lax.dynamic_update_slice(result, piece, ((tensor_at ^ bit) * rows, 0))]
    unnamed x2 -> x0, blocking collectives: 81 us -> none
    ppermute x0 -> x74, starting transfers between devices: none -> 74.8 us  [the longest x72 74.7 us: swap(): lax.ppermute(values, 'tensor', [(index, index ^ bit) for index in range(4)])]
  transfers between devices with their start and end apart: 35 -> 86, of which waited for: 23 -> 39; matrix products, arithmetic and copies ran while one was open for 35% -> 38% of each run, Pallas kernels for 0% -> 14%
where the time goes in v1:
time: 1120 us; the launch traced here: 1110 us
  waiting for transfers between devices  358 us (32%)
  matrix products  298 us (27%)
  Pallas kernels  183 us (16%)
  local copies, waits for them, and re-layouts  107 us (10%)
  starting transfers between devices  76 us (7%)
  other arithmetic  72.6 us (6%)
  between operations  17.4 us (2%)
    ppermute x72, waiting for transfers between devices, swap(): lax.ppermute(values, 'tensor', [(index, index ^ bit) for index in range(4)])  315 us
    dot_general x73, matrix products, dot(): lax.dot_general(left_side, right_side, (((left_dim,), (right_dim,)), ((),...  298 us
    pallas_call x3, Pallas kernels, weight_grad(): pl.pallas_call(weight_grad_kernel, grid=(rows // tile,), in_specs=[pl.Blo...  75.3 us
    ppermute x72, starting transfers between devices, swap(): lax.ppermute(values, 'tensor', [(index, index ^ bit) for index in range(4)])  74.7 us
    pallas_call x2, Pallas kernels, attend_back(): pl.pallas_call(attend_back_kernel, grid=(heads,), in_specs=[pl.BlockSpec(...  61 us
    pallas_call x2, Pallas kernels, attend(): pl.pallas_call(attend_kernel, grid=(heads,), in_specs=[pl.BlockSpec(memor...  47 us
    unnamed x360, local copies, waits for them, and re-layouts  43.2 us
    all_gather x1, waiting for transfers between devices, gather_everywhere(): own = lax.all_gather(values, DP, axis=0, tiled=True)  23.6 us
  transfers between devices with their start and end apart: 86, of which 39 were waited for; matrix products, arithmetic and copies ran while one was open for 38% of the time, Pallas kernels for 14%

profile of v1, /device:TPU:0, one launch (start us, length us, event | category | flops | bytes accessed | tf_op | source)
XLA Modules:
  0.0 1111.2 jit_solution(7748413241958043752)
XLA Ops:
  15.9 23.6 %all-gather.9.cloned.1.call-done = bf16[640,1152]{1,0:T(8,128)(2,1)} async-done(((bf16[80,1152]{1,0:T(8,128)(2,1)}), bf16[640,1152]{1,0:T(8,128)(2,1)}) %all-gather.9.cloned.1.call-update) | async-done | bytes 1474576 | tf_op jit(solution)/shard_map/all_gather | solution.py:336
  44.8 15.9 %collective-permute-done.1 = bf16[320,1152]{1,0:T(8,128)(2,1)S(1)} collective-permute-done((bf16[320,1152]{1,0:T(8,128)(2,1)}, bf16[320,1152]{1,0:T(8,128)(2,1)S(1)}, u32[]{:S(2)}, u32[]{:S(2)}) %collective-permute-start.1) | collective-permute-done | bytes 737312 | tf_op jit(solution)/shard_map/ppermute | solution.py:255
  92.6 3.3 fusion.236
  110.7 6.5 collective-permute-done.18
  121.3 7.5 collective-permute-done.6
  137.6 25.0 %collective-permute-done.20 = bf16[128,1056]{0,1:T(8,128)(2,1)S(1)} collective-permute-done((bf16[128,1056]{0,1:T(8,128)(2,1)S(1)}, bf16[128,1056]{0,1:T(8,128)(2,1)S(1)}, u32[]{:S(2)}, u32[]{:S(2)}) %collective-permute-start.20) | collective-permute-done | bytes 270368 | tf_op jit(solution)/shard_map/ppermute | solution.py:255
  177.9 23.4 %attend.3 = (bf16[10,64,1024]{2,1,0:T(8,128)(2,1)S(1)}, f32[10,1,1024]{2,1,0:T(1,128)S(1)}) custom-call(s32[1]{0:T(128)} %bitcast.28.prefix_ref, bf16[10,96,1024]{2,1,0:T(8,128)(2,1)S(1)} %pad_maximum_fusion.6.query_ref, bf16[10,128,1024]{2,1,0:T(8,128)(2,1)S(1)} %bitcast.190, bf16[32,1024]{1,0:T(8,128)(2,1)S(1)} %slice_bitcast_fusion.rope_ref), custom_call_target="tpu_custom_call" | custom-call | flops 8053063680 | bytes 6144000 | tf_op jit(solution)/shard_map/attend/pallas_call | solution.py:109
  210.1 23.6 %attend.2 = (bf16[10,64,1024]{2,1,0:T(8,128)(2,1)S(1)}, f32[10,1,1024]{2,1,0:T(1,128)S(1)}) custom-call(s32[1]{0:T(128)} %bitcast.prefix_ref, bf16[10,96,1024]{2,1,0:T(8,128)(2,1)S(1)} %pad_maximum_fusion.5.query_ref, bf16[10,128,1024]{2,1,0:T(8,128)(2,1)S(1)} %bitcast.188, bf16[32,1024]{1,0:T(8,128)(2,1)S(1)} %slice_bitcast_fusion.1.rope_ref), custom_call_target="tpu_custom_call" | custom-call | flops 8053063680 | bytes 6144000 | tf_op jit(solution)/shard_map/attend/pallas_call | solution.py:109
  248.2 18.7 %collective-permute-done.9 = bf16[512,1280]{1,0:T(8,128)(2,1)S(1)} collective-permute-done((bf16[512,1280]{1,0:T(8,128)(2,1)S(1)}, bf16[512,1280]{1,0:T(8,128)(2,1)S(1)}, u32[]{:S(2)}, u32[]{:S(2)}) %collective-permute-start.9) | collective-permute-done | bytes 1310752 | tf_op jit(solution)/shard_map/ppermute | solution.py:255
  270.9 26.8 %collective-permute-done.22 = bf16[256,1280]{1,0:T(8,128)(2,1)S(1)} collective-permute-done((bf16[256,1280]{1,0:T(8,128)(2,1)S(1)}, bf16[256,1280]{1,0:T(8,128)(2,1)S(1)}, u32[]{:S(2)}, u32[]{:S(2)}) %collective-permute-start.22) | collective-permute-done | bytes 655392 | tf_op jit(solution)/shard_map/ppermute | solution.py:255
  298.7 10.7 collective-permute-done.10
  322.6 25.2 %collective-permute-done.30 = bf16[256,2560]{1,0:T(8,128)(2,1)S(1)} collective-permute-done((bf16[256,2560]{1,0:T(8,128)(2,1)S(1)}, bf16[256,2560]{1,0:T(8,128)(2,1)S(1)}, u32[]{:S(2)}, u32[]{:S(2)}) %collective-permute-start.30) | collective-permute-done | bytes 1310752 | tf_op jit(solution)/shard_map/ppermute | solution.py:255
  350.1 25.8 %collective-permute-done.14 = bf16[256,2560]{1,0:T(8,128)(2,1)S(1)} collective-permute-done((bf16[256,2560]{1,0:T(8,128)(2,1)S(1)}, bf16[256,2560]{1,0:T(8,128)(2,1)S(1)}, u32[]{:S(2)}, u32[]{:S(2)}) %collective-permute-start.14) | collective-permute-done | bytes 1310752 | tf_op jit(solution)/shard_map/ppermute | solution.py:255
  379.4 20.8 %collective-permute-done.15 = bf16[128,2560]{1,0:T(8,128)(2,1)S(1)} collective-permute-done((bf16[128,2560]{1,0:T(8,128)(2,1)S(1)}, bf16[128,2560]{1,0:T(8,128)(2,1)S(1)}, u32[]{:S(2)}, u32[]{:S(2)}) %collective-permute-start.15) | collective-permute-done | bytes 655392 | tf_op jit(solution)/shard_map/ppermute | solution.py:255
  407.4 15.3 %convolution_convert_fusion.2 = bf16[1024,1600]{1,0:T(8,128)(2,1)} fusion(bf16[1024,2560]{1,0:T(8,128)(2,1)} %copy-done.86, bf16[2560,1600]{1,0:T(8,128)(2,1)} %all-gather.15.cloned.1.call-done), kind=kOutput, calls=%fused_computation.47 | convolution fusion | flops 8390246400 | bytes 16711680 | tf_op jit(solution)/shard_map/dot_general | solution.py:33
  422.7 15.2 %convolution_convert_fusion.3 = bf16[1024,1600]{1,0:T(8,128)(2,1)} fusion(bf16[1024,2560]{1,0:T(8,128)(2,1)} %copy-done.86, bf16[2560,1600]{1,0:T(8,128)(2,1)} %all-gather.13.cloned.1.call-done), kind=kOutput, calls=%fused_computation.48 | convolution fusion | flops 8390246400 | bytes 16711680 | tf_op jit(solution)/shard_map/dot_general | solution.py:33
  437.9 20.3 %fusion.14 = (bf16[1024,1600]{1,0:T(8,128)(2,1)}, bf16[1024,1600]{1,0:T(8,128)(2,1)}, bf16[1024,1600]{1,0:T(8,128)(2,1)}) fusion(bf16[1024,1600]{1,0:T(8,128)(2,1)} %convolution_convert_fusion.3, bf16[1024,1600]{1,0:T(8,128)(2,1)} %convolution_convert_fusion.2, bf16[1024,2560]{1,0:T(8,128)(2,1)} %copy-done.87, ...), kind=kOutput, calls=%fused_computation.27 | convolution fusion | flops 8418099200 | bytes 29818880 | tf_op jit(solution)/shard_map/dot_general | solution.py:33
  460.1 15.9 %convolution_convert_fusion = bf16[1024,1600]{1,0:T(8,128)(2,1)} fusion(bf16[1024,2560]{1,0:T(8,128)(2,1)} %constant_dynamic-update-slice_fusion.15.refs_1_, bf16[2560,1600]{1,0:T(8,128)(2,1)} %all-gather.15.cloned.1.call-done), kind=kOutput, calls=%fused_computation.45 | convolution fusion | flops 8390246400 | bytes 16711680 | tf_op jit(solution)/shard_map/dot_general | solution.py:33
  476.0 12.9 %convolution_convert_fusion.1 = bf16[1024,1600]{1,0:T(8,128)(2,1)} fusion(bf16[1024,2560]{1,0:T(8,128)(2,1)} %constant_dynamic-update-slice_fusion.15.refs_1_, bf16[2560,1600]{1,0:T(8,128)(2,1)S(1)} %bitcast.279), kind=kOutput, calls=%fused_computation.46 | convolution fusion | flops 8390246400 | bytes 16711680 | tf_op jit(solution)/shard_map/dot_general | solution.py:33
  491.7 11.6 %collective-permute-done.28 = bf16[128,2560]{1,0:T(8,128)(2,1)S(1)} collective-permute-done((bf16[128,2560]{1,0:T(8,128)(2,1)S(1)}, bf16[128,2560]{1,0:T(8,128)(2,1)S(1)}, u32[]{:S(2)}, u32[]{:S(2)}) %collective-permute-start.28) | collective-permute-done | bytes 655392 | tf_op jit(solution)/shard_map/ppermute | solution.py:255
  503.5 16.3 %fusion.20 = (bf16[1024,1600]{1,0:T(8,128)(2,1)}, bf16[1024,1600]{1,0:T(8,128)(2,1)}, bf16[1024,1600]{1,0:T(8,128)(2,1)}) fusion(bf16[1024,1600]{1,0:T(8,128)(2,1)} %convolution_convert_fusion.1, bf16[1024,1600]{1,0:T(8,128)(2,1)} %convolution_convert_fusion, bf16[1024,2560]{1,0:T(8,128)(2,1)S(1)} %constant_dynamic-update-slice_fusion.10.refs_1_, ...), kind=kOutput, calls=%fused_computation.33 | convolution fusion | flops 8418099200 | bytes 29818880 | tf_op jit(solution)/shard_map/dot_general | solution.py:33
  519.8 24.9 %weight_grad.3 = bf16[2560,1600]{1,0:T(8,128)(2,1)} custom-call(bf16[1024,2560]{1,0:T(8,128)(2,1)} %copy-done.87, bf16[1024,2560]{1,0:T(8,128)(2,1)} %copy-done.88, bf16[1024,1600]{1,0:T(8,128)(2,1)} %get-tuple-element.87.refs_2_, bf16[1024,1600]{1,0:T(8,128)(2,1)} %get-tuple-element.88.refs_3_), custom_call_target="tpu_custom_call" | custom-call | flops 16777216000 | bytes 25231360 | tf_op jit(solution)/shard_map/weight_grad/pallas_call | solution.py:237
  546.5 5.4 fusion.93
  552.0 6.4 fusion.22
  561.4 3.7 fusion.23
  568.6 3.9 fusion.24
  576.7 3.7 fusion.25
  600.0 25.4 %weight_grad.4 = bf16[2560,1600]{1,0:T(8,128)(2,1)} custom-call(bf16[1024,2560]{1,0:T(8,128)(2,1)} %copy-done.86, bf16[1024,2560]{1,0:T(8,128)(2,1)} %constant_dynamic-update-slice_fusion.15.refs_1_, bf16[1024,1600]{1,0:T(8,128)(2,1)} %get-tuple-element.89.refs_2_, bf16[1024,1600]{1,0:T(8,128)(2,1)} %get-tuple-element.85.refs_3_), custom_call_target="tpu_custom_call" | custom-call | flops 16777216000 | bytes 25231360 | tf_op jit(solution)/shard_map/weight_grad/pallas_call | solution.py:237
  625.5 5.1 fusion.73
  630.6 5.0 fusion.85
  635.5 4.8 fusion.67
  640.4 3.7 add_convert_fusion.9
  645.2 4.6 add_convert_fusion.8
  650.3 4.9 add_convert_fusion.3
  661.5 4.9 collective-permute-done.40
  671.0 3.9 collective-permute-done.56
  692.6 25.0 %weight_grad.5 = bf16[2560,1600]{1,0:T(8,128)(2,1)} custom-call(bf16[1024,2560]{1,0:T(8,128)(2,1)} %copy-done.86, bf16[1024,2560]{1,0:T(8,128)(2,1)} %constant_dynamic-update-slice_fusion.15.refs_1_, bf16[1024,1600]{1,0:T(8,128)(2,1)} %get-tuple-element.90.refs_2_, bf16[1024,1600]{1,0:T(8,128)(2,1)} %get-tuple-element.86.refs_3_), custom_call_target="tpu_custom_call" | custom-call | flops 16777216000 | bytes 25231360 | tf_op jit(solution)/shard_map/weight_grad/pallas_call | solution.py:237
  720.6 23.0 %collective-permute-done.58 = bf16[256,2560]{1,0:T(8,128)(2,1)} collective-permute-done((bf16[256,2560]{1,0:T(8,128)(2,1)}, bf16[256,2560]{1,0:T(8,128)(2,1)}, u32[]{:S(2)}, u32[]{:S(2)}) %collective-permute-start.58) | collective-permute-done | bytes 1310752 | tf_op jit(solution)/shard_map/ppermute | solution.py:255
  758.7 6.2 collective-permute-done.59
  765.6 8.0 convolution_convert_fusion.16
  773.7 30.7 %attend_back.3 = (bf16[10,96,1024]{2,1,0:T(8,128)(2,1)S(1)}, bf16[10,128,1024]{2,1,0:T(8,128)(2,1)S(1)}, f32[32,1024]{1,0:T(8,128)S(1)}) custom-call(s32[1]{0:T(128)} %bitcast.28.prefix_ref, bf16[10,96,1024]{2,1,0:T(8,128)(2,1)S(1)} %copy-done.12, bf16[10,128,1024]{2,1,0:T(8,128)(2,1)S(1)} %bitcast.191, bf16[32,1024]{1,0:T(8,128)(2,1)S(1)} %copy-done.16, ...), custom_call_target="tpu_custom_call" | custom-call | flops 20132659200 | bytes 11264000 | tf_op jit(solution)/shard_map/attend_back/pallas_call | solution.py:190
  804.4 3.3 fusion.227
  807.8 3.7 convolution_convert_fusion.17
  811.5 30.3 %attend_back.2 = (bf16[10,96,1024]{2,1,0:T(8,128)(2,1)S(1)}, bf16[10,128,1024]{2,1,0:T(8,128)(2,1)S(1)}, f32[32,1024]{1,0:T(8,128)S(1)}) custom-call(s32[1]{0:T(128)} %bitcast.prefix_ref, bf16[10,96,1024]{2,1,0:T(8,128)(2,1)S(1)} %copy-done.14, bf16[10,128,1024]{2,1,0:T(8,128)(2,1)S(1)} %bitcast.189, bf16[32,1024]{1,0:T(8,128)(2,1)S(1)} %copy-done.18, ...), custom_call_target="tpu_custom_call" | custom-call | flops 20132659200 | bytes 11264000 | tf_op jit(solution)/shard_map/attend_back/pallas_call | solution.py:190
  843.2 5.8 add_convert_fusion.1
  849.0 3.3 copy.102
  852.3 4.0 convolution_convert_fusion.15
  870.1 3.8 convolution_convert_fusion.11
  890.1 3.7 convolution_convert_fusion.10
  893.8 3.7 convolution_convert_fusion.13
  897.5 3.7 convolution_convert_fusion.12
  901.3 4.6 fusion.237
  905.9 5.9 add_convert_fusion
  923.1 24.8 %collective-permute-done.62 = bf16[256,512]{0,1:T(8,128)(2,1)S(1)} collective-permute-done((bf16[256,512]{0,1:T(8,128)(2,1)S(1)}, bf16[256,512]{0,1:T(8,128)(2,1)S(1)}, u32[]{:S(2)}, u32[]{:S(2)}) %collective-permute-start.62) | collective-permute-done | bytes 262176 | tf_op jit(solution)/shard_map/ppermute | solution.py:255
  956.5 3.6 collective-permute-done.68
  969.6 9.7 multiply_reduce_fusion
  981.4 6.2 fusion
  1003.5 3.7 add_convert_fusion.4
  1008.1 3.3 add_convert_fusion.7
  1012.9 3.5 add_convert_fusion.6
  1026.8 7.4 collective-permute-done.46
  1046.7 12.3 %collective-permute-done.70 = bf16[640,512]{1,0:T(8,128)(2,1)S(1)} collective-permute-done((bf16[640,512]{1,0:T(8,128)(2,1)S(1)}, bf16[640,512]{1,0:T(8,128)(2,1)S(1)}, u32[]{:S(2)}, u32[]{:S(2)}) %collective-permute-start.70) | collective-permute-done | bytes 655392 | tf_op jit(solution)/shard_map/ppermute | solution.py:255
  1060.3 4.9 collective-permute-done.72
  1081.3 16.7 %reduce-scatter.17.cloned.1.call-done = bf16[80,1152]{1,0:T(8,128)(2,1)} async-done(((bf16[320,1152]{1,0:T(8,128)(2,1)}), bf16[80,1152]{1,0:T(8,128)(2,1)}) %reduce-scatter.17.cloned.1.call-update) | async-done | bytes 184336 | tf_op jit(solution)/shard_map/reduce_scatter | solution.py:375
  (761 shorter events, 354.3 us)
Async XLA Ops:
  7.2 32.3 %all-gather.9.cloned.1.call-start = ((), (), s32[]{:S(2)}) async-start(), calls=%async_computation.7 | async-start | bytes 1658880 | tf_op jit(solution)/shard_map/all_gather | solution.py:336
  12.1 92.3 %all-gather.7.cloned.1.call-start = ((), (), s32[]{:S(2)}) async-start(), calls=%async_computation.6 | async-start | bytes 2949120 | tf_op jit(solution)/shard_map/all_gather | solution.py:411
  13.9 189.5 %all-gather.11.cloned.1.call-start = ((), (), s32[]{:S(2)}) async-start(), calls=%async_computation.8 | async-start | bytes 3686400 | tf_op jit(solution)/shard_map/all_gather | solution.py:411
  14.7 392.8 %all-gather.15.cloned.1.call-start = ((), (), s32[]{:S(2)}) async-start(), calls=%async_computation.10 | async-start | bytes 9584640 | tf_op jit(solution)/shard_map/all_gather | solution.py:411
  15.3 407.5 %all-gather.13.cloned.1.call-start = ((), (), s32[]{:S(2)}) async-start(), calls=%async_computation.9 | async-start | bytes 9584640 | tf_op jit(solution)/shard_map/all_gather | solution.py:411
  15.8 422.1 %all-gather.17.cloned.1.call-start = ((), (), s32[]{:S(2)}) async-start(), calls=%async_computation.11 | async-start | bytes 9584640 | tf_op jit(solution)/shard_map/all_gather | solution.py:411
  43.3 22.2 %collective-permute-start = (bf16[320,1152]{1,0:T(8,128)(2,1)}, bf16[320,1152]{1,0:T(8,128)(2,1)}, u32[]{:S(2)}, u32[]{:S(2)}) collective-permute-start(bf16[320,1152]{1,0:T(8,128)(2,1)} %get-tuple-element.138), channel_id=1, source_target_pairs={{0,1},{1,0},{2,3},{3,2},{4,5},{5,4},{6,7},{7,6},{8,9},{9,8},{10,11... | collective-permute-start | bytes 2211848 | tf_op jit(solution)/shard_map/ppermute | solution.py:255
  64.8 173.0 %collective-permute-start.33 = (bf16[256,2560]{1,0:T(8,128)(2,1)}, bf16[256,2560]{1,0:T(8,128)(2,1)}, u32[]{:S(2)}, u32[]{:S(2)}) collective-permute-start(bf16[256,2560]{1,0:T(8,128)(2,1)} %get-tuple-element.82), channel_id=1, source_target_pairs={{0,1},{1,0},{2,3},{3,2},{4,5},{5,4},{6,7},{7,6},{8,9},{9,8},{10,11... | collective-permute-start | bytes 3932168 | tf_op jit(solution)/shard_map/ppermute | solution.py:255
  65.4 579.7 %reduce-scatter.7.cloned.1.call-start = ((), (), s32[]{:S(2)}) async-start(), calls=%async_computation.12 | async-start | bytes 9584640 | tf_op jit(solution)/shard_map/reduce_scatter | solution.py:414
  103.3 25.5 %collective-permute-start.6 = (bf16[256,1056]{0,1:T(8,128)(2,1)}, bf16[256,1056]{0,1:T(8,128)(2,1)}, u32[]{:S(2)}, u32[]{:S(2)}) collective-permute-start(bf16[256,1056]{0,1:T(8,128)(2,1)} %get-tuple-element.180), channel_id=1, source_target_pairs={{0,2},{1,3},{2,0},{3,1},{4,6},{5,7},{6,4},{7,5},{8,10},{9,11},{10,... | collective-permute-start | bytes 1622024 | tf_op jit(solution)/shard_map/ppermute | solution.py:255
  109.8 23.9 %collective-permute-start.5 = (bf16[256,1056]{0,1:T(8,128)(2,1)}, bf16[256,1056]{0,1:T(8,128)(2,1)S(1)}, u32[]{:S(2)}, u32[]{:S(2)}) collective-permute-start(bf16[256,1056]{0,1:T(8,128)(2,1)} %get-tuple-element.180), channel_id=1, source_target_pairs={{0,1},{1,0},{2,3},{3,2},{4,5},{5,4},{6,7},{7,6},{8,9},{9,8},{10,11... | collective-permute-start | bytes 1622024 | tf_op jit(solution)/shard_map/ppermute | solution.py:255
  117.2 121.2 %collective-permute-start.34 = (bf16[256,2560]{1,0:T(8,128)(2,1)}, bf16[256,2560]{1,0:T(8,128)(2,1)}, u32[]{:S(2)}, u32[]{:S(2)}) collective-permute-start(bf16[256,2560]{1,0:T(8,128)(2,1)} %get-tuple-element.82), channel_id=1, source_target_pairs={{0,2},{1,3},{2,0},{3,1},{4,6},{5,7},{6,4},{7,5},{8,10},{9,11},{10,... | collective-permute-start | bytes 3932168 | tf_op jit(solution)/shard_map/ppermute | solution.py:255
  128.8 33.8 %collective-permute-start.20 = (bf16[128,1056]{0,1:T(8,128)(2,1)S(1)}, bf16[128,1056]{0,1:T(8,128)(2,1)S(1)}, u32[]{:S(2)}, u32[]{:S(2)}) collective-permute-start(bf16[128,1056]{0,1:T(8,128)(2,1)S(1)} %slice.717), channel_id=1, source_target_pairs={{0,2},{1,3},{2,0},{3,1},{4,6},{5,7},{6,4},{7,5},{8,10},{9,11},{10,... | collective-permute-start | bytes 811016 | tf_op jit(solution)/shard_map/ppermute | solution.py:255
  133.6 30.8 %collective-permute-start.7 = (bf16[128,1056]{0,1:T(8,128)(2,1)S(1)}, bf16[128,1056]{0,1:T(8,128)(2,1)S(1)}, u32[]{:S(2)}, u32[]{:S(2)}) collective-permute-start(bf16[128,1056]{0,1:T(8,128)(2,1)S(1)} %slice.699), channel_id=1, source_target_pairs={{0,1},{1,0},{2,3},{3,2},{4,5},{5,4},{6,7},{7,6},{8,9},{9,8},{10,11... | collective-permute-start | bytes 811016 | tf_op jit(solution)/shard_map/ppermute | solution.py:255
  137.2 30.5 %collective-permute-start.8 = (bf16[128,1056]{0,1:T(8,128)(2,1)S(1)}, bf16[128,1056]{0,1:T(8,128)(2,1)S(1)}, u32[]{:S(2)}, u32[]{:S(2)}) collective-permute-start(bf16[128,1056]{0,1:T(8,128)(2,1)S(1)} %slice.700), channel_id=1, source_target_pairs={{0,2},{1,3},{2,0},{3,1},{4,6},{5,7},{6,4},{7,5},{8,10},{9,11},{10,... | collective-permute-start | bytes 811016 | tf_op jit(solution)/shard_map/ppermute | solution.py:255
  206.4 38.1 %collective-permute-start.21 = (bf16[512,1280]{1,0:T(8,128)(2,1)S(1)}, bf16[512,1280]{1,0:T(8,128)(2,1)S(1)}, u32[]{:S(2)}, u32[]{:S(2)}) collective-permute-start(bf16[512,1280]{1,0:T(8,128)(2,1)S(1)} %convolution_convert_fusion.7), channel_id=1, source_target_pairs={{0,1},{1,0},{2,3},{3,2},{4,5},{5,4},{6,7},{7,6},{8,9},{9,8},{10,11... | collective-permute-start | bytes 3932168 | tf_op jit(solution)/shard_map/ppermute | solution.py:255
  208.5 38.1 %collective-permute-start.23 = (bf16[512,1280]{1,0:T(8,128)(2,1)S(1)}, bf16[512,1280]{1,0:T(8,128)(2,1)S(1)}, u32[]{:S(2)}, u32[]{:S(2)}) collective-permute-start(bf16[512,1280]{1,0:T(8,128)(2,1)S(1)} %convolution_convert_fusion.6), channel_id=1, source_target_pairs={{0,2},{1,3},{2,0},{3,1},{4,6},{5,7},{6,4},{7,5},{8,10},{9,11},{10,... | collective-permute-start | bytes 3932168 | tf_op jit(solution)/shard_map/ppermute | solution.py:255
  235.1 31.8 %collective-permute-start.9 = (bf16[512,1280]{1,0:T(8,128)(2,1)S(1)}, bf16[512,1280]{1,0:T(8,128)(2,1)S(1)}, u32[]{:S(2)}, u32[]{:S(2)}) collective-permute-start(bf16[512,1280]{1,0:T(8,128)(2,1)S(1)} %convolution_convert_fusion.9), channel_id=1, source_target_pairs={{0,1},{1,0},{2,3},{3,2},{4,5},{5,4},{6,7},{7,6},{8,9},{9,8},{10,11... | collective-permute-start | bytes 3932168 | tf_op jit(solution)/shard_map/ppermute | solution.py:255
  237.9 31.8 %collective-permute-start.11 = (bf16[512,1280]{1,0:T(8,128)(2,1)S(1)}, bf16[512,1280]{1,0:T(8,128)(2,1)S(1)}, u32[]{:S(2)}, u32[]{:S(2)}) collective-permute-start(bf16[512,1280]{1,0:T(8,128)(2,1)S(1)} %convolution_convert_fusion.8), channel_id=1, source_target_pairs={{0,2},{1,3},{2,0},{3,1},{4,6},{5,7},{6,4},{7,5},{8,10},{9,11},{10,... | collective-permute-start | bytes 3932168 | tf_op jit(solution)/shard_map/ppermute | solution.py:255
  239.6 78.5 %collective-permute-start.35 = (bf16[128,2560]{1,0:T(8,128)(2,1)S(1)}, bf16[128,2560]{1,0:T(8,128)(2,1)S(1)}, u32[]{:S(2)}, u32[]{:S(2)}) collective-permute-start(bf16[128,2560]{1,0:T(8,128)(2,1)S(1)} %slice.590), channel_id=1, source_target_pairs={{0,1},{1,0},{2,3},{3,2},{4,5},{5,4},{6,7},{7,6},{8,9},{9,8},{10,11... | collective-permute-start | bytes 1966088 | tf_op jit(solution)/shard_map/ppermute | solution.py:255
  244.5 76.6 %collective-permute-start.36 = (bf16[128,2560]{1,0:T(8,128)(2,1)S(1)}, bf16[128,2560]{1,0:T(8,128)(2,1)S(1)}, u32[]{:S(2)}, u32[]{:S(2)}) collective-permute-start(bf16[128,2560]{1,0:T(8,128)(2,1)S(1)} %slice.591), channel_id=1, source_target_pairs={{0,2},{1,3},{2,0},{3,1},{4,6},{5,7},{6,4},{7,5},{8,10},{9,11},{10,... | collective-permute-start | bytes 1966088 | tf_op jit(solution)/shard_map/ppermute | solution.py:255
  246.6 51.1 %collective-permute-start.22 = (bf16[256,1280]{1,0:T(8,128)(2,1)S(1)}, bf16[256,1280]{1,0:T(8,128)(2,1)S(1)}, u32[]{:S(2)}, u32[]{:S(2)}) collective-permute-start(bf16[256,1280]{1,0:T(8,128)(2,1)S(1)} %add_convert_fusion.11), channel_id=1, source_target_pairs={{0,2},{1,3},{2,0},{3,1},{4,6},{5,7},{6,4},{7,5},{8,10},{9,11},{10,... | collective-permute-start | bytes 1966088 | tf_op jit(solution)/shard_map/ppermute | solution.py:255
  266.8 31.6 %collective-permute-start.24 = (bf16[256,1280]{1,0:T(8,128)(2,1)S(1)}, bf16[256,1280]{1,0:T(8,128)(2,1)S(1)}, u32[]{:S(2)}, u32[]{:S(2)}) collective-permute-start(bf16[256,1280]{1,0:T(8,128)(2,1)S(1)} %add_convert_fusion.10), channel_id=1, source_target_pairs={{0,1},{1,0},{2,3},{3,2},{4,5},{5,4},{6,7},{7,6},{8,9},{9,8},{10,11... | collective-permute-start | bytes 1966088 | tf_op jit(solution)/shard_map/ppermute | solution.py:255
  269.6 39.8 %collective-permute-start.10 = (bf16[256,1280]{1,0:T(8,128)(2,1)S(1)}, bf16[256,1280]{1,0:T(8,128)(2,1)S(1)}, u32[]{:S(2)}, u32[]{:S(2)}) collective-permute-start(bf16[256,1280]{1,0:T(8,128)(2,1)S(1)} %add_convert_fusion.13), channel_id=1, source_target_pairs={{0,2},{1,3},{2,0},{3,1},{4,6},{5,7},{6,4},{7,5},{8,10},{9,11},{10,... | collective-permute-start | bytes 1966088 | tf_op jit(solution)/shard_map/ppermute | solution.py:255
  315.5 33.9 %collective-permute-start.29 = (bf16[256,2560]{1,0:T(8,128)(2,1)S(1)}, bf16[256,2560]{1,0:T(8,128)(2,1)S(1)}, u32[]{:S(2)}, u32[]{:S(2)}) collective-permute-start(bf16[256,2560]{1,0:T(8,128)(2,1)S(1)} %get-tuple-element.163), channel_id=1, source_target_pairs={{0,1},{1,0},{2,3},{3,2},{4,5},{5,4},{6,7},{7,6},{8,9},{9,8},{10,11... | collective-permute-start | bytes 3932168 | tf_op jit(solution)/shard_map/ppermute | solution.py:255
  316.1 31.7 %collective-permute-start.30 = (bf16[256,2560]{1,0:T(8,128)(2,1)S(1)}, bf16[256,2560]{1,0:T(8,128)(2,1)S(1)}, u32[]{:S(2)}, u32[]{:S(2)}) collective-permute-start(bf16[256,2560]{1,0:T(8,128)(2,1)S(1)} %get-tuple-element.163), channel_id=1, source_target_pairs={{0,2},{1,3},{2,0},{3,1},{4,6},{5,7},{6,4},{7,5},{8,10},{9,11},{10,... | collective-permute-start | bytes 3932168 | tf_op jit(solution)/shard_map/ppermute | solution.py:255
  317.6 59.9 %collective-permute-start.13 = (bf16[256,2560]{1,0:T(8,128)(2,1)S(1)}, bf16[256,2560]{1,0:T(8,128)(2,1)S(1)}, u32[]{:S(2)}, u32[]{:S(2)}) collective-permute-start(bf16[256,2560]{1,0:T(8,128)(2,1)S(1)} %get-tuple-element.134), channel_id=1, source_target_pairs={{0,1},{1,0},{2,3},{3,2},{4,5},{5,4},{6,7},{7,6},{8,9},{9,8},{10,11... | collective-permute-start | bytes 3932168 | tf_op jit(solution)/shard_map/ppermute | solution.py:255
  318.2 57.7 %collective-permute-start.14 = (bf16[256,2560]{1,0:T(8,128)(2,1)S(1)}, bf16[256,2560]{1,0:T(8,128)(2,1)S(1)}, u32[]{:S(2)}, u32[]{:S(2)}) collective-permute-start(bf16[256,2560]{1,0:T(8,128)(2,1)S(1)} %get-tuple-element.134), channel_id=1, source_target_pairs={{0,2},{1,3},{2,0},{3,1},{4,6},{5,7},{6,4},{7,5},{8,10},{9,11},{10,... | collective-permute-start | bytes 3932168 | tf_op jit(solution)/shard_map/ppermute | solution.py:255
  347.9 55.5 %collective-permute-start.31 = (bf16[128,2560]{1,0:T(8,128)(2,1)S(1)}, bf16[128,2560]{1,0:T(8,128)(2,1)S(1)}, u32[]{:S(2)}, u32[]{:S(2)}) collective-permute-start(bf16[128,2560]{1,0:T(8,128)(2,1)S(1)} %slice.726), channel_id=1, source_target_pairs={{0,1},{1,0},{2,3},{3,2},{4,5},{5,4},{6,7},{7,6},{8,9},{9,8},{10,11... | collective-permute-start | bytes 1966088 | tf_op jit(solution)/shard_map/ppermute | solution.py:255
  349.4 54.8 %collective-permute-start.32 = (bf16[128,2560]{1,0:T(8,128)(2,1)S(1)}, bf16[128,2560]{1,0:T(8,128)(2,1)S(1)}, u32[]{:S(2)}, u32[]{:S(2)}) collective-permute-start(bf16[128,2560]{1,0:T(8,128)(2,1)S(1)} %slice.727), channel_id=1, source_target_pairs={{0,2},{1,3},{2,0},{3,1},{4,6},{5,7},{6,4},{7,5},{8,10},{9,11},{10,... | collective-permute-start | bytes 1966088 | tf_op jit(solution)/shard_map/ppermute | solution.py:255
  375.9 24.3 %collective-permute-start.15 = (bf16[128,2560]{1,0:T(8,128)(2,1)S(1)}, bf16[128,2560]{1,0:T(8,128)(2,1)S(1)}, u32[]{:S(2)}, u32[]{:S(2)}) collective-permute-start(bf16[128,2560]{1,0:T(8,128)(2,1)S(1)} %slice.713), channel_id=1, source_target_pairs={{0,1},{1,0},{2,3},{3,2},{4,5},{5,4},{6,7},{7,6},{8,9},{9,8},{10,11... | collective-permute-start | bytes 1966088 | tf_op jit(solution)/shard_map/ppermute | solution.py:255
  377.5 23.6 %collective-permute-start.16 = (bf16[128,2560]{1,0:T(8,128)(2,1)S(1)}, bf16[128,2560]{1,0:T(8,128)(2,1)S(1)}, u32[]{:S(2)}, u32[]{:S(2)}) collective-permute-start(bf16[128,2560]{1,0:T(8,128)(2,1)S(1)} %slice.714), channel_id=1, source_target_pairs={{0,2},{1,3},{2,0},{3,1},{4,6},{5,7},{6,4},{7,5},{8,10},{9,11},{10,... | collective-permute-start | bytes 1966088 | tf_op jit(solution)/shard_map/ppermute | solution.py:255
  401.2 57.0 %collective-permute-start.25 = (bf16[256,2560]{1,0:T(8,128)(2,1)S(1)}, bf16[256,2560]{1,0:T(8,128)(2,1)}, u32[]{:S(2)}, u32[]{:S(2)}) collective-permute-start(bf16[256,2560]{1,0:T(8,128)(2,1)S(1)} %copy-done.58), channel_id=1, source_target_pairs={{0,1},{1,0},{2,3},{3,2},{4,5},{5,4},{6,7},{7,6},{8,9},{9,8},{10,11... | collective-permute-start | bytes 3932168 | tf_op jit(solution)/shard_map/ppermute | solution.py:255
  402.2 56.0 %collective-permute-start.26 = (bf16[256,2560]{1,0:T(8,128)(2,1)S(1)}, bf16[256,2560]{1,0:T(8,128)(2,1)S(1)}, u32[]{:S(2)}, u32[]{:S(2)}) collective-permute-start(bf16[256,2560]{1,0:T(8,128)(2,1)S(1)} %copy-done.58), channel_id=1, source_target_pairs={{0,2},{1,3},{2,0},{3,1},{4,6},{5,7},{6,4},{7,5},{8,10},{9,11},{10,... | collective-permute-start | bytes 3932168 | tf_op jit(solution)/shard_map/ppermute | solution.py:255
  458.4 33.3 %collective-permute-start.27 = (bf16[128,2560]{1,0:T(8,128)(2,1)S(1)}, bf16[128,2560]{1,0:T(8,128)(2,1)S(1)}, u32[]{:S(2)}, u32[]{:S(2)}) collective-permute-start(bf16[128,2560]{1,0:T(8,128)(2,1)S(1)} %slice.585), channel_id=1, source_target_pairs={{0,1},{1,0},{2,3},{3,2},{4,5},{5,4},{6,7},{7,6},{8,9},{9,8},{10,11... | collective-permute-start | bytes 1966088 | tf_op jit(solution)/shard_map/ppermute | solution.py:255
  544.7 298.3 %reduce-scatter.9.cloned.1.call-start = ((), (), s32[]{:S(2)}) async-start(), calls=%async_computation.13 | async-start | bytes 9584640 | tf_op jit(solution)/shard_map/reduce_scatter | solution.py:414
  558.4 81.9 %collective-permute-start.37 = (bf16[512,1280]{1,0:T(8,128)(2,1)}, bf16[512,1280]{1,0:T(8,128)(2,1)}, u32[]{:S(2)}, u32[]{:S(2)}) collective-permute-start(bf16[512,1280]{1,0:T(8,128)(2,1)} %fusion.22), channel_id=1, source_target_pairs={{0,1},{1,0},{2,3},{3,2},{4,5},{5,4},{6,7},{7,6},{8,9},{9,8},{10,11... | collective-permute-start | bytes 3932168 | tf_op jit(solution)/shard_map/ppermute | solution.py:255
  565.1 80.1 %collective-permute-start.39 = (bf16[512,1280]{1,0:T(8,128)(2,1)}, bf16[512,1280]{1,0:T(8,128)(2,1)}, u32[]{:S(2)}, u32[]{:S(2)}) collective-permute-start(bf16[512,1280]{1,0:T(8,128)(2,1)} %fusion.23), channel_id=1, source_target_pairs={{0,2},{1,3},{2,0},{3,1},{4,6},{5,7},{6,4},{7,5},{8,10},{9,11},{10,... | collective-permute-start | bytes 3932168 | tf_op jit(solution)/shard_map/ppermute | solution.py:255
  572.6 77.7 %collective-permute-start.53 = (bf16[512,1280]{1,0:T(8,128)(2,1)}, bf16[512,1280]{1,0:T(8,128)(2,1)}, u32[]{:S(2)}, u32[]{:S(2)}) collective-permute-start(bf16[512,1280]{1,0:T(8,128)(2,1)} %fusion.24), channel_id=1, source_target_pairs={{0,1},{1,0},{2,3},{3,2},{4,5},{5,4},{6,7},{7,6},{8,9},{9,8},{10,11... | collective-permute-start | bytes 3932168 | tf_op jit(solution)/shard_map/ppermute | solution.py:255
  580.4 76.3 %collective-permute-start.55 = (bf16[512,1280]{1,0:T(8,128)(2,1)}, bf16[512,1280]{1,0:T(8,128)(2,1)}, u32[]{:S(2)}, u32[]{:S(2)}) collective-permute-start(bf16[512,1280]{1,0:T(8,128)(2,1)} %fusion.25), channel_id=1, source_target_pairs={{0,2},{1,3},{2,0},{3,1},{4,6},{5,7},{6,4},{7,5},{8,10},{9,11},{10,... | collective-permute-start | bytes 3932168 | tf_op jit(solution)/shard_map/ppermute | solution.py:255
  645.1 335.8 %reduce-scatter.11.cloned.1.call-start = ((), (), s32[]{:S(2)}) async-start(), calls=%async_computation.14 | async-start | bytes 9584640 | tf_op jit(solution)/shard_map/reduce_scatter | solution.py:414
  683.1 36.3 %collective-permute-start.41 = (bf16[256,2560]{1,0:T(8,128)(2,1)}, bf16[256,2560]{1,0:T(8,128)(2,1)S(1)}, u32[]{:S(2)}, u32[]{:S(2)}) collective-permute-start(bf16[256,2560]{1,0:T(8,128)(2,1)} %get-tuple-element.131), channel_id=1, source_target_pairs={{0,1},{1,0},{2,3},{3,2},{4,5},{5,4},{6,7},{7,6},{8,9},{9,8},{10,11... | collective-permute-start | bytes 3932168 | tf_op jit(solution)/shard_map/ppermute | solution.py:255
  683.5 34.6 %collective-permute-start.42 = (bf16[256,2560]{1,0:T(8,128)(2,1)}, bf16[256,2560]{1,0:T(8,128)(2,1)S(1)}, u32[]{:S(2)}, u32[]{:S(2)}) collective-permute-start(bf16[256,2560]{1,0:T(8,128)(2,1)} %get-tuple-element.131), channel_id=1, source_target_pairs={{0,2},{1,3},{2,0},{3,1},{4,6},{5,7},{6,4},{7,5},{8,10},{9,11},{10,... | collective-permute-start | bytes 3932168 | tf_op jit(solution)/shard_map/ppermute | solution.py:255
  690.8 55.7 %collective-permute-start.57 = (bf16[256,2560]{1,0:T(8,128)(2,1)}, bf16[256,2560]{1,0:T(8,128)(2,1)}, u32[]{:S(2)}, u32[]{:S(2)}) collective-permute-start(bf16[256,2560]{1,0:T(8,128)(2,1)} %get-tuple-element.128), channel_id=1, source_target_pairs={{0,1},{1,0},{2,3},{3,2},{4,5},{5,4},{6,7},{7,6},{8,9},{9,8},{10,11... | collective-permute-start | bytes 3932168 | tf_op jit(solution)/shard_map/ppermute | solution.py:255
  691.5 52.1 %collective-permute-start.58 = (bf16[256,2560]{1,0:T(8,128)(2,1)}, bf16[256,2560]{1,0:T(8,128)(2,1)}, u32[]{:S(2)}, u32[]{:S(2)}) collective-permute-start(bf16[256,2560]{1,0:T(8,128)(2,1)} %get-tuple-element.128), channel_id=1, source_target_pairs={{0,2},{1,3},{2,0},{3,1},{4,6},{5,7},{6,4},{7,5},{8,10},{9,11},{10,... | collective-permute-start | bytes 3932168 | tf_op jit(solution)/shard_map/ppermute | solution.py:255
  718.2 39.0 %collective-permute-start.43 = (bf16[128,2560]{1,0:T(8,128)(2,1)S(1)}, bf16[128,2560]{1,0:T(8,128)(2,1)S(1)}, u32[]{:S(2)}, u32[]{:S(2)}) collective-permute-start(bf16[128,2560]{1,0:T(8,128)(2,1)S(1)} %slice.736), channel_id=1, source_target_pairs={{0,1},{1,0},{2,3},{3,2},{4,5},{5,4},{6,7},{7,6},{8,9},{9,8},{10,11... | collective-permute-start | bytes 1966088 | tf_op jit(solution)/shard_map/ppermute | solution.py:255
  719.5 38.1 %collective-permute-start.44 = (bf16[128,2560]{1,0:T(8,128)(2,1)S(1)}, bf16[128,2560]{1,0:T(8,128)(2,1)S(1)}, u32[]{:S(2)}, u32[]{:S(2)}) collective-permute-start(bf16[128,2560]{1,0:T(8,128)(2,1)S(1)} %slice.737), channel_id=1, source_target_pairs={{0,2},{1,3},{2,0},{3,1},{4,6},{5,7},{6,4},{7,5},{8,10},{9,11},{10,... | collective-permute-start | bytes 1966088 | tf_op jit(solution)/shard_map/ppermute | solution.py:255
  843.1 180.4 %reduce-scatter.13.cloned.1.call-start = ((), (), s32[]{:S(2)}) async-start(), calls=%async_computation.15 | async-start | bytes 3686400 | tf_op jit(solution)/shard_map/reduce_scatter | solution.py:414
  859.3 56.8 %collective-permute-start.61 = (bf16[512,512]{0,1:T(8,128)(2,1)}, bf16[512,512]{0,1:T(8,128)(2,1)}, u32[]{:S(2)}, u32[]{:S(2)}) collective-permute-start(bf16[512,512]{0,1:T(8,128)(2,1)} %pad_maximum_fusion.18), channel_id=1, source_target_pairs={{0,1},{1,0},{2,3},{3,2},{4,5},{5,4},{6,7},{7,6},{8,9},{9,8},{10,11... | collective-permute-start | bytes 1572872 | tf_op jit(solution)/shard_map/ppermute | solution.py:255
  865.6 54.2 %collective-permute-start.63 = (bf16[512,544]{0,1:T(8,128)(2,1)}, bf16[512,544]{0,1:T(8,128)(2,1)S(1)}, u32[]{:S(2)}, u32[]{:S(2)}) collective-permute-start(bf16[512,544]{0,1:T(8,128)(2,1)} %pad_maximum_fusion.16), channel_id=1, source_target_pairs={{0,2},{1,3},{2,0},{3,1},{4,6},{5,7},{6,4},{7,5},{8,10},{9,11},{10,... | collective-permute-start | bytes 1671176 | tf_op jit(solution)/shard_map/ppermute | solution.py:255
  867.0 50.7 %collective-permute-start.65 = (bf16[512,512]{0,1:T(8,128)(2,1)}, bf16[512,512]{0,1:T(8,128)(2,1)}, u32[]{:S(2)}, u32[]{:S(2)}) collective-permute-start(bf16[512,512]{0,1:T(8,128)(2,1)} %pad_maximum_fusion.19), channel_id=1, source_target_pairs={{0,1},{1,0},{2,3},{3,2},{4,5},{5,4},{6,7},{7,6},{8,9},{9,8},{10,11... | collective-permute-start | bytes 1572872 | tf_op jit(solution)/shard_map/ppermute | solution.py:255
  868.8 52.4 %collective-permute-start.67 = (bf16[512,544]{0,1:T(8,128)(2,1)}, bf16[512,544]{0,1:T(8,128)(2,1)}, u32[]{:S(2)}, u32[]{:S(2)}) collective-permute-start(bf16[512,544]{0,1:T(8,128)(2,1)} %pad_maximum_fusion.17), channel_id=1, source_target_pairs={{0,2},{1,3},{2,0},{3,1},{4,6},{5,7},{6,4},{7,5},{8,10},{9,11},{10,... | collective-permute-start | bytes 1671176 | tf_op jit(solution)/shard_map/ppermute | solution.py:255
  873.9 123.6 %collective-permute-start.49 = (bf16[512,1280]{1,0:T(8,128)(2,1)}, bf16[512,1280]{1,0:T(8,128)(2,1)}, u32[]{:S(2)}, u32[]{:S(2)}) collective-permute-start(bf16[512,1280]{1,0:T(8,128)(2,1)} %convolution_convert_fusion.11), channel_id=1, source_target_pairs={{0,1},{1,0},{2,3},{3,2},{4,5},{5,4},{6,7},{7,6},{8,9},{9,8},{10,11... | collective-permute-start | bytes 3932168 | tf_op jit(solution)/shard_map/ppermute | solution.py:255
  916.1 87.4 %collective-permute-start.51 = (bf16[512,1280]{1,0:T(8,128)(2,1)}, bf16[512,1280]{1,0:T(8,128)(2,1)}, u32[]{:S(2)}, u32[]{:S(2)}) collective-permute-start(bf16[512,1280]{1,0:T(8,128)(2,1)} %convolution_convert_fusion.10), channel_id=1, source_target_pairs={{0,2},{1,3},{2,0},{3,1},{4,6},{5,7},{6,4},{7,5},{8,10},{9,11},{10,... | collective-permute-start | bytes 3932168 | tf_op jit(solution)/shard_map/ppermute | solution.py:255
  917.7 90.4 %collective-permute-start.45 = (bf16[512,1280]{1,0:T(8,128)(2,1)}, bf16[512,1280]{1,0:T(8,128)(2,1)}, u32[]{:S(2)}, u32[]{:S(2)}) collective-permute-start(bf16[512,1280]{1,0:T(8,128)(2,1)} %convolution_convert_fusion.13), channel_id=1, source_target_pairs={{0,1},{1,0},{2,3},{3,2},{4,5},{5,4},{6,7},{7,6},{8,9},{9,8},{10,11... | collective-permute-start | bytes 3932168 | tf_op jit(solution)/shard_map/ppermute | solution.py:255
  919.8 28.1 %collective-permute-start.62 = (bf16[256,512]{0,1:T(8,128)(2,1)S(1)}, bf16[256,512]{0,1:T(8,128)(2,1)S(1)}, u32[]{:S(2)}, u32[]{:S(2)}) collective-permute-start(bf16[256,512]{0,1:T(8,128)(2,1)S(1)} %add_convert_fusion.23), channel_id=1, source_target_pairs={{0,2},{1,3},{2,0},{3,1},{4,6},{5,7},{6,4},{7,5},{8,10},{9,11},{10,... | collective-permute-start | bytes 786440 | tf_op jit(solution)/shard_map/ppermute | solution.py:255
  921.3 32.3 %collective-permute-start.66 = (bf16[256,512]{0,1:T(8,128)(2,1)S(1)}, bf16[256,512]{0,1:T(8,128)(2,1)S(1)}, u32[]{:S(2)}, u32[]{:S(2)}) collective-permute-start(bf16[256,512]{0,1:T(8,128)(2,1)S(1)} %add_convert_fusion.22), channel_id=1, source_target_pairs={{0,2},{1,3},{2,0},{3,1},{4,6},{5,7},{6,4},{7,5},{8,10},{9,11},{10,... | collective-permute-start | bytes 786440 | tf_op jit(solution)/shard_map/ppermute | solution.py:255
  956.0 56.9 %collective-permute-start.47 = (bf16[512,1280]{1,0:T(8,128)(2,1)}, bf16[512,1280]{1,0:T(8,128)(2,1)}, u32[]{:S(2)}, u32[]{:S(2)}) collective-permute-start(bf16[512,1280]{1,0:T(8,128)(2,1)} %convolution_convert_fusion.12), channel_id=1, source_target_pairs={{0,2},{1,3},{2,0},{3,1},{4,6},{5,7},{6,4},{7,5},{8,10},{9,11},{10,... | collective-permute-start | bytes 3932168 | tf_op jit(solution)/shard_map/ppermute | solution.py:255
  981.0 93.5 %reduce-scatter.15.cloned.1.call-start = ((), (), s32[]{:S(2)}) async-start(), calls=%async_computation.16 | async-start | bytes 2949120 | tf_op jit(solution)/shard_map/reduce_scatter | solution.py:414
  991.0 48.9 %collective-permute-start.69 = (bf16[4,4,80,1152]{3,2,1,0:T(8,128)(2,1)}, bf16[4,4,80,1152]{3,2,1,0:T(8,128)(2,1)}, u32[]{:S(2)}, u32[]{:S(2)}) collective-permute-start(bf16[4,4,80,1152]{3,2,1,0:T(8,128)(2,1)} %dynamic-slice_bitcast_fusion), channel_id=1, source_target_pairs={{0,4},{4,0},{1,5},{5,1},{2,6},{6,2},{3,7},{7,3},{8,12},{12,8},{9,1... | collective-permute-start | bytes 8847368 | tf_op jit(solution)/shard_map/ppermute | solution.py:329
  1011.4 22.8 %collective-permute-start.46 = (bf16[256,1280]{1,0:T(8,128)(2,1)}, bf16[256,1280]{1,0:T(8,128)(2,1)}, u32[]{:S(2)}, u32[]{:S(2)}) collective-permute-start(bf16[256,1280]{1,0:T(8,128)(2,1)} %add_convert_fusion.7), channel_id=1, source_target_pairs={{0,2},{1,3},{2,0},{3,1},{4,6},{5,7},{6,4},{7,5},{8,10},{9,11},{10,... | collective-permute-start | bytes 1966088 | tf_op jit(solution)/shard_map/ppermute | solution.py:255
  1016.4 21.9 %collective-permute-start.48 = (bf16[256,1280]{1,0:T(8,128)(2,1)}, bf16[256,1280]{1,0:T(8,128)(2,1)}, u32[]{:S(2)}, u32[]{:S(2)}) collective-permute-start(bf16[256,1280]{1,0:T(8,128)(2,1)} %add_convert_fusion.6), channel_id=1, source_target_pairs={{0,1},{1,0},{2,3},{3,2},{4,5},{5,4},{6,7},{7,6},{8,9},{9,8},{10,11... | collective-permute-start | bytes 1966088 | tf_op jit(solution)/shard_map/ppermute | solution.py:255
  1023.5 74.6 %reduce-scatter.17.cloned.1.call-start = ((), (), s32[]{:S(2)}) async-start(), calls=%async_computation.17 | async-start | bytes 921600 | tf_op jit(solution)/shard_map/reduce_scatter | solution.py:375
  1044.0 21.2 %collective-permute-start.72 = (bf16[640,640]{1,0:T(8,128)(2,1)S(1)}, bf16[640,640]{1,0:T(8,128)(2,1)S(1)}, u32[]{:S(2)}, u32[]{:S(2)}) collective-permute-start(bf16[640,640]{1,0:T(8,128)(2,1)S(1)} %pad_maximum_fusion.12), channel_id=1, source_target_pairs={{0,2},{1,3},{2,0},{3,1},{4,6},{5,7},{6,4},{7,5},{8,10},{9,11},{10,... | collective-permute-start | bytes 2457608 | tf_op jit(solution)/shard_map/ppermute | solution.py:255
  (192 other events, 1799.7 us)
Sparse Core Ops, SparseCore 0:
  12.2 27.2 all-gather.8
  41.7 33.3 all-gather.6
  76.8 38.3 all-gather.10
  116.7 81.9 all-gather.14
  200.2 81.6 all-gather.12
  283.4 81.6 all-gather.16
  544.9 89.5 reduce-scatter.6
  645.2 89.9 reduce-scatter.8
  843.2 91.1 reduce-scatter.10
  981.1 42.3 reduce-scatter.12
  1025.8 36.0 reduce-scatter.14
  1074.6 23.4 reduce-scatter.16

commit v2 on v1

--- a/solution.py
+++ b/solution.py
@@ -1,3 +1,4 @@
+import functools
 import math
 
 import jax
@@ -139,12 +140,9 @@
     log_ref,
     cos_ref,
     sin_ref,
-    dquery_ref,
-    dkeyval_ref,
-    drope_ref,
-    dkey_acc,
-    dvalue_acc,
+    *refs,
 ):
+    dquery_ref, dkeyval_ref, drope_ref, dkey_acc, dvalue_acc = refs[-5:]
     seq_length = query_ref.shape[-1]
     prefix_len = prefix_ref[0]
     keyval = keyval_ref[0]
@@ -183,7 +181,7 @@
         drope_ref[...] += rope_part
 
 
-def attend_back(prefix_len, queries_t, keyval_t, rope_t, grad_t, logs, cos_t, sin_t):
+def attend_back(prefix_len, queries_t, keyval_t, rope_t, grad_t, logs, cos_t, sin_t, *others):
     heads, _, seq_length = queries_t.shape
     head_block = lambda rows: pl.BlockSpec((1, rows, seq_length), lambda h: (h, 0, 0))
     whole = lambda rows: pl.BlockSpec((rows, seq_length), lambda h: (0, 0))
@@ -199,6 +197,7 @@
             head_block(1),
             whole(ROPE // 2),
             whole(ROPE // 2),
+            *[pl.BlockSpec(memory_space=pl.ANY) for other in others],
         ],
         out_specs=[head_block(HEAD), head_block(NOPE + VD), whole(ROPE)],
         out_shape=[
@@ -217,7 +216,7 @@
             transcendentals=heads * seq_length * seq_length,
         ),
         name="attend_back",
-    )(prefix_len, queries_t, keyval_t, rope_t, grad_t, logs, cos_t, sin_t)
+    )(prefix_len, queries_t, keyval_t, rope_t, grad_t, logs, cos_t, sin_t, *others)
 
 
 def weight_grad_kernel(*refs):
@@ -319,6 +318,24 @@
 
 def after(values, *others):
     return lax.optimization_barrier((values, *others))[0]
+
+
+def nothing_kernel(*refs):
+    pass
+
+
+def tie(values, *others):
+    if not others:
+        return values
+    anywhere = pl.BlockSpec(memory_space=pl.ANY)
+    return pl.pallas_call(
+        nothing_kernel,
+        in_specs=[anywhere] * (1 + len(others)),
+        out_specs=anywhere,
+        out_shape=jax.ShapeDtypeStruct(values.shape, values.dtype),
+        input_output_aliases={0: 0},
+        name="tie",
+    )(values, *others)
 
 
 def widen(values, columns):
@@ -496,7 +513,7 @@
 
     def gather_branch(micro, start_after, hold):
         branch = (RESIDUAL * cotangent[micro].astype(F32)).astype(BF16)
-        return gather_ring(after(branch, start_after), (hold,))
+        return gather_ring(tie(branch, start_after), (hold,))
 
     for micro in micros:
         st = state[micro]
@@ -587,6 +604,7 @@
             st["logs"],
             cos_t,
             sin_t,
+            *([] if micro else [gate_grad]),
         )
         st["dquery_t"] = dquery_t.reshape(heads * HEAD, seq_length)
         st["dkeyval_t"] = dkeyval_t.reshape(heads * (NOPE + VD), seq_length)

time: 1120 us -> 1100 us (0.982)
  waiting for transfers between devices: 358 us -> 301 us
  matrix products: 298 us -> 320 us
  other arithmetic: 72.6 us -> 86.1 us
    ppermute x72, waiting for transfers between devices: 315 us -> 261 us  [swap(): lax.ppermute(values, 'tensor', [(index, index ^ bit) for index in range(4)])]
    dot_general x73, matrix products: 298 us -> 320 us  [dot(): lax.dot_general(left_side, right_side, (((left_dim,), (right_dim,)), ((),...]
    unnamed x360 -> x336, local copies, waits for them, and re-layouts: 43.2 us -> 33.2 us
  transfers between devices with their start and end apart: 86 -> 86, of which waited for: 39 -> 41; matrix products, arithmetic and copies ran while one was open for 38% -> 42% of each run, Pallas kernels for 14% -> 15%
where the time goes in v2:
time: 1100 us; the launch traced here: 1090 us
  matrix products  320 us (29%)
  waiting for transfers between devices  301 us (27%)
  Pallas kernels  184 us (17%)
  local copies, waits for them, and re-layouts  99.4 us (9%)
  other arithmetic  86.1 us (8%)
  starting transfers between devices  82.8 us (8%)
  between operations  17.3 us (2%)
    dot_general x73, matrix products, dot(): lax.dot_general(left_side, right_side, (((left_dim,), (right_dim,)), ((),...  320 us
    ppermute x72, waiting for transfers between devices, swap(): lax.ppermute(values, 'tensor', [(index, index ^ bit) for index in range(4)])  261 us
    ppermute x72, starting transfers between devices, swap(): lax.ppermute(values, 'tensor', [(index, index ^ bit) for index in range(4)])  81.5 us
    pallas_call x3, Pallas kernels, weight_grad(): pl.pallas_call(weight_grad_kernel, grid=(rows // tile,), in_specs=[pl.Blo...  75.5 us
    pallas_call x2, Pallas kernels, attend_back(): pl.pallas_call(attend_back_kernel, grid=(heads,), in_specs=[pl.BlockSpec(...  60.7 us
    pallas_call x2, Pallas kernels, attend(): pl.pallas_call(attend_kernel, grid=(heads,), in_specs=[pl.BlockSpec(memor...  47.2 us
    unnamed x336, local copies, waits for them, and re-layouts  33.2 us
    all_gather x1, waiting for transfers between devices, gather_everywhere(): own = lax.all_gather(values, DP, axis=0, tiled=True)  23.6 us
  transfers between devices with their start and end apart: 86, of which 41 were waited for; matrix products, arithmetic and copies ran while one was open for 42% of the time, Pallas kernels for 15%

profile of v2, /device:TPU:0, one launch (start us, length us, event | category | flops | bytes accessed | tf_op | source)
XLA Modules:
  0.0 1089.5 jit_solution(5630012394986021405)
XLA Ops:
  15.9 23.6 %all-gather.9.cloned.1.call-done = bf16[640,1152]{1,0:T(8,128)(2,1)} async-done(((bf16[80,1152]{1,0:T(8,128)(2,1)}), bf16[640,1152]{1,0:T(8,128)(2,1)}) %all-gather.9.cloned.1.call-update) | async-done | bytes 1474576 | tf_op jit(solution)/shard_map/all_gather | solution.py:353
  44.6 15.6 %collective-permute-done.1 = bf16[320,1152]{1,0:T(8,128)(2,1)S(1)} collective-permute-done((bf16[320,1152]{1,0:T(8,128)(2,1)S(1)}, bf16[320,1152]{1,0:T(8,128)(2,1)S(1)}, u32[]{:S(2)}, u32[]{:S(2)}) %collective-permute-start.1) | collective-permute-done | bytes 737312 | tf_op jit(solution)/shard_map/ppermute | solution.py:254
  64.3 6.0 collective-permute-done.2
  100.5 6.4 collective-permute-done.18
  111.5 7.0 collective-permute-done.6
  142.7 23.4 %attend.3 = (bf16[10,64,1024]{2,1,0:T(8,128)(2,1)S(1)}, f32[10,1,1024]{2,1,0:T(1,128)S(1)}) custom-call(s32[1]{0:T(128)} %bitcast.28.prefix_ref, bf16[10,96,1024]{2,1,0:T(8,128)(2,1)S(1)} %pad_maximum_fusion.6.query_ref, bf16[10,128,1024]{2,1,0:T(8,128)(2,1)S(1)} %bitcast.190, bf16[32,1024]{1,0:T(8,128)(2,1)S(1)} %slice_bitcast_fusion.rope_ref), custom_call_target="tpu_custom_call" | custom-call | flops 8053063680 | bytes 6144000 | tf_op jit(solution)/shard_map/attend/pallas_call | solution.py:110
  168.2 4.1 convolution_convert_fusion.7
  176.4 23.8 %attend.2 = (bf16[10,64,1024]{2,1,0:T(8,128)(2,1)S(1)}, f32[10,1,1024]{2,1,0:T(1,128)S(1)}) custom-call(s32[1]{0:T(128)} %bitcast.prefix_ref, bf16[10,96,1024]{2,1,0:T(8,128)(2,1)S(1)} %pad_maximum_fusion.5.query_ref, bf16[10,128,1024]{2,1,0:T(8,128)(2,1)S(1)} %bitcast.188, bf16[32,1024]{1,0:T(8,128)(2,1)S(1)} %slice_bitcast_fusion.1.rope_ref), custom_call_target="tpu_custom_call" | custom-call | flops 8053063680 | bytes 6144000 | tf_op jit(solution)/shard_map/attend/pallas_call | solution.py:110
  223.0 11.7 %collective-permute-done.9 = bf16[512,1280]{1,0:T(8,128)(2,1)} collective-permute-done((bf16[512,1280]{1,0:T(8,128)(2,1)}, bf16[512,1280]{1,0:T(8,128)(2,1)}, u32[]{:S(2)}, u32[]{:S(2)}) %collective-permute-start.9) | collective-permute-done | bytes 1310752 | tf_op jit(solution)/shard_map/ppermute | solution.py:254
  241.4 21.3 %collective-permute-done.33 = bf16[256,2560]{1,0:T(8,128)(2,1)S(1)} collective-permute-done((bf16[256,2560]{1,0:T(8,128)(2,1)}, bf16[256,2560]{1,0:T(8,128)(2,1)S(1)}, u32[]{:S(2)}, u32[]{:S(2)}) %collective-permute-start.33) | collective-permute-done | bytes 1310752 | tf_op jit(solution)/shard_map/ppermute | solution.py:254
  267.2 12.9 %collective-permute-done.22 = bf16[256,1280]{1,0:T(8,128)(2,1)S(1)} collective-permute-done((bf16[256,1280]{1,0:T(8,128)(2,1)S(1)}, bf16[256,1280]{1,0:T(8,128)(2,1)S(1)}, u32[]{:S(2)}, u32[]{:S(2)}) %collective-permute-start.22) | collective-permute-done | bytes 655392 | tf_op jit(solution)/shard_map/ppermute | solution.py:254
  284.7 9.5 collective-permute-done.10
  308.3 27.9 %collective-permute-done.30 = bf16[256,2560]{1,0:T(8,128)(2,1)S(1)} collective-permute-done((bf16[256,2560]{1,0:T(8,128)(2,1)S(1)}, bf16[256,2560]{1,0:T(8,128)(2,1)S(1)}, u32[]{:S(2)}, u32[]{:S(2)}) %collective-permute-start.30) | collective-permute-done | bytes 1310752 | tf_op jit(solution)/shard_map/ppermute | solution.py:254
  340.5 23.9 %collective-permute-done.14 = bf16[256,2560]{1,0:T(8,128)(2,1)S(1)} collective-permute-done((bf16[256,2560]{1,0:T(8,128)(2,1)S(1)}, bf16[256,2560]{1,0:T(8,128)(2,1)S(1)}, u32[]{:S(2)}, u32[]{:S(2)}) %collective-permute-start.14) | collective-permute-done | bytes 1310752 | tf_op jit(solution)/shard_map/ppermute | solution.py:254
  368.3 16.5 %collective-permute-done.15 = bf16[128,2560]{1,0:T(8,128)(2,1)S(1)} collective-permute-done((bf16[128,2560]{1,0:T(8,128)(2,1)S(1)}, bf16[128,2560]{1,0:T(8,128)(2,1)S(1)}, u32[]{:S(2)}, u32[]{:S(2)}) %collective-permute-start.15) | collective-permute-done | bytes 655392 | tf_op jit(solution)/shard_map/ppermute | solution.py:254
  397.6 15.3 %convolution_convert_fusion.2 = bf16[1024,1600]{1,0:T(8,128)(2,1)} fusion(bf16[1024,2560]{1,0:T(8,128)(2,1)} %constant_dynamic-update-slice_fusion.5.refs_1_.refs_0_, bf16[2560,1600]{1,0:T(8,128)(2,1)} %all-gather.15.cloned.1.call-done), kind=kOutput, calls=%fused_computation.47 | convolution fusion | flops 8390246400 | bytes 16711680 | tf_op jit(solution)/shard_map/dot_general | solution.py:34
  412.9 15.2 %convolution_convert_fusion.3 = bf16[1024,1600]{1,0:T(8,128)(2,1)} fusion(bf16[1024,2560]{1,0:T(8,128)(2,1)} %constant_dynamic-update-slice_fusion.5.refs_1_.refs_0_, bf16[2560,1600]{1,0:T(8,128)(2,1)} %all-gather.13.cloned.1.call-done), kind=kOutput, calls=%fused_computation.48 | convolution fusion | flops 8390246400 | bytes 16711680 | tf_op jit(solution)/shard_map/dot_general | solution.py:34
  428.1 20.5 %fusion.14 = (bf16[1024,1600]{1,0:T(8,128)(2,1)}, bf16[1024,1600]{1,0:T(8,128)(2,1)}, bf16[1024,1600]{1,0:T(8,128)(2,1)}) fusion(bf16[1024,1600]{1,0:T(8,128)(2,1)} %convolution_convert_fusion.3, bf16[1024,1600]{1,0:T(8,128)(2,1)} %convolution_convert_fusion.2, bf16[1024,2560]{1,0:T(8,128)(2,1)} %copy-done.79, ...), kind=kOutput, calls=%fused_computation.27 | convolution fusion | flops 8418099200 | bytes 29818880 | tf_op jit(solution)/shard_map/dot_general | solution.py:34
  450.9 15.4 %convolution_convert_fusion = bf16[1024,1600]{1,0:T(8,128)(2,1)} fusion(bf16[1024,2560]{1,0:T(8,128)(2,1)} %constant_dynamic-update-slice_fusion.15.refs_1_, bf16[2560,1600]{1,0:T(8,128)(2,1)} %all-gather.15.cloned.1.call-done), kind=kOutput, calls=%fused_computation.45 | convolution fusion | flops 8390246400 | bytes 16711680 | tf_op jit(solution)/shard_map/dot_general | solution.py:34
  466.3 14.6 %convolution_convert_fusion.1 = bf16[1024,1600]{1,0:T(8,128)(2,1)} fusion(bf16[1024,2560]{1,0:T(8,128)(2,1)S(1)} %bitcast.255, bf16[2560,1600]{1,0:T(8,128)(2,1)} %all-gather.13.cloned.1.call-done), kind=kOutput, calls=%fused_computation.46 | convolution fusion | flops 8390246400 | bytes 16711680 | tf_op jit(solution)/shard_map/dot_general | solution.py:34
  484.6 8.7 collective-permute-done.28
  494.9 16.3 %fusion.20 = (bf16[1024,1600]{1,0:T(8,128)(2,1)}, bf16[1024,1600]{1,0:T(8,128)(2,1)}, bf16[1024,1600]{1,0:T(8,128)(2,1)}) fusion(bf16[1024,1600]{1,0:T(8,128)(2,1)} %convolution_convert_fusion.1, bf16[1024,1600]{1,0:T(8,128)(2,1)} %convolution_convert_fusion, bf16[1024,2560]{1,0:T(8,128)(2,1)S(1)} %constant_dynamic-update-slice_fusion.10.refs_1_, ...), kind=kOutput, calls=%fused_computation.33 | convolution fusion | flops 8418099200 | bytes 29818880 | tf_op jit(solution)/shard_map/dot_general | solution.py:34
  511.2 24.9 %weight_grad.3 = bf16[2560,1600]{1,0:T(8,128)(2,1)} custom-call(bf16[1024,2560]{1,0:T(8,128)(2,1)} %copy-done.79, bf16[1024,2560]{1,0:T(8,128)(2,1)} %copy-done.80, bf16[1024,1600]{1,0:T(8,128)(2,1)} %get-tuple-element.83.refs_2_, bf16[1024,1600]{1,0:T(8,128)(2,1)} %get-tuple-element.84.refs_3_), custom_call_target="tpu_custom_call" | custom-call | flops 16777216000 | bytes 25231360 | tf_op jit(solution)/shard_map/weight_grad/pallas_call | solution.py:236
  537.9 5.5 fusion.93
  543.4 6.3 fusion.22
  553.7 3.7 fusion.23
  560.8 3.9 fusion.24
  569.0 3.7 fusion.25
  591.9 25.2 %weight_grad.4 = bf16[2560,1600]{1,0:T(8,128)(2,1)} custom-call(bf16[1024,2560]{1,0:T(8,128)(2,1)} %constant_dynamic-update-slice_fusion.5.refs_1_.refs_0_, bf16[1024,2560]{1,0:T(8,128)(2,1)} %constant_dynamic-update-slice_fusion.15.refs_1_, bf16[1024,1600]{1,0:T(8,128)(2,1)} %get-tuple-element.85.refs_2_, bf16[1024,1600]{1,0:T(8,128)(2,1)} %get-tuple-element.81.refs_3_), custom_call_target="tpu_custom_call" | custom-call | flops 16777216000 | bytes 25231360 | tf_op jit(solution)/shard_map/weight_grad/pallas_call | solution.py:236
  617.1 5.1 fusion.73
  622.2 5.1 fusion.85
  631.3 4.6 add_convert_fusion.9
  637.3 4.8 add_convert_fusion.8
  653.7 4.0 collective-permute-done.40
  682.9 25.4 %weight_grad.5 = bf16[2560,1600]{1,0:T(8,128)(2,1)} custom-call(bf16[1024,2560]{1,0:T(8,128)(2,1)} %constant_dynamic-update-slice_fusion.5.refs_1_.refs_0_, bf16[1024,2560]{1,0:T(8,128)(2,1)} %constant_dynamic-update-slice_fusion.15.refs_1_, bf16[1024,1600]{1,0:T(8,128)(2,1)} %get-tuple-element.86.refs_2_, bf16[1024,1600]{1,0:T(8,128)(2,1)} %get-tuple-element.82.refs_3_), custom_call_target="tpu_custom_call" | custom-call | flops 16777216000 | bytes 25231360 | tf_op jit(solution)/shard_map/weight_grad/pallas_call | solution.py:236
  711.2 23.3 %collective-permute-done.58 = bf16[256,2560]{1,0:T(8,128)(2,1)} collective-permute-done((bf16[256,2560]{1,0:T(8,128)(2,1)}, bf16[256,2560]{1,0:T(8,128)(2,1)}, u32[]{:S(2)}, u32[]{:S(2)}) %collective-permute-start.58) | collective-permute-done | bytes 1310752 | tf_op jit(solution)/shard_map/ppermute | solution.py:254
  746.2 6.7 collective-permute-done.59
  754.2 6.0 convolution_convert_fusion.11
  761.8 3.8 convolution_convert_fusion.10
  766.0 3.8 convolution_convert_fusion.13
  770.3 3.7 convolution_convert_fusion.12
  775.5 3.8 convolution_convert_fusion.16
  779.3 30.3 %attend_back.3 = (bf16[10,96,1024]{2,1,0:T(8,128)(2,1)S(1)}, bf16[10,128,1024]{2,1,0:T(8,128)(2,1)S(1)}, f32[32,1024]{1,0:T(8,128)S(1)}) custom-call(s32[1]{0:T(128)} %bitcast.28.prefix_ref, bf16[10,96,1024]{2,1,0:T(8,128)(2,1)S(1)} %copy-done.13, bf16[10,128,1024]{2,1,0:T(8,128)(2,1)S(1)} %bitcast.191, bf16[32,1024]{1,0:T(8,128)(2,1)S(1)} %copy-done.19, ...), custom_call_target="tpu_custom_call" | custom-call | flops 20132659200 | bytes 11264000 | tf_op jit(solution)/shard_map/attend_back/pallas_call | solution.py:188
  811.0 5.6 fusion.227
  816.6 5.6 fusion.54
  825.9 3.8 fusion.59
  832.6 4.3 fusion.237
  836.9 7.7 convolution_convert_fusion.17
  844.6 8.6 add_convert_fusion
  857.4 4.9 fusion.49
  865.4 3.8 add_convert_fusion.5
  892.6 30.4 %attend_back.2 = (bf16[10,96,1024]{2,1,0:T(8,128)(2,1)S(1)}, bf16[10,128,1024]{2,1,0:T(8,128)(2,1)S(1)}, f32[32,1024]{1,0:T(8,128)S(1)}) custom-call(s32[1]{0:T(128)} %bitcast.prefix_ref, bf16[10,96,1024]{2,1,0:T(8,128)(2,1)S(1)} %copy-done.11, bf16[10,128,1024]{2,1,0:T(8,128)(2,1)S(1)} %bitcast.189, bf16[32,1024]{1,0:T(8,128)(2,1)S(1)} %copy-done.17, ...), custom_call_target="tpu_custom_call" | custom-call | flops 20132659200 | bytes 11264000 | tf_op jit(solution)/shard_map/attend_back/pallas_call | solution.py:188
  930.8 5.8 collective-permute-done.61
  938.8 7.2 collective-permute-done.65
  970.2 10.0 multiply_reduce_fusion
  981.8 6.2 fusion
  995.1 4.3 add_convert_fusion.1
  1009.1 4.6 fusion.27
  1024.3 11.9 %collective-permute-done.70 = bf16[640,512]{1,0:T(8,128)(2,1)S(1)} collective-permute-done((bf16[640,512]{1,0:T(8,128)(2,1)S(1)}, bf16[640,512]{1,0:T(8,128)(2,1)S(1)}, u32[]{:S(2)}, u32[]{:S(2)}) %collective-permute-start.70) | collective-permute-done | bytes 655392 | tf_op jit(solution)/shard_map/ppermute | solution.py:254
  1036.9 3.8 collective-permute-done.72
  1042.7 3.7 subtract_multiply_fusion
  1047.1 3.9 collective-permute-done.73
  1052.2 4.3 fusion.35
  1063.0 13.0 %reduce-scatter.17.cloned.1.call-done = bf16[80,1152]{1,0:T(8,128)(2,1)} async-done(((bf16[320,1152]{1,0:T(8,128)(2,1)}), bf16[80,1152]{1,0:T(8,128)(2,1)}) %reduce-scatter.17.cloned.1.call-update) | async-done | bytes 184336 | tf_op jit(solution)/shard_map/reduce_scatter | solution.py:392
  (739 shorter events, 375.6 us)
Async XLA Ops:
  7.2 32.3 %all-gather.9.cloned.1.call-start = ((), (), s32[]{:S(2)}) async-start(), calls=%async_computation.7 | async-start | bytes 1658880 | tf_op jit(solution)/shard_map/all_gather | solution.py:353
  12.1 82.9 %all-gather.7.cloned.1.call-start = ((), (), s32[]{:S(2)}) async-start(), calls=%async_computation.6 | async-start | bytes 2949120 | tf_op jit(solution)/shard_map/all_gather | solution.py:428
  13.9 154.2 %all-gather.11.cloned.1.call-start = ((), (), s32[]{:S(2)}) async-start(), calls=%async_computation.8 | async-start | bytes 3686400 | tf_op jit(solution)/shard_map/all_gather | solution.py:428
  14.7 382.9 %all-gather.15.cloned.1.call-start = ((), (), s32[]{:S(2)}) async-start(), calls=%async_computation.10 | async-start | bytes 9584640 | tf_op jit(solution)/shard_map/all_gather | solution.py:428
  15.2 397.6 %all-gather.13.cloned.1.call-start = ((), (), s32[]{:S(2)}) async-start(), calls=%async_computation.9 | async-start | bytes 9584640 | tf_op jit(solution)/shard_map/all_gather | solution.py:428
  15.8 412.2 %all-gather.17.cloned.1.call-start = ((), (), s32[]{:S(2)}) async-start(), calls=%async_computation.11 | async-start | bytes 9584640 | tf_op jit(solution)/shard_map/all_gather | solution.py:428
  41.6 18.6 %collective-permute-start.1 = (bf16[320,1152]{1,0:T(8,128)(2,1)S(1)}, bf16[320,1152]{1,0:T(8,128)(2,1)S(1)}, u32[]{:S(2)}, u32[]{:S(2)}) collective-permute-start(bf16[320,1152]{1,0:T(8,128)(2,1)S(1)} %get-tuple-element.134), channel_id=1, source_target_pairs={{0,2},{1,3},{2,0},{3,1},{4,6},{5,7},{6,4},{7,5},{8,10},{9,11},{10,... | collective-permute-start | bytes 2211848 | tf_op jit(solution)/shard_map/ppermute | solution.py:254
  43.1 18.7 %collective-permute-start = (bf16[320,1152]{1,0:T(8,128)(2,1)S(1)}, bf16[320,1152]{1,0:T(8,128)(2,1)S(1)}, u32[]{:S(2)}, u32[]{:S(2)}) collective-permute-start(bf16[320,1152]{1,0:T(8,128)(2,1)S(1)} %get-tuple-element.134), channel_id=1, source_target_pairs={{0,1},{1,0},{2,3},{3,2},{4,5},{5,4},{6,7},{7,6},{8,9},{9,8},{10,11... | collective-permute-start | bytes 2211848 | tf_op jit(solution)/shard_map/ppermute | solution.py:254
  44.5 586.4 %reduce-scatter.7.cloned.1.call-start = ((), (), s32[]{:S(2)}) async-start(), calls=%async_computation.12 | async-start | bytes 9584640 | tf_op jit(solution)/shard_map/reduce_scatter | solution.py:431
  90.4 18.5 %collective-permute-start.17 = (bf16[256,1056]{0,1:T(8,128)(2,1)}, bf16[256,1056]{0,1:T(8,128)(2,1)}, u32[]{:S(2)}, u32[]{:S(2)}) collective-permute-start(bf16[256,1056]{0,1:T(8,128)(2,1)} %get-tuple-element.178), channel_id=1, source_target_pairs={{0,1},{1,0},{2,3},{3,2},{4,5},{5,4},{6,7},{7,6},{8,9},{9,8},{10,11... | collective-permute-start | bytes 1622024 | tf_op jit(solution)/shard_map/ppermute | solution.py:254
  92.8 27.7 %collective-permute-start.5 = (bf16[256,1056]{0,1:T(8,128)(2,1)}, bf16[256,1056]{0,1:T(8,128)(2,1)}, u32[]{:S(2)}, u32[]{:S(2)}) collective-permute-start(bf16[256,1056]{0,1:T(8,128)(2,1)} %get-tuple-element.176), channel_id=1, source_target_pairs={{0,1},{1,0},{2,3},{3,2},{4,5},{5,4},{6,7},{7,6},{8,9},{9,8},{10,11... | collective-permute-start | bytes 1622024 | tf_op jit(solution)/shard_map/ppermute | solution.py:254
  93.9 24.6 %collective-permute-start.6 = (bf16[256,1056]{0,1:T(8,128)(2,1)}, bf16[256,1056]{0,1:T(8,128)(2,1)}, u32[]{:S(2)}, u32[]{:S(2)}) collective-permute-start(bf16[256,1056]{0,1:T(8,128)(2,1)} %get-tuple-element.176), channel_id=1, source_target_pairs={{0,2},{1,3},{2,0},{3,1},{4,6},{5,7},{6,4},{7,5},{8,10},{9,11},{10,... | collective-permute-start | bytes 1622024 | tf_op jit(solution)/shard_map/ppermute | solution.py:254
  107.9 21.4 %collective-permute-start.19 = (bf16[128,1056]{0,1:T(8,128)(2,1)S(1)}, bf16[128,1056]{0,1:T(8,128)(2,1)S(1)}, u32[]{:S(2)}, u32[]{:S(2)}) collective-permute-start(bf16[128,1056]{0,1:T(8,128)(2,1)S(1)} %slice.716), channel_id=1, source_target_pairs={{0,1},{1,0},{2,3},{3,2},{4,5},{5,4},{6,7},{7,6},{8,9},{9,8},{10,11... | collective-permute-start | bytes 811016 | tf_op jit(solution)/shard_map/ppermute | solution.py:254
  109.9 19.3 %collective-permute-start.20 = (bf16[128,1056]{0,1:T(8,128)(2,1)S(1)}, bf16[128,1056]{0,1:T(8,128)(2,1)S(1)}, u32[]{:S(2)}, u32[]{:S(2)}) collective-permute-start(bf16[128,1056]{0,1:T(8,128)(2,1)S(1)} %slice.717), channel_id=1, source_target_pairs={{0,2},{1,3},{2,0},{3,1},{4,6},{5,7},{6,4},{7,5},{8,10},{9,11},{10,... | collective-permute-start | bytes 811016 | tf_op jit(solution)/shard_map/ppermute | solution.py:254
  172.3 44.1 %collective-permute-start.21 = (bf16[512,1280]{1,0:T(8,128)(2,1)}, bf16[512,1280]{1,0:T(8,128)(2,1)}, u32[]{:S(2)}, u32[]{:S(2)}) collective-permute-start(bf16[512,1280]{1,0:T(8,128)(2,1)} %convolution_convert_fusion.7), channel_id=1, source_target_pairs={{0,1},{1,0},{2,3},{3,2},{4,5},{5,4},{6,7},{7,6},{8,9},{9,8},{10,11... | collective-permute-start | bytes 3932168 | tf_op jit(solution)/shard_map/ppermute | solution.py:254
  175.6 44.3 %collective-permute-start.23 = (bf16[512,1280]{1,0:T(8,128)(2,1)}, bf16[512,1280]{1,0:T(8,128)(2,1)}, u32[]{:S(2)}, u32[]{:S(2)}) collective-permute-start(bf16[512,1280]{1,0:T(8,128)(2,1)} %convolution_convert_fusion.6), channel_id=1, source_target_pairs={{0,2},{1,3},{2,0},{3,1},{4,6},{5,7},{6,4},{7,5},{8,10},{9,11},{10,... | collective-permute-start | bytes 3932168 | tf_op jit(solution)/shard_map/ppermute | solution.py:254
  202.7 32.0 %collective-permute-start.9 = (bf16[512,1280]{1,0:T(8,128)(2,1)}, bf16[512,1280]{1,0:T(8,128)(2,1)}, u32[]{:S(2)}, u32[]{:S(2)}) collective-permute-start(bf16[512,1280]{1,0:T(8,128)(2,1)} %convolution_convert_fusion.9), channel_id=1, source_target_pairs={{0,1},{1,0},{2,3},{3,2},{4,5},{5,4},{6,7},{7,6},{8,9},{9,8},{10,11... | collective-permute-start | bytes 3932168 | tf_op jit(solution)/shard_map/ppermute | solution.py:254
  206.0 32.0 %collective-permute-start.11 = (bf16[512,1280]{1,0:T(8,128)(2,1)}, bf16[512,1280]{1,0:T(8,128)(2,1)}, u32[]{:S(2)}, u32[]{:S(2)}) collective-permute-start(bf16[512,1280]{1,0:T(8,128)(2,1)} %convolution_convert_fusion.8), channel_id=1, source_target_pairs={{0,2},{1,3},{2,0},{3,1},{4,6},{5,7},{6,4},{7,5},{8,10},{9,11},{10,... | collective-permute-start | bytes 3932168 | tf_op jit(solution)/shard_map/ppermute | solution.py:254
  209.1 53.6 %collective-permute-start.33 = (bf16[256,2560]{1,0:T(8,128)(2,1)}, bf16[256,2560]{1,0:T(8,128)(2,1)S(1)}, u32[]{:S(2)}, u32[]{:S(2)}) collective-permute-start(bf16[256,2560]{1,0:T(8,128)(2,1)} %tie.3), channel_id=1, source_target_pairs={{0,1},{1,0},{2,3},{3,2},{4,5},{5,4},{6,7},{7,6},{8,9},{9,8},{10,11... | collective-permute-start | bytes 3932168 | tf_op jit(solution)/shard_map/ppermute | solution.py:254
  216.4 49.6 %collective-permute-start.34 = (bf16[256,2560]{1,0:T(8,128)(2,1)S(1)}, bf16[256,2560]{1,0:T(8,128)(2,1)S(1)}, u32[]{:S(2)}, u32[]{:S(2)}) collective-permute-start(bf16[256,2560]{1,0:T(8,128)(2,1)S(1)} %copy-done.44), channel_id=1, source_target_pairs={{0,2},{1,3},{2,0},{3,1},{4,6},{5,7},{6,4},{7,5},{8,10},{9,11},{10,... | collective-permute-start | bytes 3932168 | tf_op jit(solution)/shard_map/ppermute | solution.py:254
  220.0 60.1 %collective-permute-start.22 = (bf16[256,1280]{1,0:T(8,128)(2,1)S(1)}, bf16[256,1280]{1,0:T(8,128)(2,1)S(1)}, u32[]{:S(2)}, u32[]{:S(2)}) collective-permute-start(bf16[256,1280]{1,0:T(8,128)(2,1)S(1)} %add_convert_fusion.11), channel_id=1, source_target_pairs={{0,2},{1,3},{2,0},{3,1},{4,6},{5,7},{6,4},{7,5},{8,10},{9,11},{10,... | collective-permute-start | bytes 1966088 | tf_op jit(solution)/shard_map/ppermute | solution.py:254
  234.7 48.1 %collective-permute-start.24 = (bf16[256,1280]{1,0:T(8,128)(2,1)S(1)}, bf16[256,1280]{1,0:T(8,128)(2,1)S(1)}, u32[]{:S(2)}, u32[]{:S(2)}) collective-permute-start(bf16[256,1280]{1,0:T(8,128)(2,1)S(1)} %add_convert_fusion.10), channel_id=1, source_target_pairs={{0,1},{1,0},{2,3},{3,2},{4,5},{5,4},{6,7},{7,6},{8,9},{9,8},{10,11... | collective-permute-start | bytes 1966088 | tf_op jit(solution)/shard_map/ppermute | solution.py:254
  238.1 56.1 %collective-permute-start.10 = (bf16[256,1280]{1,0:T(8,128)(2,1)S(1)}, bf16[256,1280]{1,0:T(8,128)(2,1)S(1)}, u32[]{:S(2)}, u32[]{:S(2)}) collective-permute-start(bf16[256,1280]{1,0:T(8,128)(2,1)S(1)} %add_convert_fusion.13), channel_id=1, source_target_pairs={{0,2},{1,3},{2,0},{3,1},{4,6},{5,7},{6,4},{7,5},{8,10},{9,11},{10,... | collective-permute-start | bytes 1966088 | tf_op jit(solution)/shard_map/ppermute | solution.py:254
  262.7 32.8 %collective-permute-start.12 = (bf16[256,1280]{1,0:T(8,128)(2,1)S(1)}, bf16[256,1280]{1,0:T(8,128)(2,1)S(1)}, u32[]{:S(2)}, u32[]{:S(2)}) collective-permute-start(bf16[256,1280]{1,0:T(8,128)(2,1)S(1)} %add_convert_fusion.12), channel_id=1, source_target_pairs={{0,1},{1,0},{2,3},{3,2},{4,5},{5,4},{6,7},{7,6},{8,9},{9,8},{10,11... | collective-permute-start | bytes 1966088 | tf_op jit(solution)/shard_map/ppermute | solution.py:254
  266.1 38.8 %collective-permute-start.35 = (bf16[128,2560]{1,0:T(8,128)(2,1)S(1)}, bf16[128,2560]{1,0:T(8,128)(2,1)S(1)}, u32[]{:S(2)}, u32[]{:S(2)}) collective-permute-start(bf16[128,2560]{1,0:T(8,128)(2,1)S(1)} %slice.590), channel_id=1, source_target_pairs={{0,1},{1,0},{2,3},{3,2},{4,5},{5,4},{6,7},{7,6},{8,9},{9,8},{10,11... | collective-permute-start | bytes 1966088 | tf_op jit(solution)/shard_map/ppermute | solution.py:254
  280.1 28.1 %collective-permute-start.36 = (bf16[128,2560]{1,0:T(8,128)(2,1)S(1)}, bf16[128,2560]{1,0:T(8,128)(2,1)S(1)}, u32[]{:S(2)}, u32[]{:S(2)}) collective-permute-start(bf16[128,2560]{1,0:T(8,128)(2,1)S(1)} %slice.591), channel_id=1, source_target_pairs={{0,2},{1,3},{2,0},{3,1},{4,6},{5,7},{6,4},{7,5},{8,10},{9,11},{10,... | collective-permute-start | bytes 1966088 | tf_op jit(solution)/shard_map/ppermute | solution.py:254
  301.4 36.7 %collective-permute-start.29 = (bf16[256,2560]{1,0:T(8,128)(2,1)S(1)}, bf16[256,2560]{1,0:T(8,128)(2,1)S(1)}, u32[]{:S(2)}, u32[]{:S(2)}) collective-permute-start(bf16[256,2560]{1,0:T(8,128)(2,1)S(1)} %get-tuple-element.159), channel_id=1, source_target_pairs={{0,1},{1,0},{2,3},{3,2},{4,5},{5,4},{6,7},{7,6},{8,9},{9,8},{10,11... | collective-permute-start | bytes 3932168 | tf_op jit(solution)/shard_map/ppermute | solution.py:254
  302.5 33.8 %collective-permute-start.30 = (bf16[256,2560]{1,0:T(8,128)(2,1)S(1)}, bf16[256,2560]{1,0:T(8,128)(2,1)S(1)}, u32[]{:S(2)}, u32[]{:S(2)}) collective-permute-start(bf16[256,2560]{1,0:T(8,128)(2,1)S(1)} %get-tuple-element.159), channel_id=1, source_target_pairs={{0,2},{1,3},{2,0},{3,1},{4,6},{5,7},{6,4},{7,5},{8,10},{9,11},{10,... | collective-permute-start | bytes 3932168 | tf_op jit(solution)/shard_map/ppermute | solution.py:254
  303.9 61.6 %collective-permute-start.13 = (bf16[256,2560]{1,0:T(8,128)(2,1)S(1)}, bf16[256,2560]{1,0:T(8,128)(2,1)S(1)}, u32[]{:S(2)}, u32[]{:S(2)}) collective-permute-start(bf16[256,2560]{1,0:T(8,128)(2,1)S(1)} %get-tuple-element.130), channel_id=1, source_target_pairs={{0,1},{1,0},{2,3},{3,2},{4,5},{5,4},{6,7},{7,6},{8,9},{9,8},{10,11... | collective-permute-start | bytes 3932168 | tf_op jit(solution)/shard_map/ppermute | solution.py:254
  304.9 59.5 %collective-permute-start.14 = (bf16[256,2560]{1,0:T(8,128)(2,1)S(1)}, bf16[256,2560]{1,0:T(8,128)(2,1)S(1)}, u32[]{:S(2)}, u32[]{:S(2)}) collective-permute-start(bf16[256,2560]{1,0:T(8,128)(2,1)S(1)} %get-tuple-element.130), channel_id=1, source_target_pairs={{0,2},{1,3},{2,0},{3,1},{4,6},{5,7},{6,4},{7,5},{8,10},{9,11},{10,... | collective-permute-start | bytes 3932168 | tf_op jit(solution)/shard_map/ppermute | solution.py:254
  337.2 55.2 %collective-permute-start.31 = (bf16[128,2560]{1,0:T(8,128)(2,1)}, bf16[128,2560]{1,0:T(8,128)(2,1)S(1)}, u32[]{:S(2)}, u32[]{:S(2)}) collective-permute-start(bf16[128,2560]{1,0:T(8,128)(2,1)} %slice.726), channel_id=1, source_target_pairs={{0,1},{1,0},{2,3},{3,2},{4,5},{5,4},{6,7},{7,6},{8,9},{9,8},{10,11... | collective-permute-start | bytes 1966088 | tf_op jit(solution)/shard_map/ppermute | solution.py:254
  339.0 54.3 %collective-permute-start.32 = (bf16[128,2560]{1,0:T(8,128)(2,1)}, bf16[128,2560]{1,0:T(8,128)(2,1)}, u32[]{:S(2)}, u32[]{:S(2)}) collective-permute-start(bf16[128,2560]{1,0:T(8,128)(2,1)} %slice.727), channel_id=1, source_target_pairs={{0,2},{1,3},{2,0},{3,1},{4,6},{5,7},{6,4},{7,5},{8,10},{9,11},{10,... | collective-permute-start | bytes 1966088 | tf_op jit(solution)/shard_map/ppermute | solution.py:254
  364.4 20.5 %collective-permute-start.15 = (bf16[128,2560]{1,0:T(8,128)(2,1)S(1)}, bf16[128,2560]{1,0:T(8,128)(2,1)S(1)}, u32[]{:S(2)}, u32[]{:S(2)}) collective-permute-start(bf16[128,2560]{1,0:T(8,128)(2,1)S(1)} %slice.713), channel_id=1, source_target_pairs={{0,1},{1,0},{2,3},{3,2},{4,5},{5,4},{6,7},{7,6},{8,9},{9,8},{10,11... | collective-permute-start | bytes 1966088 | tf_op jit(solution)/shard_map/ppermute | solution.py:254
  365.5 22.8 %collective-permute-start.16 = (bf16[128,2560]{1,0:T(8,128)(2,1)S(1)}, bf16[128,2560]{1,0:T(8,128)(2,1)S(1)}, u32[]{:S(2)}, u32[]{:S(2)}) collective-permute-start(bf16[128,2560]{1,0:T(8,128)(2,1)S(1)} %slice.714), channel_id=1, source_target_pairs={{0,2},{1,3},{2,0},{3,1},{4,6},{5,7},{6,4},{7,5},{8,10},{9,11},{10,... | collective-permute-start | bytes 1966088 | tf_op jit(solution)/shard_map/ppermute | solution.py:254
  390.3 58.2 %collective-permute-start.25 = (bf16[256,2560]{1,0:T(8,128)(2,1)}, bf16[256,2560]{1,0:T(8,128)(2,1)}, u32[]{:S(2)}, u32[]{:S(2)}) collective-permute-start(bf16[256,2560]{1,0:T(8,128)(2,1)} %tie.2), channel_id=1, source_target_pairs={{0,1},{1,0},{2,3},{3,2},{4,5},{5,4},{6,7},{7,6},{8,9},{9,8},{10,11... | collective-permute-start | bytes 3932168 | tf_op jit(solution)/shard_map/ppermute | solution.py:254
  391.0 57.6 %collective-permute-start.26 = (bf16[256,2560]{1,0:T(8,128)(2,1)}, bf16[256,2560]{1,0:T(8,128)(2,1)}, u32[]{:S(2)}, u32[]{:S(2)}) collective-permute-start(bf16[256,2560]{1,0:T(8,128)(2,1)} %tie.2), channel_id=1, source_target_pairs={{0,2},{1,3},{2,0},{3,1},{4,6},{5,7},{6,4},{7,5},{8,10},{9,11},{10,... | collective-permute-start | bytes 3932168 | tf_op jit(solution)/shard_map/ppermute | solution.py:254
  449.9 34.7 %collective-permute-start.27 = (bf16[128,2560]{1,0:T(8,128)(2,1)S(1)}, bf16[128,2560]{1,0:T(8,128)(2,1)S(1)}, u32[]{:S(2)}, u32[]{:S(2)}) collective-permute-start(bf16[128,2560]{1,0:T(8,128)(2,1)S(1)} %slice.585), channel_id=1, source_target_pairs={{0,1},{1,0},{2,3},{3,2},{4,5},{5,4},{6,7},{7,6},{8,9},{9,8},{10,11... | collective-permute-start | bytes 1966088 | tf_op jit(solution)/shard_map/ppermute | solution.py:254
  536.1 274.8 %reduce-scatter.9.cloned.1.call-start = ((), (), s32[]{:S(2)}) async-start(), calls=%async_computation.13 | async-start | bytes 9584640 | tf_op jit(solution)/shard_map/reduce_scatter | solution.py:431
  549.8 81.5 %collective-permute-start.37 = (bf16[512,1280]{1,0:T(8,128)(2,1)}, bf16[512,1280]{1,0:T(8,128)(2,1)}, u32[]{:S(2)}, u32[]{:S(2)}) collective-permute-start(bf16[512,1280]{1,0:T(8,128)(2,1)} %fusion.22), channel_id=1, source_target_pairs={{0,1},{1,0},{2,3},{3,2},{4,5},{5,4},{6,7},{7,6},{8,9},{9,8},{10,11... | collective-permute-start | bytes 3932168 | tf_op jit(solution)/shard_map/ppermute | solution.py:254
  557.4 79.9 %collective-permute-start.39 = (bf16[512,1280]{1,0:T(8,128)(2,1)}, bf16[512,1280]{1,0:T(8,128)(2,1)}, u32[]{:S(2)}, u32[]{:S(2)}) collective-permute-start(bf16[512,1280]{1,0:T(8,128)(2,1)} %fusion.23), channel_id=1, source_target_pairs={{0,2},{1,3},{2,0},{3,1},{4,6},{5,7},{6,4},{7,5},{8,10},{9,11},{10,... | collective-permute-start | bytes 3932168 | tf_op jit(solution)/shard_map/ppermute | solution.py:254
  564.7 78.2 %collective-permute-start.53 = (bf16[512,1280]{1,0:T(8,128)(2,1)}, bf16[512,1280]{1,0:T(8,128)(2,1)}, u32[]{:S(2)}, u32[]{:S(2)}) collective-permute-start(bf16[512,1280]{1,0:T(8,128)(2,1)} %fusion.24), channel_id=1, source_target_pairs={{0,1},{1,0},{2,3},{3,2},{4,5},{5,4},{6,7},{7,6},{8,9},{9,8},{10,11... | collective-permute-start | bytes 3932168 | tf_op jit(solution)/shard_map/ppermute | solution.py:254
  572.7 74.1 %collective-permute-start.55 = (bf16[512,1280]{1,0:T(8,128)(2,1)}, bf16[512,1280]{1,0:T(8,128)(2,1)}, u32[]{:S(2)}, u32[]{:S(2)}) collective-permute-start(bf16[512,1280]{1,0:T(8,128)(2,1)} %fusion.25), channel_id=1, source_target_pairs={{0,2},{1,3},{2,0},{3,1},{4,6},{5,7},{6,4},{7,5},{8,10},{9,11},{10,... | collective-permute-start | bytes 3932168 | tf_op jit(solution)/shard_map/ppermute | solution.py:254
  631.0 328.9 %reduce-scatter.11.cloned.1.call-start = ((), (), s32[]{:S(2)}) async-start(), calls=%async_computation.14 | async-start | bytes 9584640 | tf_op jit(solution)/shard_map/reduce_scatter | solution.py:431
  673.0 37.5 %collective-permute-start.41 = (bf16[256,2560]{1,0:T(8,128)(2,1)}, bf16[256,2560]{1,0:T(8,128)(2,1)S(1)}, u32[]{:S(2)}, u32[]{:S(2)}) collective-permute-start(bf16[256,2560]{1,0:T(8,128)(2,1)} %get-tuple-element.127), channel_id=1, source_target_pairs={{0,1},{1,0},{2,3},{3,2},{4,5},{5,4},{6,7},{7,6},{8,9},{9,8},{10,11... | collective-permute-start | bytes 3932168 | tf_op jit(solution)/shard_map/ppermute | solution.py:254
  674.4 34.5 %collective-permute-start.42 = (bf16[256,2560]{1,0:T(8,128)(2,1)}, bf16[256,2560]{1,0:T(8,128)(2,1)S(1)}, u32[]{:S(2)}, u32[]{:S(2)}) collective-permute-start(bf16[256,2560]{1,0:T(8,128)(2,1)} %get-tuple-element.127), channel_id=1, source_target_pairs={{0,2},{1,3},{2,0},{3,1},{4,6},{5,7},{6,4},{7,5},{8,10},{9,11},{10,... | collective-permute-start | bytes 3932168 | tf_op jit(solution)/shard_map/ppermute | solution.py:254
  680.9 55.5 %collective-permute-start.57 = (bf16[256,2560]{1,0:T(8,128)(2,1)}, bf16[256,2560]{1,0:T(8,128)(2,1)}, u32[]{:S(2)}, u32[]{:S(2)}) collective-permute-start(bf16[256,2560]{1,0:T(8,128)(2,1)} %get-tuple-element.124), channel_id=1, source_target_pairs={{0,1},{1,0},{2,3},{3,2},{4,5},{5,4},{6,7},{7,6},{8,9},{9,8},{10,11... | collective-permute-start | bytes 3932168 | tf_op jit(solution)/shard_map/ppermute | solution.py:254
  682.3 52.2 %collective-permute-start.58 = (bf16[256,2560]{1,0:T(8,128)(2,1)}, bf16[256,2560]{1,0:T(8,128)(2,1)}, u32[]{:S(2)}, u32[]{:S(2)}) collective-permute-start(bf16[256,2560]{1,0:T(8,128)(2,1)} %get-tuple-element.124), channel_id=1, source_target_pairs={{0,2},{1,3},{2,0},{3,1},{4,6},{5,7},{6,4},{7,5},{8,10},{9,11},{10,... | collective-permute-start | bytes 3932168 | tf_op jit(solution)/shard_map/ppermute | solution.py:254
  709.0 36.9 %collective-permute-start.43 = (bf16[128,2560]{1,0:T(8,128)(2,1)S(1)}, bf16[128,2560]{1,0:T(8,128)(2,1)S(1)}, u32[]{:S(2)}, u32[]{:S(2)}) collective-permute-start(bf16[128,2560]{1,0:T(8,128)(2,1)S(1)} %slice.736), channel_id=1, source_target_pairs={{0,1},{1,0},{2,3},{3,2},{4,5},{5,4},{6,7},{7,6},{8,9},{9,8},{10,11... | collective-permute-start | bytes 1966088 | tf_op jit(solution)/shard_map/ppermute | solution.py:254
  710.6 35.4 %collective-permute-start.44 = (bf16[128,2560]{1,0:T(8,128)(2,1)S(1)}, bf16[128,2560]{1,0:T(8,128)(2,1)S(1)}, u32[]{:S(2)}, u32[]{:S(2)}) collective-permute-start(bf16[128,2560]{1,0:T(8,128)(2,1)S(1)} %slice.737), channel_id=1, source_target_pairs={{0,2},{1,3},{2,0},{3,1},{4,6},{5,7},{6,4},{7,5},{8,10},{9,11},{10,... | collective-permute-start | bytes 1966088 | tf_op jit(solution)/shard_map/ppermute | solution.py:254
  735.7 17.2 %collective-permute-start.59 = (bf16[128,2560]{1,0:T(8,128)(2,1)S(1)}, bf16[128,2560]{1,0:T(8,128)(2,1)S(1)}, u32[]{:S(2)}, u32[]{:S(2)}) collective-permute-start(bf16[128,2560]{1,0:T(8,128)(2,1)S(1)} %slice.752), channel_id=1, source_target_pairs={{0,1},{1,0},{2,3},{3,2},{4,5},{5,4},{6,7},{7,6},{8,9},{9,8},{10,11... | collective-permute-start | bytes 1966088 | tf_op jit(solution)/shard_map/ppermute | solution.py:254
  760.2 105.2 %collective-permute-start.49 = (bf16[512,1280]{1,0:T(8,128)(2,1)}, bf16[512,1280]{1,0:T(8,128)(2,1)}, u32[]{:S(2)}, u32[]{:S(2)}) collective-permute-start(bf16[512,1280]{1,0:T(8,128)(2,1)} %convolution_convert_fusion.11), channel_id=1, source_target_pairs={{0,1},{1,0},{2,3},{3,2},{4,5},{5,4},{6,7},{7,6},{8,9},{9,8},{10,11... | collective-permute-start | bytes 3932168 | tf_op jit(solution)/shard_map/ppermute | solution.py:254
  765.6 104.2 %collective-permute-start.51 = (bf16[512,1280]{1,0:T(8,128)(2,1)}, bf16[512,1280]{1,0:T(8,128)(2,1)}, u32[]{:S(2)}, u32[]{:S(2)}) collective-permute-start(bf16[512,1280]{1,0:T(8,128)(2,1)} %convolution_convert_fusion.10), channel_id=1, source_target_pairs={{0,2},{1,3},{2,0},{3,1},{4,6},{5,7},{6,4},{7,5},{8,10},{9,11},{10,... | collective-permute-start | bytes 3932168 | tf_op jit(solution)/shard_map/ppermute | solution.py:254
  769.9 104.2 %collective-permute-start.45 = (bf16[512,1280]{1,0:T(8,128)(2,1)}, bf16[512,1280]{1,0:T(8,128)(2,1)}, u32[]{:S(2)}, u32[]{:S(2)}) collective-permute-start(bf16[512,1280]{1,0:T(8,128)(2,1)} %convolution_convert_fusion.13), channel_id=1, source_target_pairs={{0,1},{1,0},{2,3},{3,2},{4,5},{5,4},{6,7},{7,6},{8,9},{9,8},{10,11... | collective-permute-start | bytes 3932168 | tf_op jit(solution)/shard_map/ppermute | solution.py:254
  774.0 104.3 %collective-permute-start.47 = (bf16[512,1280]{1,0:T(8,128)(2,1)}, bf16[512,1280]{1,0:T(8,128)(2,1)}, u32[]{:S(2)}, u32[]{:S(2)}) collective-permute-start(bf16[512,1280]{1,0:T(8,128)(2,1)} %convolution_convert_fusion.12), channel_id=1, source_target_pairs={{0,2},{1,3},{2,0},{3,1},{4,6},{5,7},{6,4},{7,5},{8,10},{9,11},{10,... | collective-permute-start | bytes 3932168 | tf_op jit(solution)/shard_map/ppermute | solution.py:254
  811.0 196.4 %reduce-scatter.13.cloned.1.call-start = ((), (), s32[]{:S(2)}) async-start(), calls=%async_computation.15 | async-start | bytes 3686400 | tf_op jit(solution)/shard_map/reduce_scatter | solution.py:431
  881.7 110.7 %collective-permute-start.48 = (bf16[256,1280]{1,0:T(8,128)(2,1)}, bf16[256,1280]{1,0:T(8,128)(2,1)}, u32[]{:S(2)}, u32[]{:S(2)}) collective-permute-start(bf16[256,1280]{1,0:T(8,128)(2,1)} %add_convert_fusion.6), channel_id=1, source_target_pairs={{0,1},{1,0},{2,3},{3,2},{4,5},{5,4},{6,7},{7,6},{8,9},{9,8},{10,11... | collective-permute-start | bytes 1966088 | tf_op jit(solution)/shard_map/ppermute | solution.py:254
  926.8 19.2 %collective-permute-start.65 = (bf16[512,512]{0,1:T(8,128)(2,1)S(1)}, bf16[512,512]{0,1:T(8,128)(2,1)S(1)}, u32[]{:S(2)}, u32[]{:S(2)}) collective-permute-start(bf16[512,512]{0,1:T(8,128)(2,1)S(1)} %pad_maximum_fusion.19), channel_id=1, source_target_pairs={{0,1},{1,0},{2,3},{3,2},{4,5},{5,4},{6,7},{7,6},{8,9},{9,8},{10,11... | collective-permute-start | bytes 1572872 | tf_op jit(solution)/shard_map/ppermute | solution.py:254
  928.6 19.0 %collective-permute-start.63 = (bf16[512,544]{0,1:T(8,128)(2,1)S(1)}, bf16[512,544]{0,1:T(8,128)(2,1)S(1)}, u32[]{:S(2)}, u32[]{:S(2)}) collective-permute-start(bf16[512,544]{0,1:T(8,128)(2,1)S(1)} %pad_maximum_fusion.16), channel_id=1, source_target_pairs={{0,2},{1,3},{2,0},{3,1},{4,6},{5,7},{6,4},{7,5},{8,10},{9,11},{10,... | collective-permute-start | bytes 1671176 | tf_op jit(solution)/shard_map/ppermute | solution.py:254
  930.0 19.4 %collective-permute-start.67 = (bf16[512,544]{0,1:T(8,128)(2,1)S(1)}, bf16[512,544]{0,1:T(8,128)(2,1)S(1)}, u32[]{:S(2)}, u32[]{:S(2)}) collective-permute-start(bf16[512,544]{0,1:T(8,128)(2,1)S(1)} %pad_maximum_fusion.17), channel_id=1, source_target_pairs={{0,2},{1,3},{2,0},{3,1},{4,6},{5,7},{6,4},{7,5},{8,10},{9,11},{10,... | collective-permute-start | bytes 1671176 | tf_op jit(solution)/shard_map/ppermute | solution.py:254
  959.9 92.2 %reduce-scatter.15.cloned.1.call-start = ((), (), s32[]{:S(2)}) async-start(), calls=%async_computation.16 | async-start | bytes 2949120 | tf_op jit(solution)/shard_map/reduce_scatter | solution.py:431
  992.4 23.0 %collective-permute-start.69 = (bf16[4,4,80,1152]{3,2,1,0:T(8,128)(2,1)}, bf16[4,4,80,1152]{3,2,1,0:T(8,128)(2,1)}, u32[]{:S(2)}, u32[]{:S(2)}) collective-permute-start(bf16[4,4,80,1152]{3,2,1,0:T(8,128)(2,1)} %dynamic-slice_bitcast_fusion), channel_id=1, source_target_pairs={{0,4},{4,0},{1,5},{5,1},{2,6},{6,2},{3,7},{7,3},{8,12},{12,8},{9,1... | collective-permute-start | bytes 8847368 | tf_op jit(solution)/shard_map/ppermute | solution.py:346
  1007.4 68.6 %reduce-scatter.17.cloned.1.call-start = ((), (), s32[]{:S(2)}) async-start(), calls=%async_computation.17 | async-start | bytes 921600 | tf_op jit(solution)/shard_map/reduce_scatter | solution.py:392
  1019.2 17.1 %collective-permute-start.70 = (bf16[640,512]{1,0:T(8,128)(2,1)S(1)}, bf16[640,512]{1,0:T(8,128)(2,1)S(1)}, u32[]{:S(2)}, u32[]{:S(2)}) collective-permute-start(bf16[640,512]{1,0:T(8,128)(2,1)S(1)} %pad_maximum_fusion.15), channel_id=1, source_target_pairs={{0,1},{1,0},{2,3},{3,2},{4,5},{5,4},{6,7},{7,6},{8,9},{9,8},{10,11... | collective-permute-start | bytes 1966088 | tf_op jit(solution)/shard_map/ppermute | solution.py:254
  1019.5 21.1 %collective-permute-start.72 = (bf16[640,640]{1,0:T(8,128)(2,1)S(1)}, bf16[640,640]{1,0:T(8,128)(2,1)S(1)}, u32[]{:S(2)}, u32[]{:S(2)}) collective-permute-start(bf16[640,640]{1,0:T(8,128)(2,1)S(1)} %pad_maximum_fusion.12), channel_id=1, source_target_pairs={{0,2},{1,3},{2,0},{3,1},{4,6},{5,7},{6,4},{7,5},{8,10},{9,11},{10,... | collective-permute-start | bytes 2457608 | tf_op jit(solution)/shard_map/ppermute | solution.py:254
  (180 other events, 1626.3 us)
Sparse Core Ops, SparseCore 0:
  12.2 27.2 all-gather.8
  41.7 36.8 all-gather.6
  80.3 38.3 all-gather.10
  120.2 81.9 all-gather.14
  203.7 81.6 all-gather.12
  286.9 81.6 all-gather.16
  536.2 89.3 reduce-scatter.6
  631.1 89.3 reduce-scatter.8
  811.1 91.1 reduce-scatter.10
  960.0 41.2 reduce-scatter.12
  1007.5 37.6 reduce-scatter.14
  1052.3 23.7 reduce-scatter.16

commit v3 on v2

--- a/solution.py
+++ b/solution.py
@@ -589,7 +589,7 @@
     gate_part = weight_grad(both("hidden"), both("grad_gate"))
     gate_grad = scatter_dp(after(gate_part, down_grad))
     up_part = weight_grad(both("hidden"), both("grad_up"))
-    up_grad = scatter_dp(after(up_part, gate_grad))
+    up_grad = scatter_dp(up_part)
 
     for micro in micros:
         st = state[micro]

time: 1100 us -> 1100 us (level)
  local copies, waits for them, and re-layouts: 99.4 us -> 112 us
    unnamed x336 -> x330, local copies, waits for them, and re-layouts: 33.2 us -> 38.4 us
  transfers between devices with their start and end apart: 86 -> 86, of which waited for: 41 -> 40; matrix products, arithmetic and copies ran while one was open for 42% -> 43% of each run, Pallas kernels for 15% -> 14%
where the time goes in v3:
time: 1100 us; the launch traced here: 1090 us
  matrix products  317 us (29%)
  waiting for transfers between devices  297 us (27%)
  Pallas kernels  183 us (17%)
  local copies, waits for them, and re-layouts  112 us (10%)
  other arithmetic  84.7 us (8%)
  starting transfers between devices  80.1 us (7%)
  between operations  17.3 us (2%)
    dot_general x73, matrix products, dot(): lax.dot_general(left_side, right_side, (((left_dim,), (right_dim,)), ((),...  317 us
    ppermute x72, waiting for transfers between devices, swap(): lax.ppermute(values, 'tensor', [(index, index ^ bit) for index in range(4)])  258 us
    ppermute x72, starting transfers between devices, swap(): lax.ppermute(values, 'tensor', [(index, index ^ bit) for index in range(4)])  79.1 us
    pallas_call x3, Pallas kernels, weight_grad(): pl.pallas_call(weight_grad_kernel, grid=(rows // tile,), in_specs=[pl.Blo...  75 us
    pallas_call x2, Pallas kernels, attend_back(): pl.pallas_call(attend_back_kernel, grid=(heads,), in_specs=[pl.BlockSpec(...  60.9 us
    pallas_call x2, Pallas kernels, attend(): pl.pallas_call(attend_kernel, grid=(heads,), in_specs=[pl.BlockSpec(memor...  47.2 us
    unnamed x330, local copies, waits for them, and re-layouts  38.4 us
    all_gather x1, waiting for transfers between devices, gather_everywhere(): own = lax.all_gather(values, DP, axis=0, tiled=True)  23.6 us
  transfers between devices with their start and end apart: 86, of which 40 were waited for; matrix products, arithmetic and copies ran while one was open for 43% of the time, Pallas kernels for 14%

profile of v3, /device:TPU:0, one launch (start us, length us, event | category | flops | bytes accessed | tf_op | source)
XLA Modules:
  0.0 1091.3 jit_solution(12931776504870964157)
XLA Ops:
  15.9 23.6 %all-gather.9.cloned.1.call-done = bf16[640,1152]{1,0:T(8,128)(2,1)} async-done(((bf16[80,1152]{1,0:T(8,128)(2,1)}), bf16[640,1152]{1,0:T(8,128)(2,1)}) %all-gather.9.cloned.1.call-update) | async-done | bytes 1474576 | tf_op jit(solution)/shard_map/all_gather | solution.py:353
  44.6 15.6 %collective-permute-done.1 = bf16[320,1152]{1,0:T(8,128)(2,1)S(1)} collective-permute-done((bf16[320,1152]{1,0:T(8,128)(2,1)S(1)}, bf16[320,1152]{1,0:T(8,128)(2,1)S(1)}, u32[]{:S(2)}, u32[]{:S(2)}) %collective-permute-start.1) | collective-permute-done | bytes 737312 | tf_op jit(solution)/shard_map/ppermute | solution.py:254
  64.3 6.0 collective-permute-done.2
  100.5 6.5 collective-permute-done.18
  111.5 7.0 collective-permute-done.6
  142.7 23.4 %attend.3 = (bf16[10,64,1024]{2,1,0:T(8,128)(2,1)S(1)}, f32[10,1,1024]{2,1,0:T(1,128)S(1)}) custom-call(s32[1]{0:T(128)} %bitcast.28.prefix_ref, bf16[10,96,1024]{2,1,0:T(8,128)(2,1)S(1)} %pad_maximum_fusion.6.query_ref, bf16[10,128,1024]{2,1,0:T(8,128)(2,1)S(1)} %bitcast.190, bf16[32,1024]{1,0:T(8,128)(2,1)S(1)} %slice_bitcast_fusion.rope_ref), custom_call_target="tpu_custom_call" | custom-call | flops 8053063680 | bytes 6144000 | tf_op jit(solution)/shard_map/attend/pallas_call | solution.py:110
  168.2 4.1 convolution_convert_fusion.7
  176.4 23.8 %attend.2 = (bf16[10,64,1024]{2,1,0:T(8,128)(2,1)S(1)}, f32[10,1,1024]{2,1,0:T(1,128)S(1)}) custom-call(s32[1]{0:T(128)} %bitcast.prefix_ref, bf16[10,96,1024]{2,1,0:T(8,128)(2,1)S(1)} %pad_maximum_fusion.5.query_ref, bf16[10,128,1024]{2,1,0:T(8,128)(2,1)S(1)} %bitcast.188, bf16[32,1024]{1,0:T(8,128)(2,1)S(1)} %slice_bitcast_fusion.1.rope_ref), custom_call_target="tpu_custom_call" | custom-call | flops 8053063680 | bytes 6144000 | tf_op jit(solution)/shard_map/attend/pallas_call | solution.py:110
  223.1 11.7 %collective-permute-done.9 = bf16[512,1280]{1,0:T(8,128)(2,1)} collective-permute-done((bf16[512,1280]{1,0:T(8,128)(2,1)}, bf16[512,1280]{1,0:T(8,128)(2,1)}, u32[]{:S(2)}, u32[]{:S(2)}) %collective-permute-start.9) | collective-permute-done | bytes 1310752 | tf_op jit(solution)/shard_map/ppermute | solution.py:254
  241.4 21.4 %collective-permute-done.33 = bf16[256,2560]{1,0:T(8,128)(2,1)S(1)} collective-permute-done((bf16[256,2560]{1,0:T(8,128)(2,1)}, bf16[256,2560]{1,0:T(8,128)(2,1)S(1)}, u32[]{:S(2)}, u32[]{:S(2)}) %collective-permute-start.33) | collective-permute-done | bytes 1310752 | tf_op jit(solution)/shard_map/ppermute | solution.py:254
  267.3 12.8 %collective-permute-done.22 = bf16[256,1280]{1,0:T(8,128)(2,1)S(1)} collective-permute-done((bf16[256,1280]{1,0:T(8,128)(2,1)S(1)}, bf16[256,1280]{1,0:T(8,128)(2,1)S(1)}, u32[]{:S(2)}, u32[]{:S(2)}) %collective-permute-start.22) | collective-permute-done | bytes 655392 | tf_op jit(solution)/shard_map/ppermute | solution.py:254
  284.6 9.5 collective-permute-done.10
  308.3 27.9 %collective-permute-done.30 = bf16[256,2560]{1,0:T(8,128)(2,1)S(1)} collective-permute-done((bf16[256,2560]{1,0:T(8,128)(2,1)S(1)}, bf16[256,2560]{1,0:T(8,128)(2,1)S(1)}, u32[]{:S(2)}, u32[]{:S(2)}) %collective-permute-start.30) | collective-permute-done | bytes 1310752 | tf_op jit(solution)/shard_map/ppermute | solution.py:254
  340.5 23.9 %collective-permute-done.14 = bf16[256,2560]{1,0:T(8,128)(2,1)S(1)} collective-permute-done((bf16[256,2560]{1,0:T(8,128)(2,1)S(1)}, bf16[256,2560]{1,0:T(8,128)(2,1)S(1)}, u32[]{:S(2)}, u32[]{:S(2)}) %collective-permute-start.14) | collective-permute-done | bytes 1310752 | tf_op jit(solution)/shard_map/ppermute | solution.py:254
  368.4 16.6 %collective-permute-done.15 = bf16[128,2560]{1,0:T(8,128)(2,1)S(1)} collective-permute-done((bf16[128,2560]{1,0:T(8,128)(2,1)S(1)}, bf16[128,2560]{1,0:T(8,128)(2,1)S(1)}, u32[]{:S(2)}, u32[]{:S(2)}) %collective-permute-start.15) | collective-permute-done | bytes 655392 | tf_op jit(solution)/shard_map/ppermute | solution.py:254
  397.6 15.3 %convolution_convert_fusion.2 = bf16[1024,1600]{1,0:T(8,128)(2,1)} fusion(bf16[1024,2560]{1,0:T(8,128)(2,1)} %constant_dynamic-update-slice_fusion.5.refs_1_.refs_0_, bf16[2560,1600]{1,0:T(8,128)(2,1)} %all-gather.15.cloned.1.call-done), kind=kOutput, calls=%fused_computation.47 | convolution fusion | flops 8390246400 | bytes 16711680 | tf_op jit(solution)/shard_map/dot_general | solution.py:34
  412.8 15.2 %convolution_convert_fusion.3 = bf16[1024,1600]{1,0:T(8,128)(2,1)} fusion(bf16[1024,2560]{1,0:T(8,128)(2,1)} %constant_dynamic-update-slice_fusion.5.refs_1_.refs_0_, bf16[2560,1600]{1,0:T(8,128)(2,1)} %all-gather.13.cloned.1.call-done), kind=kOutput, calls=%fused_computation.48 | convolution fusion | flops 8390246400 | bytes 16711680 | tf_op jit(solution)/shard_map/dot_general | solution.py:34
  428.0 20.5 %fusion.14 = (bf16[1024,1600]{1,0:T(8,128)(2,1)}, bf16[1024,1600]{1,0:T(8,128)(2,1)}, bf16[1024,1600]{1,0:T(8,128)(2,1)}) fusion(bf16[1024,1600]{1,0:T(8,128)(2,1)} %convolution_convert_fusion.3, bf16[1024,1600]{1,0:T(8,128)(2,1)} %convolution_convert_fusion.2, bf16[1024,2560]{1,0:T(8,128)(2,1)} %copy-done.76, ...), kind=kOutput, calls=%fused_computation.27 | convolution fusion | flops 8418099200 | bytes 29818880 | tf_op jit(solution)/shard_map/dot_general | solution.py:34
  450.9 15.4 %convolution_convert_fusion = bf16[1024,1600]{1,0:T(8,128)(2,1)} fusion(bf16[1024,2560]{1,0:T(8,128)(2,1)} %constant_dynamic-update-slice_fusion.15.refs_1_, bf16[2560,1600]{1,0:T(8,128)(2,1)} %all-gather.15.cloned.1.call-done), kind=kOutput, calls=%fused_computation.45 | convolution fusion | flops 8390246400 | bytes 16711680 | tf_op jit(solution)/shard_map/dot_general | solution.py:34
  466.3 14.5 %convolution_convert_fusion.1 = bf16[1024,1600]{1,0:T(8,128)(2,1)} fusion(bf16[1024,2560]{1,0:T(8,128)(2,1)S(1)} %bitcast.253, bf16[2560,1600]{1,0:T(8,128)(2,1)} %all-gather.13.cloned.1.call-done), kind=kOutput, calls=%fused_computation.46 | convolution fusion | flops 8390246400 | bytes 16711680 | tf_op jit(solution)/shard_map/dot_general | solution.py:34
  484.6 8.7 collective-permute-done.28
  494.8 16.3 %fusion.20 = (bf16[1024,1600]{1,0:T(8,128)(2,1)}, bf16[1024,1600]{1,0:T(8,128)(2,1)}, bf16[1024,1600]{1,0:T(8,128)(2,1)}) fusion(bf16[1024,1600]{1,0:T(8,128)(2,1)} %convolution_convert_fusion.1, bf16[1024,1600]{1,0:T(8,128)(2,1)} %convolution_convert_fusion, bf16[1024,2560]{1,0:T(8,128)(2,1)S(1)} %constant_dynamic-update-slice_fusion.10.refs_1_, ...), kind=kOutput, calls=%fused_computation.33 | convolution fusion | flops 8418099200 | bytes 29818880 | tf_op jit(solution)/shard_map/dot_general | solution.py:34
  511.1 25.0 %weight_grad.3 = bf16[2560,1600]{1,0:T(8,128)(2,1)} custom-call(bf16[1024,2560]{1,0:T(8,128)(2,1)} %copy-done.76, bf16[1024,2560]{1,0:T(8,128)(2,1)} %copy-done.77, bf16[1024,1600]{1,0:T(8,128)(2,1)} %get-tuple-element.82.refs_2_, bf16[1024,1600]{1,0:T(8,128)(2,1)} %get-tuple-element.83.refs_3_), custom_call_target="tpu_custom_call" | custom-call | flops 16777216000 | bytes 25231360 | tf_op jit(solution)/shard_map/weight_grad/pallas_call | solution.py:236
  537.9 5.5 fusion.93
  543.4 6.4 fusion.22
  553.6 3.7 fusion.23
  558.2 4.2 fusion.87
  562.4 4.2 fusion.24
  568.2 25.0 %weight_grad.5 = bf16[2560,1600]{1,0:T(8,128)(2,1)} custom-call(bf16[1024,2560]{1,0:T(8,128)(2,1)} %constant_dynamic-update-slice_fusion.5.refs_1_.refs_0_, bf16[1024,2560]{1,0:T(8,128)(2,1)} %constant_dynamic-update-slice_fusion.15.refs_1_, bf16[1024,1600]{1,0:T(8,128)(2,1)} %get-tuple-element.85.refs_2_, bf16[1024,1600]{1,0:T(8,128)(2,1)} %get-tuple-element.81.refs_3_), custom_call_target="tpu_custom_call" | custom-call | flops 16777216000 | bytes 25231360 | tf_op jit(solution)/shard_map/weight_grad/pallas_call | solution.py:236
  593.3 5.5 fusion.69
  598.9 5.1 fusion.25
  621.8 3.7 fusion.73
  625.6 3.7 fusion.85
  646.7 4.7 collective-permute-done.38
  658.7 3.9 collective-permute-done.56
  681.4 25.0 %weight_grad.4 = bf16[2560,1600]{1,0:T(8,128)(2,1)} custom-call(bf16[1024,2560]{1,0:T(8,128)(2,1)} %constant_dynamic-update-slice_fusion.5.refs_1_.refs_0_, bf16[1024,2560]{1,0:T(8,128)(2,1)} %constant_dynamic-update-slice_fusion.15.refs_1_, bf16[1024,1600]{1,0:T(8,128)(2,1)} %get-tuple-element.84.refs_2_, bf16[1024,1600]{1,0:T(8,128)(2,1)} %get-tuple-element.80.refs_3_), custom_call_target="tpu_custom_call" | custom-call | flops 16777216000 | bytes 25231360 | tf_op jit(solution)/shard_map/weight_grad/pallas_call | solution.py:236
  708.8 22.9 %collective-permute-done.58 = bf16[256,2560]{1,0:T(8,128)(2,1)} collective-permute-done((bf16[256,2560]{1,0:T(8,128)(2,1)}, bf16[256,2560]{1,0:T(8,128)(2,1)}, u32[]{:S(2)}, u32[]{:S(2)}) %collective-permute-start.58) | collective-permute-done | bytes 1310752 | tf_op jit(solution)/shard_map/ppermute | solution.py:254
  752.7 6.0 convolution_convert_fusion.11
  760.1 5.9 convolution_convert_fusion.10
  767.1 3.7 convolution_convert_fusion.13
  771.3 3.7 convolution_convert_fusion.12
  776.4 6.5 convolution_convert_fusion.16
  783.0 30.5 %attend_back.3 = (bf16[10,96,1024]{2,1,0:T(8,128)(2,1)S(1)}, bf16[10,128,1024]{2,1,0:T(8,128)(2,1)S(1)}, f32[32,1024]{1,0:T(8,128)S(1)}) custom-call(s32[1]{0:T(128)} %bitcast.28.prefix_ref, bf16[10,96,1024]{2,1,0:T(8,128)(2,1)S(1)} %copy-done.13, bf16[10,128,1024]{2,1,0:T(8,128)(2,1)S(1)} %bitcast.191, bf16[32,1024]{1,0:T(8,128)(2,1)S(1)} %copy-done.19, ...), custom_call_target="tpu_custom_call" | custom-call | flops 20132659200 | bytes 11264000 | tf_op jit(solution)/shard_map/attend_back/pallas_call | solution.py:188
  816.8 4.9 fusion.54
  824.3 3.8 fusion.59
  831.1 6.7 fusion.237
  837.8 7.4 convolution_convert_fusion.17
  845.2 8.5 add_convert_fusion
  858.5 4.8 fusion.49
  866.5 3.8 add_convert_fusion.5
  900.4 30.4 %attend_back.2 = (bf16[10,96,1024]{2,1,0:T(8,128)(2,1)S(1)}, bf16[10,128,1024]{2,1,0:T(8,128)(2,1)S(1)}, f32[32,1024]{1,0:T(8,128)S(1)}) custom-call(s32[1]{0:T(128)} %bitcast.prefix_ref, bf16[10,96,1024]{2,1,0:T(8,128)(2,1)S(1)} %copy-done.11, bf16[10,128,1024]{2,1,0:T(8,128)(2,1)S(1)} %bitcast.189, bf16[32,1024]{1,0:T(8,128)(2,1)S(1)} %copy-done.17, ...), custom_call_target="tpu_custom_call" | custom-call | flops 20132659200 | bytes 11264000 | tf_op jit(solution)/shard_map/attend_back/pallas_call | solution.py:188
  938.8 6.4 collective-permute-done.61
  945.7 8.1 collective-permute-done.65
  973.8 10.1 multiply_reduce_fusion
  985.5 6.2 fusion
  998.8 4.3 add_convert_fusion.1
  1012.8 5.1 fusion.27
  1019.6 3.5 fusion.21
  1031.0 9.4 collective-permute-done.70
  1041.6 4.1 collective-permute-done.72
  1046.9 3.7 subtract_multiply_fusion
  1051.9 3.7 collective-permute-done.73
  1056.9 4.3 fusion.35
  1065.3 12.6 %reduce-scatter.17.cloned.1.call-done = bf16[80,1152]{1,0:T(8,128)(2,1)} async-done(((bf16[320,1152]{1,0:T(8,128)(2,1)}), bf16[80,1152]{1,0:T(8,128)(2,1)}) %reduce-scatter.17.cloned.1.call-update) | async-done | bytes 184336 | tf_op jit(solution)/shard_map/reduce_scatter | solution.py:392
  (732 shorter events, 377.7 us)
Async XLA Ops:
  7.2 32.3 %all-gather.9.cloned.1.call-start = ((), (), s32[]{:S(2)}) async-start(), calls=%async_computation.7 | async-start | bytes 1658880 | tf_op jit(solution)/shard_map/all_gather | solution.py:353
  12.1 83.0 %all-gather.7.cloned.1.call-start = ((), (), s32[]{:S(2)}) async-start(), calls=%async_computation.6 | async-start | bytes 2949120 | tf_op jit(solution)/shard_map/all_gather | solution.py:428
  13.9 154.3 %all-gather.11.cloned.1.call-start = ((), (), s32[]{:S(2)}) async-start(), calls=%async_computation.8 | async-start | bytes 3686400 | tf_op jit(solution)/shard_map/all_gather | solution.py:428
  14.7 382.9 %all-gather.15.cloned.1.call-start = ((), (), s32[]{:S(2)}) async-start(), calls=%async_computation.10 | async-start | bytes 9584640 | tf_op jit(solution)/shard_map/all_gather | solution.py:428
  15.2 397.6 %all-gather.13.cloned.1.call-start = ((), (), s32[]{:S(2)}) async-start(), calls=%async_computation.9 | async-start | bytes 9584640 | tf_op jit(solution)/shard_map/all_gather | solution.py:428
  15.8 412.2 %all-gather.17.cloned.1.call-start = ((), (), s32[]{:S(2)}) async-start(), calls=%async_computation.11 | async-start | bytes 9584640 | tf_op jit(solution)/shard_map/all_gather | solution.py:428
  41.6 18.6 %collective-permute-start.1 = (bf16[320,1152]{1,0:T(8,128)(2,1)S(1)}, bf16[320,1152]{1,0:T(8,128)(2,1)S(1)}, u32[]{:S(2)}, u32[]{:S(2)}) collective-permute-start(bf16[320,1152]{1,0:T(8,128)(2,1)S(1)} %get-tuple-element.132), channel_id=1, source_target_pairs={{0,2},{1,3},{2,0},{3,1},{4,6},{5,7},{6,4},{7,5},{8,10},{9,11},{10,... | collective-permute-start | bytes 2211848 | tf_op jit(solution)/shard_map/ppermute | solution.py:254
  43.1 18.7 %collective-permute-start = (bf16[320,1152]{1,0:T(8,128)(2,1)S(1)}, bf16[320,1152]{1,0:T(8,128)(2,1)S(1)}, u32[]{:S(2)}, u32[]{:S(2)}) collective-permute-start(bf16[320,1152]{1,0:T(8,128)(2,1)S(1)} %get-tuple-element.132), channel_id=1, source_target_pairs={{0,1},{1,0},{2,3},{3,2},{4,5},{5,4},{6,7},{7,6},{8,9},{9,8},{10,11... | collective-permute-start | bytes 2211848 | tf_op jit(solution)/shard_map/ppermute | solution.py:254
  44.5 700.6 %reduce-scatter.7.cloned.1.call-start = ((), (), s32[]{:S(2)}) async-start(), calls=%async_computation.12 | async-start | bytes 9584640 | tf_op jit(solution)/shard_map/reduce_scatter | solution.py:431
  90.4 18.5 %collective-permute-start.17 = (bf16[256,1056]{0,1:T(8,128)(2,1)}, bf16[256,1056]{0,1:T(8,128)(2,1)}, u32[]{:S(2)}, u32[]{:S(2)}) collective-permute-start(bf16[256,1056]{0,1:T(8,128)(2,1)} %get-tuple-element.176), channel_id=1, source_target_pairs={{0,1},{1,0},{2,3},{3,2},{4,5},{5,4},{6,7},{7,6},{8,9},{9,8},{10,11... | collective-permute-start | bytes 1622024 | tf_op jit(solution)/shard_map/ppermute | solution.py:254
  92.9 27.7 %collective-permute-start.5 = (bf16[256,1056]{0,1:T(8,128)(2,1)}, bf16[256,1056]{0,1:T(8,128)(2,1)}, u32[]{:S(2)}, u32[]{:S(2)}) collective-permute-start(bf16[256,1056]{0,1:T(8,128)(2,1)} %get-tuple-element.174), channel_id=1, source_target_pairs={{0,1},{1,0},{2,3},{3,2},{4,5},{5,4},{6,7},{7,6},{8,9},{9,8},{10,11... | collective-permute-start | bytes 1622024 | tf_op jit(solution)/shard_map/ppermute | solution.py:254
  93.9 24.6 %collective-permute-start.6 = (bf16[256,1056]{0,1:T(8,128)(2,1)}, bf16[256,1056]{0,1:T(8,128)(2,1)}, u32[]{:S(2)}, u32[]{:S(2)}) collective-permute-start(bf16[256,1056]{0,1:T(8,128)(2,1)} %get-tuple-element.174), channel_id=1, source_target_pairs={{0,2},{1,3},{2,0},{3,1},{4,6},{5,7},{6,4},{7,5},{8,10},{9,11},{10,... | collective-permute-start | bytes 1622024 | tf_op jit(solution)/shard_map/ppermute | solution.py:254
  107.9 21.4 %collective-permute-start.19 = (bf16[128,1056]{0,1:T(8,128)(2,1)S(1)}, bf16[128,1056]{0,1:T(8,128)(2,1)S(1)}, u32[]{:S(2)}, u32[]{:S(2)}) collective-permute-start(bf16[128,1056]{0,1:T(8,128)(2,1)S(1)} %slice.716), channel_id=1, source_target_pairs={{0,1},{1,0},{2,3},{3,2},{4,5},{5,4},{6,7},{7,6},{8,9},{9,8},{10,11... | collective-permute-start | bytes 811016 | tf_op jit(solution)/shard_map/ppermute | solution.py:254
  110.0 19.4 %collective-permute-start.20 = (bf16[128,1056]{0,1:T(8,128)(2,1)S(1)}, bf16[128,1056]{0,1:T(8,128)(2,1)S(1)}, u32[]{:S(2)}, u32[]{:S(2)}) collective-permute-start(bf16[128,1056]{0,1:T(8,128)(2,1)S(1)} %slice.717), channel_id=1, source_target_pairs={{0,2},{1,3},{2,0},{3,1},{4,6},{5,7},{6,4},{7,5},{8,10},{9,11},{10,... | collective-permute-start | bytes 811016 | tf_op jit(solution)/shard_map/ppermute | solution.py:254
  172.3 44.1 %collective-permute-start.21 = (bf16[512,1280]{1,0:T(8,128)(2,1)}, bf16[512,1280]{1,0:T(8,128)(2,1)}, u32[]{:S(2)}, u32[]{:S(2)}) collective-permute-start(bf16[512,1280]{1,0:T(8,128)(2,1)} %convolution_convert_fusion.7), channel_id=1, source_target_pairs={{0,1},{1,0},{2,3},{3,2},{4,5},{5,4},{6,7},{7,6},{8,9},{9,8},{10,11... | collective-permute-start | bytes 3932168 | tf_op jit(solution)/shard_map/ppermute | solution.py:254
  175.6 44.4 %collective-permute-start.23 = (bf16[512,1280]{1,0:T(8,128)(2,1)}, bf16[512,1280]{1,0:T(8,128)(2,1)}, u32[]{:S(2)}, u32[]{:S(2)}) collective-permute-start(bf16[512,1280]{1,0:T(8,128)(2,1)} %convolution_convert_fusion.6), channel_id=1, source_target_pairs={{0,2},{1,3},{2,0},{3,1},{4,6},{5,7},{6,4},{7,5},{8,10},{9,11},{10,... | collective-permute-start | bytes 3932168 | tf_op jit(solution)/shard_map/ppermute | solution.py:254
  202.8 32.0 %collective-permute-start.9 = (bf16[512,1280]{1,0:T(8,128)(2,1)}, bf16[512,1280]{1,0:T(8,128)(2,1)}, u32[]{:S(2)}, u32[]{:S(2)}) collective-permute-start(bf16[512,1280]{1,0:T(8,128)(2,1)} %convolution_convert_fusion.9), channel_id=1, source_target_pairs={{0,1},{1,0},{2,3},{3,2},{4,5},{5,4},{6,7},{7,6},{8,9},{9,8},{10,11... | collective-permute-start | bytes 3932168 | tf_op jit(solution)/shard_map/ppermute | solution.py:254
  206.0 32.0 %collective-permute-start.11 = (bf16[512,1280]{1,0:T(8,128)(2,1)}, bf16[512,1280]{1,0:T(8,128)(2,1)}, u32[]{:S(2)}, u32[]{:S(2)}) collective-permute-start(bf16[512,1280]{1,0:T(8,128)(2,1)} %convolution_convert_fusion.8), channel_id=1, source_target_pairs={{0,2},{1,3},{2,0},{3,1},{4,6},{5,7},{6,4},{7,5},{8,10},{9,11},{10,... | collective-permute-start | bytes 3932168 | tf_op jit(solution)/shard_map/ppermute | solution.py:254
  209.1 53.7 %collective-permute-start.33 = (bf16[256,2560]{1,0:T(8,128)(2,1)}, bf16[256,2560]{1,0:T(8,128)(2,1)S(1)}, u32[]{:S(2)}, u32[]{:S(2)}) collective-permute-start(bf16[256,2560]{1,0:T(8,128)(2,1)} %tie.3), channel_id=1, source_target_pairs={{0,1},{1,0},{2,3},{3,2},{4,5},{5,4},{6,7},{7,6},{8,9},{9,8},{10,11... | collective-permute-start | bytes 3932168 | tf_op jit(solution)/shard_map/ppermute | solution.py:254
  216.4 49.6 %collective-permute-start.34 = (bf16[256,2560]{1,0:T(8,128)(2,1)S(1)}, bf16[256,2560]{1,0:T(8,128)(2,1)S(1)}, u32[]{:S(2)}, u32[]{:S(2)}) collective-permute-start(bf16[256,2560]{1,0:T(8,128)(2,1)S(1)} %copy-done.43), channel_id=1, source_target_pairs={{0,2},{1,3},{2,0},{3,1},{4,6},{5,7},{6,4},{7,5},{8,10},{9,11},{10,... | collective-permute-start | bytes 3932168 | tf_op jit(solution)/shard_map/ppermute | solution.py:254
  220.0 60.1 %collective-permute-start.22 = (bf16[256,1280]{1,0:T(8,128)(2,1)S(1)}, bf16[256,1280]{1,0:T(8,128)(2,1)S(1)}, u32[]{:S(2)}, u32[]{:S(2)}) collective-permute-start(bf16[256,1280]{1,0:T(8,128)(2,1)S(1)} %add_convert_fusion.11), channel_id=1, source_target_pairs={{0,2},{1,3},{2,0},{3,1},{4,6},{5,7},{6,4},{7,5},{8,10},{9,11},{10,... | collective-permute-start | bytes 1966088 | tf_op jit(solution)/shard_map/ppermute | solution.py:254
  234.8 48.1 %collective-permute-start.24 = (bf16[256,1280]{1,0:T(8,128)(2,1)S(1)}, bf16[256,1280]{1,0:T(8,128)(2,1)S(1)}, u32[]{:S(2)}, u32[]{:S(2)}) collective-permute-start(bf16[256,1280]{1,0:T(8,128)(2,1)S(1)} %add_convert_fusion.10), channel_id=1, source_target_pairs={{0,1},{1,0},{2,3},{3,2},{4,5},{5,4},{6,7},{7,6},{8,9},{9,8},{10,11... | collective-permute-start | bytes 1966088 | tf_op jit(solution)/shard_map/ppermute | solution.py:254
  238.1 56.1 %collective-permute-start.10 = (bf16[256,1280]{1,0:T(8,128)(2,1)S(1)}, bf16[256,1280]{1,0:T(8,128)(2,1)S(1)}, u32[]{:S(2)}, u32[]{:S(2)}) collective-permute-start(bf16[256,1280]{1,0:T(8,128)(2,1)S(1)} %add_convert_fusion.13), channel_id=1, source_target_pairs={{0,2},{1,3},{2,0},{3,1},{4,6},{5,7},{6,4},{7,5},{8,10},{9,11},{10,... | collective-permute-start | bytes 1966088 | tf_op jit(solution)/shard_map/ppermute | solution.py:254
  262.8 32.8 %collective-permute-start.12 = (bf16[256,1280]{1,0:T(8,128)(2,1)S(1)}, bf16[256,1280]{1,0:T(8,128)(2,1)S(1)}, u32[]{:S(2)}, u32[]{:S(2)}) collective-permute-start(bf16[256,1280]{1,0:T(8,128)(2,1)S(1)} %add_convert_fusion.12), channel_id=1, source_target_pairs={{0,1},{1,0},{2,3},{3,2},{4,5},{5,4},{6,7},{7,6},{8,9},{9,8},{10,11... | collective-permute-start | bytes 1966088 | tf_op jit(solution)/shard_map/ppermute | solution.py:254
  266.1 38.9 %collective-permute-start.35 = (bf16[128,2560]{1,0:T(8,128)(2,1)S(1)}, bf16[128,2560]{1,0:T(8,128)(2,1)S(1)}, u32[]{:S(2)}, u32[]{:S(2)}) collective-permute-start(bf16[128,2560]{1,0:T(8,128)(2,1)S(1)} %slice.590), channel_id=1, source_target_pairs={{0,1},{1,0},{2,3},{3,2},{4,5},{5,4},{6,7},{7,6},{8,9},{9,8},{10,11... | collective-permute-start | bytes 1966088 | tf_op jit(solution)/shard_map/ppermute | solution.py:254
  280.1 28.1 %collective-permute-start.36 = (bf16[128,2560]{1,0:T(8,128)(2,1)S(1)}, bf16[128,2560]{1,0:T(8,128)(2,1)S(1)}, u32[]{:S(2)}, u32[]{:S(2)}) collective-permute-start(bf16[128,2560]{1,0:T(8,128)(2,1)S(1)} %slice.591), channel_id=1, source_target_pairs={{0,2},{1,3},{2,0},{3,1},{4,6},{5,7},{6,4},{7,5},{8,10},{9,11},{10,... | collective-permute-start | bytes 1966088 | tf_op jit(solution)/shard_map/ppermute | solution.py:254
  301.4 36.8 %collective-permute-start.29 = (bf16[256,2560]{1,0:T(8,128)(2,1)S(1)}, bf16[256,2560]{1,0:T(8,128)(2,1)S(1)}, u32[]{:S(2)}, u32[]{:S(2)}) collective-permute-start(bf16[256,2560]{1,0:T(8,128)(2,1)S(1)} %get-tuple-element.157), channel_id=1, source_target_pairs={{0,1},{1,0},{2,3},{3,2},{4,5},{5,4},{6,7},{7,6},{8,9},{9,8},{10,11... | collective-permute-start | bytes 3932168 | tf_op jit(solution)/shard_map/ppermute | solution.py:254
  302.5 33.7 %collective-permute-start.30 = (bf16[256,2560]{1,0:T(8,128)(2,1)S(1)}, bf16[256,2560]{1,0:T(8,128)(2,1)S(1)}, u32[]{:S(2)}, u32[]{:S(2)}) collective-permute-start(bf16[256,2560]{1,0:T(8,128)(2,1)S(1)} %get-tuple-element.157), channel_id=1, source_target_pairs={{0,2},{1,3},{2,0},{3,1},{4,6},{5,7},{6,4},{7,5},{8,10},{9,11},{10,... | collective-permute-start | bytes 3932168 | tf_op jit(solution)/shard_map/ppermute | solution.py:254
  303.9 61.6 %collective-permute-start.13 = (bf16[256,2560]{1,0:T(8,128)(2,1)S(1)}, bf16[256,2560]{1,0:T(8,128)(2,1)S(1)}, u32[]{:S(2)}, u32[]{:S(2)}) collective-permute-start(bf16[256,2560]{1,0:T(8,128)(2,1)S(1)} %get-tuple-element.128), channel_id=1, source_target_pairs={{0,1},{1,0},{2,3},{3,2},{4,5},{5,4},{6,7},{7,6},{8,9},{9,8},{10,11... | collective-permute-start | bytes 3932168 | tf_op jit(solution)/shard_map/ppermute | solution.py:254
  305.0 59.4 %collective-permute-start.14 = (bf16[256,2560]{1,0:T(8,128)(2,1)S(1)}, bf16[256,2560]{1,0:T(8,128)(2,1)S(1)}, u32[]{:S(2)}, u32[]{:S(2)}) collective-permute-start(bf16[256,2560]{1,0:T(8,128)(2,1)S(1)} %get-tuple-element.128), channel_id=1, source_target_pairs={{0,2},{1,3},{2,0},{3,1},{4,6},{5,7},{6,4},{7,5},{8,10},{9,11},{10,... | collective-permute-start | bytes 3932168 | tf_op jit(solution)/shard_map/ppermute | solution.py:254
  337.2 55.2 %collective-permute-start.31 = (bf16[128,2560]{1,0:T(8,128)(2,1)}, bf16[128,2560]{1,0:T(8,128)(2,1)S(1)}, u32[]{:S(2)}, u32[]{:S(2)}) collective-permute-start(bf16[128,2560]{1,0:T(8,128)(2,1)} %slice.726), channel_id=1, source_target_pairs={{0,1},{1,0},{2,3},{3,2},{4,5},{5,4},{6,7},{7,6},{8,9},{9,8},{10,11... | collective-permute-start | bytes 1966088 | tf_op jit(solution)/shard_map/ppermute | solution.py:254
  339.1 54.2 %collective-permute-start.32 = (bf16[128,2560]{1,0:T(8,128)(2,1)}, bf16[128,2560]{1,0:T(8,128)(2,1)}, u32[]{:S(2)}, u32[]{:S(2)}) collective-permute-start(bf16[128,2560]{1,0:T(8,128)(2,1)} %slice.727), channel_id=1, source_target_pairs={{0,2},{1,3},{2,0},{3,1},{4,6},{5,7},{6,4},{7,5},{8,10},{9,11},{10,... | collective-permute-start | bytes 1966088 | tf_op jit(solution)/shard_map/ppermute | solution.py:254
  364.4 20.6 %collective-permute-start.15 = (bf16[128,2560]{1,0:T(8,128)(2,1)S(1)}, bf16[128,2560]{1,0:T(8,128)(2,1)S(1)}, u32[]{:S(2)}, u32[]{:S(2)}) collective-permute-start(bf16[128,2560]{1,0:T(8,128)(2,1)S(1)} %slice.713), channel_id=1, source_target_pairs={{0,1},{1,0},{2,3},{3,2},{4,5},{5,4},{6,7},{7,6},{8,9},{9,8},{10,11... | collective-permute-start | bytes 1966088 | tf_op jit(solution)/shard_map/ppermute | solution.py:254
  365.6 22.7 %collective-permute-start.16 = (bf16[128,2560]{1,0:T(8,128)(2,1)S(1)}, bf16[128,2560]{1,0:T(8,128)(2,1)S(1)}, u32[]{:S(2)}, u32[]{:S(2)}) collective-permute-start(bf16[128,2560]{1,0:T(8,128)(2,1)S(1)} %slice.714), channel_id=1, source_target_pairs={{0,2},{1,3},{2,0},{3,1},{4,6},{5,7},{6,4},{7,5},{8,10},{9,11},{10,... | collective-permute-start | bytes 1966088 | tf_op jit(solution)/shard_map/ppermute | solution.py:254
  390.3 58.2 %collective-permute-start.25 = (bf16[256,2560]{1,0:T(8,128)(2,1)}, bf16[256,2560]{1,0:T(8,128)(2,1)}, u32[]{:S(2)}, u32[]{:S(2)}) collective-permute-start(bf16[256,2560]{1,0:T(8,128)(2,1)} %tie.2), channel_id=1, source_target_pairs={{0,1},{1,0},{2,3},{3,2},{4,5},{5,4},{6,7},{7,6},{8,9},{9,8},{10,11... | collective-permute-start | bytes 3932168 | tf_op jit(solution)/shard_map/ppermute | solution.py:254
  391.0 57.5 %collective-permute-start.26 = (bf16[256,2560]{1,0:T(8,128)(2,1)}, bf16[256,2560]{1,0:T(8,128)(2,1)}, u32[]{:S(2)}, u32[]{:S(2)}) collective-permute-start(bf16[256,2560]{1,0:T(8,128)(2,1)} %tie.2), channel_id=1, source_target_pairs={{0,2},{1,3},{2,0},{3,1},{4,6},{5,7},{6,4},{7,5},{8,10},{9,11},{10,... | collective-permute-start | bytes 3932168 | tf_op jit(solution)/shard_map/ppermute | solution.py:254
  449.9 34.6 %collective-permute-start.27 = (bf16[128,2560]{1,0:T(8,128)(2,1)S(1)}, bf16[128,2560]{1,0:T(8,128)(2,1)S(1)}, u32[]{:S(2)}, u32[]{:S(2)}) collective-permute-start(bf16[128,2560]{1,0:T(8,128)(2,1)S(1)} %slice.585), channel_id=1, source_target_pairs={{0,1},{1,0},{2,3},{3,2},{4,5},{5,4},{6,7},{7,6},{8,9},{9,8},{10,11... | collective-permute-start | bytes 1966088 | tf_op jit(solution)/shard_map/ppermute | solution.py:254
  536.1 357.6 %reduce-scatter.11.cloned.1.call-start = ((), (), s32[]{:S(2)}) async-start(), calls=%async_computation.14 | async-start | bytes 9584640 | tf_op jit(solution)/shard_map/reduce_scatter | solution.py:431
  549.8 82.2 %collective-permute-start.37 = (bf16[512,1280]{1,0:T(8,128)(2,1)}, bf16[512,1280]{1,0:T(8,128)(2,1)}, u32[]{:S(2)}, u32[]{:S(2)}) collective-permute-start(bf16[512,1280]{1,0:T(8,128)(2,1)} %fusion.22), channel_id=1, source_target_pairs={{0,1},{1,0},{2,3},{3,2},{4,5},{5,4},{6,7},{7,6},{8,9},{9,8},{10,11... | collective-permute-start | bytes 3932168 | tf_op jit(solution)/shard_map/ppermute | solution.py:254
  557.4 79.7 %collective-permute-start.39 = (bf16[512,1280]{1,0:T(8,128)(2,1)}, bf16[512,1280]{1,0:T(8,128)(2,1)S(1)}, u32[]{:S(2)}, u32[]{:S(2)}) collective-permute-start(bf16[512,1280]{1,0:T(8,128)(2,1)} %fusion.23), channel_id=1, source_target_pairs={{0,2},{1,3},{2,0},{3,1},{4,6},{5,7},{6,4},{7,5},{8,10},{9,11},{10,... | collective-permute-start | bytes 3932168 | tf_op jit(solution)/shard_map/ppermute | solution.py:254
  566.6 73.3 %collective-permute-start.53 = (bf16[512,1280]{1,0:T(8,128)(2,1)}, bf16[512,1280]{1,0:T(8,128)(2,1)S(1)}, u32[]{:S(2)}, u32[]{:S(2)}) collective-permute-start(bf16[512,1280]{1,0:T(8,128)(2,1)} %fusion.24), channel_id=1, source_target_pairs={{0,1},{1,0},{2,3},{3,2},{4,5},{5,4},{6,7},{7,6},{8,9},{9,8},{10,11... | collective-permute-start | bytes 3932168 | tf_op jit(solution)/shard_map/ppermute | solution.py:254
  593.2 300.5 %reduce-scatter.9.cloned.1.call-start = ((), (), s32[]{:S(2)}) async-start(), calls=%async_computation.13 | async-start | bytes 9584640 | tf_op jit(solution)/shard_map/reduce_scatter | solution.py:431
  604.0 39.3 %collective-permute-start.55 = (bf16[512,1280]{1,0:T(8,128)(2,1)S(1)}, bf16[512,1280]{1,0:T(8,128)(2,1)S(1)}, u32[]{:S(2)}, u32[]{:S(2)}) collective-permute-start(bf16[512,1280]{1,0:T(8,128)(2,1)S(1)} %fusion.25), channel_id=1, source_target_pairs={{0,2},{1,3},{2,0},{3,1},{4,6},{5,7},{6,4},{7,5},{8,10},{9,11},{10,... | collective-permute-start | bytes 3932168 | tf_op jit(solution)/shard_map/ppermute | solution.py:254
  641.7 16.8 %collective-permute-start.54 = (bf16[256,1280]{1,0:T(8,128)(2,1)S(1)}, bf16[256,1280]{1,0:T(8,128)(2,1)S(1)}, u32[]{:S(2)}, u32[]{:S(2)}) collective-permute-start(bf16[256,1280]{1,0:T(8,128)(2,1)S(1)} %add_convert_fusion.3), channel_id=1, source_target_pairs={{0,2},{1,3},{2,0},{3,1},{4,6},{5,7},{6,4},{7,5},{8,10},{9,11},{10,... | collective-permute-start | bytes 1966088 | tf_op jit(solution)/shard_map/ppermute | solution.py:254
  671.4 35.9 %collective-permute-start.41 = (bf16[256,2560]{1,0:T(8,128)(2,1)}, bf16[256,2560]{1,0:T(8,128)(2,1)S(1)}, u32[]{:S(2)}, u32[]{:S(2)}) collective-permute-start(bf16[256,2560]{1,0:T(8,128)(2,1)} %get-tuple-element.125), channel_id=1, source_target_pairs={{0,1},{1,0},{2,3},{3,2},{4,5},{5,4},{6,7},{7,6},{8,9},{9,8},{10,11... | collective-permute-start | bytes 3932168 | tf_op jit(solution)/shard_map/ppermute | solution.py:254
  671.6 35.4 %collective-permute-start.42 = (bf16[256,2560]{1,0:T(8,128)(2,1)}, bf16[256,2560]{1,0:T(8,128)(2,1)S(1)}, u32[]{:S(2)}, u32[]{:S(2)}) collective-permute-start(bf16[256,2560]{1,0:T(8,128)(2,1)} %get-tuple-element.125), channel_id=1, source_target_pairs={{0,2},{1,3},{2,0},{3,1},{4,6},{5,7},{6,4},{7,5},{8,10},{9,11},{10,... | collective-permute-start | bytes 3932168 | tf_op jit(solution)/shard_map/ppermute | solution.py:254
  678.2 57.3 %collective-permute-start.57 = (bf16[256,2560]{1,0:T(8,128)(2,1)}, bf16[256,2560]{1,0:T(8,128)(2,1)}, u32[]{:S(2)}, u32[]{:S(2)}) collective-permute-start(bf16[256,2560]{1,0:T(8,128)(2,1)} %get-tuple-element.122), channel_id=1, source_target_pairs={{0,1},{1,0},{2,3},{3,2},{4,5},{5,4},{6,7},{7,6},{8,9},{9,8},{10,11... | collective-permute-start | bytes 3932168 | tf_op jit(solution)/shard_map/ppermute | solution.py:254
  679.7 52.0 %collective-permute-start.58 = (bf16[256,2560]{1,0:T(8,128)(2,1)}, bf16[256,2560]{1,0:T(8,128)(2,1)}, u32[]{:S(2)}, u32[]{:S(2)}) collective-permute-start(bf16[256,2560]{1,0:T(8,128)(2,1)} %get-tuple-element.122), channel_id=1, source_target_pairs={{0,2},{1,3},{2,0},{3,1},{4,6},{5,7},{6,4},{7,5},{8,10},{9,11},{10,... | collective-permute-start | bytes 3932168 | tf_op jit(solution)/shard_map/ppermute | solution.py:254
  707.0 38.6 %collective-permute-start.43 = (bf16[128,2560]{1,0:T(8,128)(2,1)S(1)}, bf16[128,2560]{1,0:T(8,128)(2,1)}, u32[]{:S(2)}, u32[]{:S(2)}) collective-permute-start(bf16[128,2560]{1,0:T(8,128)(2,1)S(1)} %slice.736), channel_id=1, source_target_pairs={{0,1},{1,0},{2,3},{3,2},{4,5},{5,4},{6,7},{7,6},{8,9},{9,8},{10,11... | collective-permute-start | bytes 1966088 | tf_op jit(solution)/shard_map/ppermute | solution.py:254
  708.2 37.5 %collective-permute-start.44 = (bf16[128,2560]{1,0:T(8,128)(2,1)}, bf16[128,2560]{1,0:T(8,128)(2,1)}, u32[]{:S(2)}, u32[]{:S(2)}) collective-permute-start(bf16[128,2560]{1,0:T(8,128)(2,1)} %slice.737), channel_id=1, source_target_pairs={{0,2},{1,3},{2,0},{3,1},{4,6},{5,7},{6,4},{7,5},{8,10},{9,11},{10,... | collective-permute-start | bytes 1966088 | tf_op jit(solution)/shard_map/ppermute | solution.py:254
  745.2 265.9 %reduce-scatter.13.cloned.1.call-start = ((), (), s32[]{:S(2)}) async-start(), calls=%async_computation.15 | async-start | bytes 3686400 | tf_op jit(solution)/shard_map/reduce_scatter | solution.py:431
  758.7 107.8 %collective-permute-start.49 = (bf16[512,1280]{1,0:T(8,128)(2,1)}, bf16[512,1280]{1,0:T(8,128)(2,1)}, u32[]{:S(2)}, u32[]{:S(2)}) collective-permute-start(bf16[512,1280]{1,0:T(8,128)(2,1)} %convolution_convert_fusion.11), channel_id=1, source_target_pairs={{0,1},{1,0},{2,3},{3,2},{4,5},{5,4},{6,7},{7,6},{8,9},{9,8},{10,11... | collective-permute-start | bytes 3932168 | tf_op jit(solution)/shard_map/ppermute | solution.py:254
  766.0 105.4 %collective-permute-start.51 = (bf16[512,1280]{1,0:T(8,128)(2,1)}, bf16[512,1280]{1,0:T(8,128)(2,1)}, u32[]{:S(2)}, u32[]{:S(2)}) collective-permute-start(bf16[512,1280]{1,0:T(8,128)(2,1)} %convolution_convert_fusion.10), channel_id=1, source_target_pairs={{0,2},{1,3},{2,0},{3,1},{4,6},{5,7},{6,4},{7,5},{8,10},{9,11},{10,... | collective-permute-start | bytes 3932168 | tf_op jit(solution)/shard_map/ppermute | solution.py:254
  770.8 104.8 %collective-permute-start.45 = (bf16[512,1280]{1,0:T(8,128)(2,1)}, bf16[512,1280]{1,0:T(8,128)(2,1)}, u32[]{:S(2)}, u32[]{:S(2)}) collective-permute-start(bf16[512,1280]{1,0:T(8,128)(2,1)} %convolution_convert_fusion.13), channel_id=1, source_target_pairs={{0,1},{1,0},{2,3},{3,2},{4,5},{5,4},{6,7},{7,6},{8,9},{9,8},{10,11... | collective-permute-start | bytes 3932168 | tf_op jit(solution)/shard_map/ppermute | solution.py:254
  775.0 104.2 %collective-permute-start.47 = (bf16[512,1280]{1,0:T(8,128)(2,1)}, bf16[512,1280]{1,0:T(8,128)(2,1)}, u32[]{:S(2)}, u32[]{:S(2)}) collective-permute-start(bf16[512,1280]{1,0:T(8,128)(2,1)} %convolution_convert_fusion.12), channel_id=1, source_target_pairs={{0,2},{1,3},{2,0},{3,1},{4,6},{5,7},{6,4},{7,5},{8,10},{9,11},{10,... | collective-permute-start | bytes 3932168 | tf_op jit(solution)/shard_map/ppermute | solution.py:254
  882.5 113.6 %collective-permute-start.48 = (bf16[256,1280]{1,0:T(8,128)(2,1)}, bf16[256,1280]{1,0:T(8,128)(2,1)}, u32[]{:S(2)}, u32[]{:S(2)}) collective-permute-start(bf16[256,1280]{1,0:T(8,128)(2,1)} %add_convert_fusion.6), channel_id=1, source_target_pairs={{0,1},{1,0},{2,3},{3,2},{4,5},{5,4},{6,7},{7,6},{8,9},{9,8},{10,11... | collective-permute-start | bytes 1966088 | tf_op jit(solution)/shard_map/ppermute | solution.py:254
  893.7 163.1 %reduce-scatter.15.cloned.1.call-start = ((), (), s32[]{:S(2)}) async-start(), calls=%async_computation.16 | async-start | bytes 2949120 | tf_op jit(solution)/shard_map/reduce_scatter | solution.py:431
  935.2 18.6 %collective-permute-start.65 = (bf16[512,512]{0,1:T(8,128)(2,1)S(1)}, bf16[512,512]{0,1:T(8,128)(2,1)S(1)}, u32[]{:S(2)}, u32[]{:S(2)}) collective-permute-start(bf16[512,512]{0,1:T(8,128)(2,1)S(1)} %pad_maximum_fusion.19), channel_id=1, source_target_pairs={{0,1},{1,0},{2,3},{3,2},{4,5},{5,4},{6,7},{7,6},{8,9},{9,8},{10,11... | collective-permute-start | bytes 1572872 | tf_op jit(solution)/shard_map/ppermute | solution.py:254
  936.6 18.4 %collective-permute-start.63 = (bf16[512,544]{0,1:T(8,128)(2,1)S(1)}, bf16[512,544]{0,1:T(8,128)(2,1)S(1)}, u32[]{:S(2)}, u32[]{:S(2)}) collective-permute-start(bf16[512,544]{0,1:T(8,128)(2,1)S(1)} %pad_maximum_fusion.16), channel_id=1, source_target_pairs={{0,2},{1,3},{2,0},{3,1},{4,6},{5,7},{6,4},{7,5},{8,10},{9,11},{10,... | collective-permute-start | bytes 1671176 | tf_op jit(solution)/shard_map/ppermute | solution.py:254
  937.5 20.2 %collective-permute-start.67 = (bf16[512,544]{0,1:T(8,128)(2,1)S(1)}, bf16[512,544]{0,1:T(8,128)(2,1)S(1)}, u32[]{:S(2)}, u32[]{:S(2)}) collective-permute-start(bf16[512,544]{0,1:T(8,128)(2,1)S(1)} %pad_maximum_fusion.17), channel_id=1, source_target_pairs={{0,2},{1,3},{2,0},{3,1},{4,6},{5,7},{6,4},{7,5},{8,10},{9,11},{10,... | collective-permute-start | bytes 1671176 | tf_op jit(solution)/shard_map/ppermute | solution.py:254
  996.1 23.5 %collective-permute-start.69 = (bf16[4,4,80,1152]{3,2,1,0:T(8,128)(2,1)}, bf16[4,4,80,1152]{3,2,1,0:T(8,128)(2,1)}, u32[]{:S(2)}, u32[]{:S(2)}) collective-permute-start(bf16[4,4,80,1152]{3,2,1,0:T(8,128)(2,1)} %dynamic-slice_bitcast_fusion), channel_id=1, source_target_pairs={{0,4},{4,0},{1,5},{5,1},{2,6},{6,2},{3,7},{7,3},{8,12},{12,8},{9,1... | collective-permute-start | bytes 8847368 | tf_op jit(solution)/shard_map/ppermute | solution.py:346
  1011.1 66.9 %reduce-scatter.17.cloned.1.call-start = ((), (), s32[]{:S(2)}) async-start(), calls=%async_computation.17 | async-start | bytes 921600 | tf_op jit(solution)/shard_map/reduce_scatter | solution.py:392
  1023.3 17.1 %collective-permute-start.70 = (bf16[640,512]{1,0:T(8,128)(2,1)S(1)}, bf16[640,512]{1,0:T(8,128)(2,1)S(1)}, u32[]{:S(2)}, u32[]{:S(2)}) collective-permute-start(bf16[640,512]{1,0:T(8,128)(2,1)S(1)} %pad_maximum_fusion.15), channel_id=1, source_target_pairs={{0,1},{1,0},{2,3},{3,2},{4,5},{5,4},{6,7},{7,6},{8,9},{9,8},{10,11... | collective-permute-start | bytes 1966088 | tf_op jit(solution)/shard_map/ppermute | solution.py:254
  1024.5 21.2 %collective-permute-start.72 = (bf16[640,640]{1,0:T(8,128)(2,1)S(1)}, bf16[640,640]{1,0:T(8,128)(2,1)S(1)}, u32[]{:S(2)}, u32[]{:S(2)}) collective-permute-start(bf16[640,640]{1,0:T(8,128)(2,1)S(1)} %pad_maximum_fusion.12), channel_id=1, source_target_pairs={{0,2},{1,3},{2,0},{3,1},{4,6},{5,7},{6,4},{7,5},{8,10},{9,11},{10,... | collective-permute-start | bytes 2457608 | tf_op jit(solution)/shard_map/ppermute | solution.py:254
  (177 other events, 1511.0 us)
Sparse Core Ops, SparseCore 0:
  12.2 27.2 all-gather.8
  41.7 36.8 all-gather.6
  80.3 38.3 all-gather.10
  120.2 81.9 all-gather.14
  203.7 81.6 all-gather.12
  286.9 81.6 all-gather.16
  536.3 89.4 reduce-scatter.6
  628.1 89.1 reduce-scatter.10
  745.3 89.0 reduce-scatter.8
  893.9 39.3 reduce-scatter.12
  1011.2 35.3 reduce-scatter.14
  1057.0 20.9 reduce-scatter.16
